TPU v7x, 32 devices: a whole 2x2x4 slice. The times are simulated.
32 devices in a mesh: pipe: 4 (over y, x), dp: 8 (over z, core).
Axes of the slice: x: 2, y: 2, z: 4, core: 2. Of those that a mesh axis runs over, the one named last changes fastest.
Arguments:
- queries: bfloat16 [4, 2, 4096, 4096], P('pipe', None, 'dp'), may hold values from -64 to 64
- keys: bfloat16 [4, 2, 4096, 512], P('pipe', None, 'dp'), may hold values from -6 to 6
- values: bfloat16 [4, 2, 4096, 512], P('pipe', None, 'dp'), may hold values from -6 to 6
- segment: int32 [4, 2, 4096], P('pipe', None, 'dp'), may hold values from 0 to 4095, as said below
- parent: int32 [4, 2, 4096], P('pipe', None, 'dp'), may hold values from 0 to 4094, as said below
- tree_lengths: int32 [4, 2, 32], P('pipe'), may hold values from 0 to 3, as said below
Outputs:
- forward_next: bfloat16 [4, 4096, 4096], P('pipe', 'dp')
- return_next: bfloat16 [4, 4096, 4096], P('pipe', 'dp')
Inputs may be any that keep to these rules, and one draw needn't show every extreme that they name: `tree_lengths`: each row lists the trees of one micro-batch in order: entries of 1 to 3 blocks that sum to 32, then zeros; some tree is exactly 3 blocks long. Within a micro-batch a segment is a run of rows, numbered by the index of its first row; every tree's first row opens a new segment, so no segment spans two trees; the last row of every micro-batch opens a segment of its own. The first segment of a tree is its own parent; every other segment's parent is an earlier segment of the same tree whose parent is that first segment; in every micro-batch the last row's parent is the segment opened by the row before it.
All inputs are finite; a program needn't handle non-finite values.
Results may differ from a plain program's by a relative error of at most 0.0036.
Values may be sent and summed in bfloat16 or wider, within the bound.
No kernel may reach another device: no remote copies, remote signals or barrier semaphores. Data moves between devices by JAX's collectives and lax.ppermute only.
A program may use at most 192 MiB of HBM per device.

v0:
```python
import math

import jax
import jax.numpy as jnp
from jax import lax
from jax.sharding import PartitionSpec as P

BLK = 128
TREE_MOST = 3
KV_HEADS = 4
GROUP = 8
HEAD = 128


NEG = -1e30


def shifted(value, axis, steps):
    count = lax.axis_size(axis)
    initial, last = (max(0, -steps), min(count, count - steps))
    return lax.ppermute(value, axis, [(source, source + steps) for source in range(initial, last)])


def block_trees(lengths, block_ids):
    ends = jnp.cumsum(lengths)
    starts = ends - lengths
    inside = (starts[None, :] <= block_ids[:, None]) & (lengths[None, :] > 0)
    tree = jnp.sum(inside.astype(jnp.int32), axis=1) - 1
    begins = jnp.max(jnp.where(inside, starts[None, :], -1), axis=1)
    present = (block_ids >= 0) & (block_ids < lengths.shape[0])
    return (jnp.where(present, tree, -1), begins)


def pad_front(array, fill, reach):
    padding = jnp.full((reach,) + array.shape[1:], fill, array.dtype)
    return jnp.concatenate([padding, array], axis=0)


def attend(queries, query_info, keys, values, key_info, offset):
    reach = (TREE_MOST - 1) * BLK
    span = TREE_MOST * BLK
    count = queries.shape[0] // BLK
    key_rows = pad_front(keys, 0, reach)
    value_rows = pad_front(values, 0, reach)
    key_tree = pad_front(key_info[0], -2, reach)
    key_pos = pad_front(key_info[1], -1, reach)
    key_seg = pad_front(key_info[2], -3, reach)
    key_par = pad_front(key_info[3], -4, reach)
    scale = 1.0 / math.sqrt(HEAD)
    pieces = []
    for group_start in range(0, count, 4):
        group_count = min(4, count - group_start)
        chosen = range(group_start, group_start + group_count)

        def windowed(rows):
            return jnp.stack(
                [
                    lax.slice_in_dim(
                        rows, (index + offset) * BLK, (index + offset) * BLK + span, axis=0
                    )
                    for index in chosen
                ]
            )

        keyset = windowed(key_rows).reshape(group_count, span, KV_HEADS, HEAD)
        valueset = windowed(value_rows).reshape(group_count, span, KV_HEADS, HEAD)
        window_tree = windowed(key_tree)
        window_pos = windowed(key_pos)
        window_seg = windowed(key_seg)
        window_par = windowed(key_par)
        first_row = group_start * BLK
        last_row = first_row + group_count * BLK
        query = queries[first_row:last_row].reshape(group_count, BLK, KV_HEADS, GROUP, HEAD)
        query_tree = query_info[0][first_row:last_row].reshape(group_count, BLK)
        query_pos = query_info[1][first_row:last_row].reshape(group_count, BLK)
        query_seg = query_info[2][first_row:last_row].reshape(group_count, BLK)
        query_par = query_info[3][first_row:last_row].reshape(group_count, BLK)
        related = (
            (window_seg[:, None, :] == query_seg[:, :, None])
            | (window_seg[:, None, :] == query_par[:, :, None])
            | (window_par == window_seg)[:, None, :]
        )
        allowed = (
            (window_tree[:, None, :] == query_tree[:, :, None])
            & (window_pos[:, None, :] <= query_pos[:, :, None])
            & related
        )
        scores = (
            jnp.einsum("aqhgd,akhd->ahgqk", query, keyset, preferred_element_type=jnp.float32)
            * scale
        )
        scores = jnp.where(allowed[:, None, None], scores, NEG)
        top = jnp.max(scores, axis=-1, keepdims=True)
        weights = jnp.exp(scores - top)
        totals = jnp.sum(weights, axis=-1)
        rounded = weights.astype(jnp.bfloat16)
        mixed = jnp.einsum(
            "ahgqk,akhd->aqhgd", rounded, valueset, preferred_element_type=jnp.float32
        )
        totals = jnp.transpose(totals, (0, 3, 1, 2))[..., None]
        pieces.append((mixed / totals).astype(jnp.bfloat16).reshape(group_count * BLK, -1))
    return jnp.concatenate(pieces, axis=0)


def section(queries, keys, values, segment, parent, lengths):
    rows = queries.shape[0]
    span_blocks = rows // BLK
    reach_blocks = TREE_MOST - 1
    reach = reach_blocks * BLK
    first_block = lax.axis_index("dp") * span_blocks
    moved = shifted(
        (queries[:reach], keys[:reach], values[:reach], segment[:reach], parent[:reach]), "dp", -1
    )
    all_queries = jnp.concatenate([queries, moved[0]], axis=0)
    all_keys = jnp.concatenate([keys, moved[1]], axis=0)
    all_values = jnp.concatenate([values, moved[2]], axis=0)
    all_seg = jnp.concatenate([segment, moved[3]], axis=0)
    all_par = jnp.concatenate([parent, moved[4]], axis=0)
    block_ids = first_block + jnp.arange(span_blocks + reach_blocks, dtype=jnp.int32)
    tree, begins = block_trees(lengths, block_ids)
    positions = first_block * BLK + jnp.arange(rows + reach, dtype=jnp.int32)
    info = (jnp.repeat(tree, BLK), positions, all_seg, all_par)
    result = attend(all_queries, info, all_keys, all_values, info, 0)
    returned = shifted(result[rows:], "dp", 1)
    own_start = jnp.repeat(begins[:span_blocks], BLK) >= first_block
    filled = jnp.concatenate(
        [returned, jnp.zeros((rows - reach, returned.shape[1]), jnp.bfloat16)], axis=0
    )
    return jnp.where(own_start[:, None], result[:rows], filled)


def on_device(queries, keys, values, segment, parent, tree_lengths):
    outgoing = section(
        queries[0, 0], keys[0, 0], values[0, 0], segment[0, 0], parent[0, 0], tree_lengths[0, 0]
    )
    moved_on = shifted(outgoing, "pipe", 1)
    returning = section(
        queries[0, 1], keys[0, 1], values[0, 1], segment[0, 1], parent[0, 1], tree_lengths[0, 1]
    )
    moved_back = shifted(returning, "pipe", -1)
    place = lax.axis_index("pipe")
    forward_next = jnp.where(place == 0, returning, moved_on)
    return_next = jnp.where(place == lax.axis_size("pipe") - 1, outgoing, moved_back)
    return (forward_next[None], return_next[None])


def solution(mesh):
    return jax.shard_map(
        on_device,
        mesh=mesh,
        in_specs=(
            P("pipe", None, "dp", None),
            P("pipe", None, "dp", None),
            P("pipe", None, "dp", None),
            P("pipe", None, "dp"),
            P("pipe", None, "dp"),
            P("pipe", None, None),
        ),
        out_specs=(P("pipe", "dp", None), P("pipe", "dp", None)),
        check_vma=False,
    )
```

profile of v0, /device:TPU:20, one launch (start us, length us, event | category | flops | bytes accessed | tf_op | source)
XLA Modules:
  0.0 486.9 jit_solution(1664282591844582652)
XLA Ops:
  36.3 3.8 slice_bitcast_fusion
  58.0 5.6 %copy.146 = bf16[64,8,32,128]{3,2,1,0:T(8,128)(2,1)} copy(bf16[64,8,32,128]{3,1,2,0:T(8,128)(2,1)} %get-tuple-element.12) | data formatting | bytes 8388608
  79.7 3.3 fusion.89
  85.3 5.5 %copy.140 = bf16[64,8,32,128]{3,2,1,0:T(8,128)(2,1)} copy(bf16[64,8,32,128]{3,1,2,0:T(8,128)(2,1)} %get-tuple-element.13) | data formatting | bytes 8388608
  104.5 21.9 %collective-permute-done.3 = bf16[256,512]{0,1:T(8,128)(2,1)S(1)} collective-permute-done((bf16[256,512]{0,1:T(8,128)(2,1)S(1)}, bf16[256,512]{0,1:T(8,128)(2,1)S(1)}, u32[]{:S(2)}, u32[]{:S(2)}) %collective-permute-start.3) | collective-permute-done | bytes 262176 | tf_op jit(solution)/shard_map/ppermute | solution.py:21
  126.4 4.3 collective-permute-start.4
  136.7 2.9 fusion.91
  143.5 14.4 %fusion.4 = (f32[4,4,8,128]{3,2,1,0:T(8,128)S(1)}, f32[4,4,384,128,8]{3,2,4,1,0:T(8,128)}) fusion(pred[4,128,384]{1,2,0:T(8,128)(4,1)} %get-tuple-element.47, bf16[4,128,4,8,128]{4,3,2,1,0:T(8,128)(2,1)} %bitcast.287, bf16[1,384,4,128]{3,1,2,0:T(8,128)(2,1)} %copy.83, bf16[1,384,4,128]{3,1,2,0:T(8,128)(2,1)} %copy.82, bf16[1,384,4,128]{3,1,2,0:T(8,128)(2,1)} %copy.81, ...), kind=kOutput, calls=%fused_computation.8 | convolution fusion | flops 1635762176 | bytes 31195136 | tf_op jit(solution)/shard_map/aqhgd,akhd->ahgqk/dot_general | solution.py:89
  157.9 11.5 %fusion = f32[4,4,8,128]{3,2,1,0:T(8,128)S(1)} fusion(f32[4,4,384,128,8]{3,2,4,1,0:T(8,128)} %get-tuple-element.107, f32[4,4,8,128]{3,2,1,0:T(8,128)S(1)} %get-tuple-element.106, pred[4,128,384]{1,2,0:T(8,128)(4,1)S(1)} %copy-done.15), kind=kLoop, calls=%fused_computation.4 | loop fusion | flops 25149440 | bytes 25493504 | tf_op jit(solution)/shard_map/reduce_sum | solution.py:95
  169.5 13.4 %fusion.25 = bf16[4,128,4,8,128]{1,4,3,2,0:T(8,128)(2,1)} fusion(f32[4,128,4,8]{1,3,2,0:T(8,128)S(1)} %bitcast.319, f32[4,4,384,128,8]{3,2,4,1,0:T(8,128)} %get-tuple-element.107, f32[4,4,8,128]{3,2,1,0:T(8,128)S(1)} %get-tuple-element.106, pred[4,128,384]{1,2,0:T(8,128)(4,1)S(1)} %copy-done.15, bf16[1,384,4,128]{1,3,2,0:T(8,128)(2,1)S(1)} %bitcast.308, ...), kind=kOutput, calls=%fused_computation.33 | convolution fusion | flops 1646264320 | bytes 31260672 | tf_op jit(solution)/shard_map/ahgqk,akhd->aqhgd/dot_general | solution.py:97
  205.4 7.8 %copy.86 = bf16[4,128,4,8,128]{4,3,2,1,0:T(8,128)(2,1)} copy(bf16[4,128,4,8,128]{1,4,3,2,0:T(8,128)(2,1)} %fusion.25) | data formatting | bytes 8388608 | tf_op jit(solution)/shard_map/convert_element_type | solution.py:101
  213.2 7.4 %reshape.519 = bf16[512,4096]{1,0:T(8,128)(2,1)} reshape(bf16[4,128,4,8,128]{4,3,2,1,0:T(8,128)(2,1)} %copy.86) | data formatting | bytes 8388608 | tf_op jit(solution)/shard_map/reshape | solution.py:101
  220.6 14.2 %fusion.5 = (f32[4,4,8,128]{3,2,1,0:T(8,128)S(1)}, f32[4,4,384,128,8]{3,2,4,1,0:T(8,128)}) fusion(pred[4,128,384]{1,2,0:T(8,128)(4,1)S(1)} %copy-done.14, bf16[4,128,4,8,128]{4,3,2,1,0:T(8,128)(2,1)} %bitcast.286, bf16[1,384,4,128]{3,1,2,0:T(8,128)(2,1)S(1)} %copy-done.21, bf16[1,384,4,128]{3,1,2,0:T(8,128)(2,1)S(1)} %copy-done.20, ...), kind=kOutput, calls=%fused_computation.9 | convolution fusion | flops 1635762176 | bytes 31195136 | tf_op jit(solution)/shard_map/aqhgd,akhd->ahgqk/dot_general | solution.py:89
  236.0 2.7 fusion.22
  238.8 3.5 fusion.18
  242.3 4.6 fusion.39
  247.0 3.4 copy.94
  255.1 12.3 %fusion.2 = f32[4,4,8,128]{3,2,1,0:T(8,128)} fusion(f32[4,4,384,128,8]{3,2,4,1,0:T(8,128)} %get-tuple-element.111, f32[4,4,8,128]{3,2,1,0:T(8,128)S(1)} %get-tuple-element.110, pred[4,128,384]{1,2,0:T(8,128)(4,1)S(1)} %copy-done.14), kind=kLoop, calls=%fused_computation.6 | loop fusion | flops 25149440 | bytes 25493504 | tf_op jit(solution)/shard_map/reduce_sum | solution.py:95
  269.6 2.7 fusion.23
  272.4 7.9 %collective-permute-done.5 = bf16[256,4096]{1,0:T(8,128)(2,1)S(1)} collective-permute-done((bf16[256,4096]{1,0:T(8,128)(2,1)}, bf16[256,4096]{1,0:T(8,128)(2,1)S(1)}, u32[]{:S(2)}, u32[]{:S(2)}) %collective-permute-start.5) | collective-permute-done | bytes 2097184 | tf_op jit(solution)/shard_map/ppermute | solution.py:21
  280.3 4.1 pad_select_fusion.1
  284.4 3.3 collective-permute-start.13
  287.7 3.5 fusion.20
  291.3 4.6 fusion.38
  295.9 3.5 copy.117
  304.0 13.1 %fusion.24 = bf16[4,128,4,8,128]{1,4,3,2,0:T(8,128)(2,1)} fusion(f32[4,128,4,8]{1,3,2,0:T(8,128)} %bitcast.318, f32[4,4,384,128,8]{3,2,4,1,0:T(8,128)} %get-tuple-element.111, f32[4,4,8,128]{3,2,1,0:T(8,128)S(1)} %get-tuple-element.110, pred[4,128,384]{1,2,0:T(8,128)(4,1)S(1)} %copy-done.14, bf16[1,384,4,128]{1,3,2,0:T(8,128)(2,1)S(1)} %bitcast.306, ...), kind=kOutput, calls=%fused_computation.31 | convolution fusion | flops 1646264320 | bytes 31260672 | tf_op jit(solution)/shard_map/ahgqk,akhd->aqhgd/dot_general | solution.py:97
  317.1 7.9 %copy.109 = bf16[4,128,4,8,128]{4,3,2,1,0:T(8,128)(2,1)} copy(bf16[4,128,4,8,128]{1,4,3,2,0:T(8,128)(2,1)} %fusion.24) | data formatting | bytes 8388608 | tf_op jit(solution)/shard_map/convert_element_type | solution.py:101
  325.0 7.3 %reshape.526 = bf16[512,4096]{1,0:T(8,128)(2,1)} reshape(bf16[4,128,4,8,128]{4,3,2,1,0:T(8,128)(2,1)} %copy.109) | data formatting | bytes 8388608 | tf_op jit(solution)/shard_map/reshape | solution.py:101
  332.3 46.6 %collective-permute-done.13 = bf16[512,4096]{1,0:T(8,128)(2,1)} collective-permute-done((bf16[512,4096]{1,0:T(8,128)(2,1)}, bf16[512,4096]{1,0:T(8,128)(2,1)}, u32[]{:S(2)}, u32[]{:S(2)}) %collective-permute-start.13) | collective-permute-done | bytes 4194336 | tf_op jit(solution)/shard_map/ppermute | solution.py:21
  378.9 8.4 %select_bitcast_fusion = (bf16[1,512,4096]{2,1,0:T(8,128)(2,1)}, bf16[512,4096]{1,0:T(8,128)(2,1)}) fusion(bf16[512,4096]{1,0:T(8,128)(2,1)} %collective-permute-done.13, pred[]{:T(512)S(6)} %eq.291, bf16[512,4096]{1,0:T(8,128)(2,1)} %reshape.526, bf16[256,4096]{1,0:T(8,128)(2,1)S(1)} %collective-permute-done.11, pred[512]{0:T(512)(128)(4,1)S(1)} %copy-done.50), kind=kLoop, calls=%fused_computation.52 | loop fusion | flops 4194304 | bytes 18874880 | tf_op jit(solution)/shard_map/broadcast_in_dim | solution.py:144
  389.2 92.6 %collective-permute-done.12 = bf16[512,4096]{1,0:T(8,128)(2,1)} collective-permute-done((bf16[512,4096]{1,0:T(8,128)(2,1)}, bf16[512,4096]{1,0:T(8,128)(2,1)}, u32[]{:S(2)}, u32[]{:S(2)}) %collective-permute-start.12) | collective-permute-done | bytes 4194336 | tf_op jit(solution)/shard_map/ppermute | solution.py:21
  481.8 4.6 select_bitcast_fusion.1
  (277 shorter events, 131.9 us)
Async XLA Ops:
  0.6 31.0 %copy-start.2 = (bf16[1,2,512,512]{3,2,1,0:T(8,128)(2,1)S(1)}, bf16[1,2,512,512]{3,2,1,0:T(8,128)(2,1)}, u32[]{:S(2)}) copy-start(bf16[1,2,512,512]{3,2,1,0:T(8,128)(2,1)} %param.7) | copy-start | bytes 3145732
  0.6 32.1 %copy-start.3 = (bf16[1,2,512,512]{3,2,1,0:T(8,128)(2,1)S(1)}, bf16[1,2,512,512]{3,2,1,0:T(8,128)(2,1)}, u32[]{:S(2)}) copy-start(bf16[1,2,512,512]{3,2,1,0:T(8,128)(2,1)} %param.8) | copy-start | bytes 3145732
  3.4 179.5 %collective-permute-start.9 = (bf16[256,512]{0,1:T(8,128)(2,1)}, bf16[256,512]{0,1:T(8,128)(2,1)}, u32[]{:S(2)}, u32[]{:S(2)}) collective-permute-start(bf16[256,512]{0,1:T(8,128)(2,1)} %bitcast.87), channel_id=1, source_target_pairs={{1,0},{2,1},{3,2},{4,3},{5,4},{6,5},{7,6},{9,8},{10,9},{11,10},{12... | collective-permute-start | bytes 786440 | tf_op jit(solution)/shard_map/ppermute | solution.py:21
  7.2 129.5 %collective-permute-start = (bf16[256,512]{1,0:T(8,128)(2,1)}, bf16[256,512]{1,0:T(8,128)(2,1)}, u32[]{:S(2)}, u32[]{:S(2)}) collective-permute-start(bf16[256,512]{1,0:T(8,128)(2,1)} %get-tuple-element.15), channel_id=1, source_target_pairs={{1,0},{2,1},{3,2},{4,3},{5,4},{6,5},{7,6},{9,8},{10,9},{11,10},{12... | collective-permute-start | bytes 786440 | tf_op jit(solution)/shard_map/ppermute | solution.py:21
  9.6 127.1 %collective-permute-start.6 = (bf16[256,512]{1,0:T(8,128)(2,1)}, bf16[256,512]{1,0:T(8,128)(2,1)}, u32[]{:S(2)}, u32[]{:S(2)}) collective-permute-start(bf16[256,512]{1,0:T(8,128)(2,1)} %get-tuple-element.14), channel_id=1, source_target_pairs={{1,0},{2,1},{3,2},{4,3},{5,4},{6,5},{7,6},{9,8},{10,9},{11,10},{12... | collective-permute-start | bytes 786440 | tf_op jit(solution)/shard_map/ppermute | solution.py:21
  12.9 79.8 %collective-permute-start.1 = (s32[256]{0:T(256)}, s32[256]{0:T(256)}, u32[]{:S(2)}, u32[]{:S(2)}) collective-permute-start(s32[256]{0:T(256)} %bitcast.36), channel_id=1, source_target_pairs={{1,0},{2,1},{3,2},{4,3},{5,4},{6,5},{7,6},{9,8},{10,9},{11,10},{12... | collective-permute-start | bytes 3080 | tf_op jit(solution)/shard_map/ppermute | solution.py:21
  16.7 78.6 %collective-permute-start.2 = (s32[256]{0:T(256)}, s32[256]{0:T(256)}, u32[]{:S(2)}, u32[]{:S(2)}) collective-permute-start(s32[256]{0:T(256)} %bitcast.38), channel_id=1, source_target_pairs={{1,0},{2,1},{3,2},{4,3},{5,4},{6,5},{7,6},{9,8},{10,9},{11,10},{12... | collective-permute-start | bytes 3080 | tf_op jit(solution)/shard_map/ppermute | solution.py:21
  40.1 14.5 %copy-start.6 = (bf16[1,1,512,512]{3,2,1,0:T(8,128)(2,1)S(1)}, bf16[1,1,512,512]{3,2,1,0:T(8,128)(2,1)}, u32[]{:S(2)}) copy-start(bf16[1,1,512,512]{3,2,1,0:T(8,128)(2,1)} %get-tuple-element.24) | copy-start | bytes 1572868
  40.2 15.5 %copy-start.11 = (bf16[1,1,384,512]{3,2,1,0:T(8,128)(2,1)S(1)}, bf16[1,1,384,512]{3,2,1,0:T(8,128)(2,1)}, u32[]{:S(2)}) copy-start(bf16[1,1,384,512]{3,2,1,0:T(8,128)(2,1)} %get-tuple-element.26) | copy-start | bytes 1179652
  40.2 16.7 %copy-start.9 = (bf16[1,1,384,512]{3,2,1,0:T(8,128)(2,1)S(1)}, bf16[1,1,384,512]{3,2,1,0:T(8,128)(2,1)}, u32[]{:S(2)}) copy-start(bf16[1,1,384,512]{3,2,1,0:T(8,128)(2,1)} %get-tuple-element.27) | copy-start | bytes 1179652
  58.0 12.8 %copy-start.5 = (bf16[1,1,512,512]{3,2,1,0:T(8,128)(2,1)S(1)}, bf16[1,1,512,512]{3,2,1,0:T(8,128)(2,1)}, u32[]{:S(2)}) copy-start(bf16[1,1,512,512]{3,2,1,0:T(8,128)(2,1)} %get-tuple-element.25) | copy-start | bytes 1572868
  58.0 25.0 %copy-start.8 = (bf16[1,1,384,512]{3,2,1,0:T(8,128)(2,1)S(1)}, bf16[1,1,384,512]{3,2,1,0:T(8,128)(2,1)}, u32[]{:S(2)}) copy-start(bf16[1,1,384,512]{3,2,1,0:T(8,128)(2,1)} %get-tuple-element.29) | copy-start | bytes 1179652
  63.6 20.5 %copy-start.7 = (bf16[1,1,384,512]{3,2,1,0:T(8,128)(2,1)S(1)}, bf16[1,1,384,512]{3,2,1,0:T(8,128)(2,1)}, u32[]{:S(2)}) copy-start(bf16[1,1,384,512]{3,2,1,0:T(8,128)(2,1)} %get-tuple-element.28) | copy-start | bytes 1179652
  85.3 14.7 %copy-start.36 = (bf16[1,1,256,512]{2,3,1,0:T(8,128)(2,1)S(1)}, bf16[1,1,256,512]{2,3,1,0:T(8,128)(2,1)}, u32[]{:S(2)}) copy-start(bf16[1,1,256,512]{2,3,1,0:T(8,128)(2,1)} %copy.133) | copy-start | bytes 786436
  85.3 17.0 %copy-start.43 = (s32[2,128]{1,0:T(2,128)S(1)}, s32[2,128]{1,0:T(2,128)}, u32[]{:S(2)}) copy-start(s32[2,128]{1,0:T(2,128)} %slice_bitcast_fusion.17) | copy-start | bytes 3076
  85.3 17.0 %copy-start.51 = (s32[2]{0:T(128)S(1)}, s32[2]{0:T(128)}, u32[]{:S(2)}) copy-start(s32[2]{0:T(128)} %slice.449) | copy-start | bytes 28
  85.3 17.0 %copy-start.52 = (s32[2]{0:T(128)S(1)}, s32[2]{0:T(128)}, u32[]{:S(2)}) copy-start(s32[2]{0:T(128)} %slice.501) | copy-start | bytes 28
  92.7 5.2 %collective-permute-start.7 = (s32[256]{0:T(256)S(1)}, s32[256]{0:T(256)S(1)}, u32[]{:S(2)}, u32[]{:S(2)}) collective-permute-start(s32[256]{0:T(256)S(1)} %bitcast.347), channel_id=1, source_target_pairs={{1,0},{2,1},{3,2},{4,3},{5,4},{6,5},{7,6},{9,8},{10,9},{11,10},{12... | collective-permute-start | bytes 3080 | tf_op jit(solution)/shard_map/ppermute | solution.py:21
  95.3 4.6 collective-permute-start.8
  97.9 169.5 %collective-permute-start.10 = (bf16[256,4096]{1,0:T(8,128)(2,1)}, bf16[256,4096]{1,0:T(8,128)(2,1)}, u32[]{:S(2)}, u32[]{:S(2)}) collective-permute-start(bf16[256,4096]{1,0:T(8,128)(2,1)} %get-tuple-element.10), channel_id=1, source_target_pairs={{1,0},{2,1},{3,2},{4,3},{5,4},{6,5},{7,6},{9,8},{10,9},{11,10},{12... | collective-permute-start | bytes 6291464 | tf_op jit(solution)/shard_map/ppermute | solution.py:21
  100.0 26.4 %collective-permute-start.3 = (bf16[256,512]{0,1:T(8,128)(2,1)S(1)}, bf16[256,512]{0,1:T(8,128)(2,1)S(1)}, u32[]{:S(2)}, u32[]{:S(2)}) collective-permute-start(bf16[256,512]{0,1:T(8,128)(2,1)S(1)} %bitcast.317), channel_id=1, source_target_pairs={{1,0},{2,1},{3,2},{4,3},{5,4},{6,5},{7,6},{9,8},{10,9},{11,10},{12... | collective-permute-start | bytes 786440 | tf_op jit(solution)/shard_map/ppermute | solution.py:21
  126.4 108.5 %collective-permute-start.4 = (bf16[256,4096]{1,0:T(8,128)(2,1)}, bf16[256,4096]{1,0:T(8,128)(2,1)S(1)}, u32[]{:S(2)}, u32[]{:S(2)}) collective-permute-start(bf16[256,4096]{1,0:T(8,128)(2,1)} %get-tuple-element.11), channel_id=1, source_target_pairs={{1,0},{2,1},{3,2},{4,3},{5,4},{6,5},{7,6},{9,8},{10,9},{11,10},{12... | collective-permute-start | bytes 6291464 | tf_op jit(solution)/shard_map/ppermute | solution.py:21
  143.5 14.4 %copy-start.15 = (pred[4,128,384]{1,2,0:T(8,128)(4,1)S(1)}, pred[4,128,384]{1,2,0:T(8,128)(4,1)}, u32[]{:S(2)}) copy-start(pred[4,128,384]{1,2,0:T(8,128)(4,1)} %get-tuple-element.47) | copy-start | bytes 589828
  157.9 11.6 %copy-start.23 = (bf16[1,1,384,512]{2,3,1,0:T(8,128)(2,1)S(1)}, bf16[1,1,384,512]{2,3,1,0:T(8,128)(2,1)}, u32[]{:S(2)}) copy-start(bf16[1,1,384,512]{2,3,1,0:T(8,128)(2,1)} %copy.76) | copy-start | bytes 1179652
  169.5 13.4 %copy-start.4 = (bf16[1,1,512,512]{2,3,1,0:T(8,128)(2,1)S(1)}, bf16[1,1,512,512]{2,3,1,0:T(8,128)(2,1)}, u32[]{:S(2)}) copy-start(bf16[1,1,512,512]{2,3,1,0:T(8,128)(2,1)} %copy.134) | copy-start | bytes 1572868
  182.9 17.7 %copy-start.12 = (bf16[384,512]{0,1:T(8,128)(2,1)S(1)}, bf16[384,512]{0,1:T(8,128)(2,1)}, u32[]{:S(2)}) copy-start(bf16[384,512]{0,1:T(8,128)(2,1)} %get-tuple-element.36) | copy-start | bytes 1179652
  185.2 19.3 %copy-start.13 = (bf16[384,512]{1,0:T(8,128)(2,1)S(1)}, bf16[384,512]{1,0:T(8,128)(2,1)}, u32[]{:S(2)}) copy-start(bf16[384,512]{1,0:T(8,128)(2,1)} %get-tuple-element.122) | copy-start | bytes 1179652
  252.7 27.6 %collective-permute-start.5 = (bf16[256,4096]{1,0:T(8,128)(2,1)}, bf16[256,4096]{1,0:T(8,128)(2,1)S(1)}, u32[]{:S(2)}, u32[]{:S(2)}) collective-permute-start(bf16[256,4096]{1,0:T(8,128)(2,1)} %reshape.521), channel_id=1, source_target_pairs={{0,1},{1,2},{2,3},{3,4},{4,5},{5,6},{6,7},{8,9},{9,10},{10,11},{11... | collective-permute-start | bytes 6291464 | tf_op jit(solution)/shard_map/ppermute | solution.py:21
  284.4 94.5 %collective-permute-start.13 = (bf16[512,4096]{1,0:T(8,128)(2,1)}, bf16[512,4096]{1,0:T(8,128)(2,1)}, u32[]{:S(2)}, u32[]{:S(2)}) collective-permute-start(bf16[512,4096]{1,0:T(8,128)(2,1)} %pad_select_fusion.1), channel_id=1, source_target_pairs={{8,0},{16,8},{24,16},{9,1},{17,9},{25,17},{10,2},{18,10},{26,18},{... | collective-permute-start | bytes 12582920 | tf_op jit(solution)/shard_map/ppermute | solution.py:21
  301.8 30.5 %collective-permute-start.11 = (bf16[256,4096]{1,0:T(8,128)(2,1)}, bf16[256,4096]{1,0:T(8,128)(2,1)S(1)}, u32[]{:S(2)}, u32[]{:S(2)}) collective-permute-start(bf16[256,4096]{1,0:T(8,128)(2,1)} %reshape.528), channel_id=1, source_target_pairs={{0,1},{1,2},{2,3},{3,4},{4,5},{5,6},{6,7},{8,9},{9,10},{10,11},{11... | collective-permute-start | bytes 6291464 | tf_op jit(solution)/shard_map/ppermute | solution.py:21
  325.0 53.9 %copy-start.50 = (pred[512]{0:T(512)(128)(4,1)S(1)}, pred[512]{0:T(512)(128)(4,1)}, u32[]{:S(2)}) copy-start(pred[512]{0:T(512)(128)(4,1)} %broadcast_bitcast_fusion.10) | copy-start | bytes 1540
  387.3 94.6 %collective-permute-start.12 = (bf16[512,4096]{1,0:T(8,128)(2,1)}, bf16[512,4096]{1,0:T(8,128)(2,1)}, u32[]{:S(2)}, u32[]{:S(2)}) collective-permute-start(bf16[512,4096]{1,0:T(8,128)(2,1)} %get-tuple-element.9), channel_id=1, source_target_pairs={{0,8},{8,16},{16,24},{1,9},{9,17},{17,25},{2,10},{10,18},{18,26},{... | collective-permute-start | bytes 12582920 | tf_op jit(solution)/shard_map/ppermute | solution.py:21
  (36 other events, 202.9 us)
where the time goes:
time: 496 us; the launch traced here: 487 us
  waiting for transfers between devices  169 us (34%)
  local copies, waits for them, and re-layouts  144 us (29%)
  matrix products  69.9 us (14%)
  other arithmetic  69.8 us (14%)
  starting transfers between devices  32.6 us (7%)
    ppermute x14, waiting for transfers between devices, shifted(): lax.ppermute(value, axis, [(source, source + steps) for source in range(i...  169 us
    dot_general x4, matrix products, attend(): jnp.einsum('ahgqk,akhd->aqhgd', rounded, valueset, preferred_element_type...  35.8 us
    dot_general x4, matrix products, attend(): jnp.einsum('aqhgd,akhd->ahgqk', query, keyset, preferred_element_type=jnp...  34.1 us
    ppermute x14, starting transfers between devices, shifted(): lax.ppermute(value, axis, [(source, source + steps) for source in range(i...  32.6 us
    reduce_sum x4, other arithmetic, attend(): totals = jnp.sum(weights, axis=-1)  30.9 us
    another operation x40, local copies, waits for them, and re-layouts, windowed(): jnp.stack([lax.slice_in_dim(rows, (index + offset) * BLK, (index + offset...  30.3 us
    unnamed x137, local copies, waits for them, and re-layouts  29.3 us
    slice x27, local copies, waits for them, and re-layouts, windowed(): lax.slice_in_dim(rows, (index + offset) * BLK, (index + offset) * BLK + s...  23.4 us
  transfers between devices with their start and end apart: 14, of which 4 were waited for; matrix products, arithmetic and copies ran while one was open for 54% of the time, Pallas kernels for 0%

commit v1 on v0

v1 whole, which is shorter than its diff:
```python
import functools
import math

import jax
import jax.numpy as jnp
from jax import lax
from jax.experimental import pallas as pl
from jax.experimental.pallas import tpu as pltpu
from jax.sharding import PartitionSpec as P

BLK = 128
TREE_MOST = 3
HEAD = 128
REACH = (TREE_MOST - 1) * BLK
SPAN = TREE_MOST * BLK
NEG = -1e30
TOGETHER = 8
FACTOR = math.log2(math.e) / math.sqrt(HEAD)

VMEM_LIMIT = 60 * 1024 * 1024

ANY = pl.BlockSpec(memory_space=pl.ANY)
HBM = pl.BlockSpec(memory_space=pltpu.HBM)
VMEM = pl.BlockSpec(memory_space=pltpu.VMEM)
SMEM = pl.BlockSpec(memory_space=pltpu.SMEM)


def pick(table, index):
    value = jnp.int32(table[-1])
    for at in range(len(table) - 1):
        value = jnp.where(index == at, jnp.int32(table[at]), value)
    return value


def attend_kernel(blocks, halo, pack, *refs):
    refs = list(refs)
    lengths_in, queries, keys, values, seg_in, par_in = refs[:6]
    refs = refs[6:]
    if halo:
        halo_kv, halo_info = refs[:2]
        refs = refs[2:]
    out = refs.pop(0)
    if pack:
        pack_kv, pack_info = refs[:2]
        refs = refs[2:]
    kbuf, vbuf, bias, seg, par, lengths, counter, sems = refs[:8]
    if pack:
        held_kv = refs[8]
    kv_heads = keys.shape[2] // HEAD
    width = queries.shape[2] // kv_heads
    group = width // HEAD
    rows = keys.shape[1]
    lead = REACH if halo else 0
    swap_path = lax.rem(lax.axis_index("pipe"), 2)
    first_block = lax.axis_index("dp") * (rows // BLK)

    copies = []
    packing = []
    count = 0

    def start(source, target, group_of):
        copy = pltpu.make_async_copy(source, target, sems.at[len(copies) + len(packing)])
        copy.start()
        group_of.append(copy)

    start(seg_in, seg, copies)
    start(par_in, par, copies)
    start(lengths_in, lengths, copies)
    for payload in sorted({payload for payload, _ in blocks}):
        path = swap_path if payload == 0 else 1 - swap_path
        for which, (source, target) in enumerate(((keys, kbuf), (values, vbuf))):
            start(source.at[path], target.at[payload, pl.ds(lead, rows)], copies)
            if halo:
                start(halo_kv.at[which, path], target.at[payload, pl.ds(0, lead)], copies)
    if pack:
        for path in range(2):
            for which, source in enumerate((keys, values)):
                start(source.at[path, pl.ds(rows - REACH, REACH)], held_kv.at[which, path], copies)
    for copy in copies:
        copy.wait()
    if pack:
        start(held_kv, pack_kv, packing)
        pack_info[0] = seg[:, rows - REACH :]
        pack_info[1] = par[:, rows - REACH :]

    def build_bias(place, payload, block):
        path = swap_path if payload == 0 else 1 - swap_path
        here = first_block + block

        def step(entry, carry):
            end, begin = carry
            end = end + lengths[path, entry]
            return (end, jnp.where(end <= here, end, begin))

        _, begin = lax.fori_loop(0, lengths.shape[1], step, (jnp.int32(0), jnp.int32(0)))

        def chosen(array, at):
            lanes = slice(at, at + BLK)
            return jnp.where(path == 0, array[0:1, lanes], array[1:2, lanes])

        def column(row):
            return jnp.transpose(jnp.broadcast_to(row, (BLK, BLK)))

        query_seg = column(chosen(seg, block * BLK))
        query_par = column(chosen(par, block * BLK))
        for back in range(TREE_MOST):
            key_block = block - (TREE_MOST - 1) + back
            if key_block >= 0:
                key_seg = chosen(seg, key_block * BLK)
                key_par = chosen(par, key_block * BLK)
            else:
                at = REACH + key_block * BLK
                key_seg = chosen(halo_info.at[0], at)
                key_par = chosen(halo_info.at[1], at)
            related = (key_seg == query_seg) | (key_seg == query_par) | (key_par == key_seg)
            if back == TREE_MOST - 1:
                causal = lax.broadcasted_iota(jnp.int32, (BLK, BLK), 1) <= lax.broadcasted_iota(
                    jnp.int32, (BLK, BLK), 0
                )
                allowed = related & causal
            else:
                allowed = related & (first_block + key_block >= begin)
            bias[place, :, back * BLK : (back + 1) * BLK] = jnp.where(allowed, 0.0, NEG)

    payload_of = functools.partial(pick, [payload for payload, _ in blocks])
    block_of = functools.partial(pick, [block for _, block in blocks])

    def path_of(place):
        payload = payload_of(place)
        return jnp.where(payload == 0, swap_path, 1 - swap_path)

    counter[0] = 0

    def body(query_ref, out_ref):
        step = counter[0]
        counter[0] = step + 1
        place, head = (lax.div(step, kv_heads), lax.rem(step, kv_heads))
        for at, (payload, block) in enumerate(blocks):

            @pl.when((place == at) & (head == 0))
            def _():
                build_bias(at, payload, block)

        payload = payload_of(place)
        window = pl.ds(pl.multiple_of(block_of(place) * BLK + (lead - REACH), BLK), SPAN)
        lanes = pl.ds(pl.multiple_of(head * HEAD, HEAD), HEAD)
        key = kbuf[payload, window, lanes]
        value = vbuf[payload, window, lanes]
        for first in range(0, group, TOGETHER):
            heads = range(first, first + TOGETHER)
            query = jnp.concatenate([query_ref[0, :, g * HEAD : (g + 1) * HEAD] for g in heads], axis=0)
            scores = lax.dot_general(query, key, (((1,), (1,)), ((), ())), preferred_element_type=jnp.float32)
            scores = scores.reshape(TOGETHER, BLK, SPAN) + bias[place][None]
            top = jnp.max(scores, axis=-1, keepdims=True)
            weights = jnp.exp2((scores - top) * FACTOR)
            totals = jnp.sum(weights, axis=-1, keepdims=True)
            rounded = weights.astype(jnp.bfloat16).reshape(TOGETHER * BLK, SPAN)
            mixed = lax.dot_general(rounded, value, (((1,), (0,)), ((), ())), preferred_element_type=jnp.float32)
            mixed = (mixed.reshape(TOGETHER, BLK, HEAD) / totals).astype(jnp.bfloat16)
            for at, g in enumerate(heads):
                out_ref[:, g * HEAD : (g + 1) * HEAD] = mixed[at]

    pltpu.emit_pipeline(
        body,
        grid=(len(blocks), kv_heads),
        in_specs=[pl.BlockSpec((1, BLK, width), lambda i, h: (path_of(i), block_of(i), h))],
        out_specs=[pl.BlockSpec((BLK, width), lambda i, h: (i, h))],
    )(queries, out)
    for copy in packing:
        copy.wait()


def attend(blocks, operands, after=(), halo=None, pack=False):
    lengths, queries, keys, values, seg, par = operands
    rows, columns = queries.shape[1:]
    kv_heads = keys.shape[2] // HEAD
    held = rows + (REACH if halo else 0)
    out_shape = [jax.ShapeDtypeStruct((len(blocks) * BLK, columns), jnp.bfloat16)]
    out_specs = [ANY]
    if pack:
        out_shape.append(jax.ShapeDtypeStruct((2, 2, REACH, keys.shape[2]), jnp.bfloat16))
        out_shape.append(jax.ShapeDtypeStruct((2, 2, REACH), jnp.int32))
        out_specs += [ANY, VMEM]
    taken = 6 + (2 if halo else 0)

    def kernel(*refs):
        return attend_kernel(blocks, halo is not None, pack, *refs[:taken], *refs[taken + len(after) :])

    return pl.pallas_call(
        kernel,
        out_shape=out_shape,
        in_specs=[HBM] * 6 + ([ANY, VMEM] if halo else []) + [ANY] * len(after),
        out_specs=out_specs,
        scratch_shapes=[
            pltpu.VMEM((2, held, keys.shape[2]), jnp.bfloat16),
            pltpu.VMEM((2, held, keys.shape[2]), jnp.bfloat16),
            pltpu.VMEM((len(blocks), BLK, SPAN), jnp.float32),
            pltpu.VMEM(seg.shape, jnp.int32),
            pltpu.VMEM(par.shape, jnp.int32),
            pltpu.SMEM(lengths.shape, jnp.int32),
            pltpu.SMEM((1,), jnp.int32),
            pltpu.SemaphoreType.DMA((16,)),
        ]
        + ([pltpu.VMEM((2, 2, REACH, keys.shape[2]), jnp.bfloat16)] if pack else []),
        compiler_params=pltpu.CompilerParams(vmem_limit_bytes=VMEM_LIMIT),
        cost_estimate=COST,
    )(lengths, queries, keys, values, seg, par, *(halo or ()), *after)


def behind(value, *after):
    return pl.pallas_call(
        lambda *refs: None,
        out_shape=jax.ShapeDtypeStruct(value.shape, value.dtype),
        in_specs=[ANY] * (1 + len(after)),
        out_specs=ANY,
        input_output_aliases={0: 0},
        cost_estimate=COST,
    )(value, *after)


def place_kernel(held, aliased, *refs):
    pieces = refs[: len(held)]
    forward, back, stage, in_sems, out_sems = refs[len(held) + aliased :]
    place = lax.axis_index("pipe")
    even = lax.rem(place, 2) == 0
    edge = (place == 0) | (place == lax.axis_size("pipe") - 1)

    def go(kinds, even_here):
        moves = []
        for piece, (kind, blocks) in zip(pieces, held):
            if kind in kinds:
                target = forward if even_here == (kind != "swap") else back
                moves += [(piece, at, target, block) for at, block in enumerate(blocks)]
        loads = [
            pltpu.make_async_copy(piece.at[pl.ds(at * BLK, BLK)], stage.at[i], in_sems.at[i])
            for i, (piece, at, _, _) in enumerate(moves)
        ]
        stores = [
            pltpu.make_async_copy(stage.at[i], target.at[pl.ds(block * BLK, BLK)], out_sems.at[i])
            for i, (_, _, target, block) in enumerate(moves)
        ]
        for load in loads:
            load.start()
        for load, store in zip(loads, stores):
            load.wait()
            store.start()
        for store in stores:
            store.wait()

    for kinds, there in ((("swap", "own"), edge), (("swap", "far"), jnp.logical_not(edge))):
        if any(kind in kinds for kind, _ in held):
            for even_here in (True, False):

                @pl.when(there & (even == even_here))
                def _():
                    go(kinds, even_here)


def place(pieces, rows, outs=()):
    columns = pieces[0][1].shape[1]
    shape = jax.ShapeDtypeStruct((rows, columns), jnp.bfloat16)
    count = sum(len(blocks) for _, _, blocks in pieces)
    return pl.pallas_call(
        functools.partial(place_kernel, [(kind, blocks) for kind, _, blocks in pieces], len(outs)),
        out_shape=[shape, shape],
        in_specs=[ANY] * len(pieces) + [HBM] * len(outs),
        out_specs=[HBM, HBM],
        scratch_shapes=[
            pltpu.VMEM((count, BLK, columns), jnp.bfloat16),
            pltpu.SemaphoreType.DMA((count,)),
            pltpu.SemaphoreType.DMA((count,)),
        ],
        input_output_aliases={len(pieces) + i: i for i in range(len(outs))},
        compiler_params=pltpu.CompilerParams(vmem_limit_bytes=24 * 1024 * 1024),
        cost_estimate=COST,
    )(*(array for _, array, _ in pieces), *outs)


COST = pl.CostEstimate(flops=1024, bytes_accessed=1024, transcendentals=0)

SWAP = [(0, 1), (1, 0), (2, 3), (3, 2)]
DIAGONAL = [(1, 2), (2, 1)]
ACROSS = [(1, 3), (2, 0)]
ONWARD = [(3, 2), (0, 1)]


def on_device(queries, keys, values, segment, parent, tree_lengths):
    rows = queries.shape[2]
    operands = (tree_lengths[0], queries[0], keys[0], values[0], segment[0], parent[0])
    ring = [(source, source + 1) for source in range(lax.axis_size("dp") - 1)]

    swap_1, halo_kv, halo_info = attend([(0, 2), (0, 3)], operands, pack=True)
    got_1 = lax.ppermute(swap_1, "pipe", SWAP)
    halo = (lax.ppermute(halo_kv, "dp", ring), lax.ppermute(halo_info, "dp", ring))
    (routed_1,) = attend([(1, 2)], operands, after=(swap_1,))
    across_1 = lax.ppermute(routed_1, "pipe", ACROSS)
    (routed_2,) = attend([(1, 3)], operands, after=(routed_1,))
    across_2 = lax.ppermute(routed_2, "pipe", ACROSS)
    (swap_2,) = attend([(0, 0), (0, 1)], operands, after=(routed_2,), halo=halo)
    got_2 = lax.ppermute(swap_2, "pipe", SWAP)
    (direct,) = attend([(1, 0), (1, 1)], operands, after=(swap_2, got_1), halo=halo)
    diagonal = lax.ppermute(direct, "pipe", DIAGONAL)
    onward_1 = lax.ppermute(behind(across_1, direct), "pipe", ONWARD)
    onward_2 = lax.ppermute(behind(across_2, direct), "pipe", ONWARD)
    outs = place(
        [("swap", got_1, [2, 3]), ("own", direct, [0, 1]), ("own", routed_1, [2]), ("own", routed_2, [3])], rows
    )
    forward, back = place(
        [("swap", got_2, [0, 1]), ("far", diagonal, [0, 1]), ("far", onward_1, [2]), ("far", onward_2, [3])], rows, outs
    )
    return (forward[None], back[None])


def solution(mesh):
    return jax.shard_map(
        on_device,
        mesh=mesh,
        in_specs=(
            P("pipe", None, "dp", None),
            P("pipe", None, "dp", None),
            P("pipe", None, "dp", None),
            P("pipe", None, "dp"),
            P("pipe", None, "dp"),
            P("pipe", None, None),
        ),
        out_specs=(P("pipe", "dp", None), P("pipe", "dp", None)),
        check_vma=False,
    )
```

time: 496 us -> 156 us (0.31); the launches traced: 487 us -> 154 us
  local copies, waits for them, and re-layouts: 144 us -> 5.69 us
  waiting for transfers between devices: 169 us -> 76.8 us
  matrix products: 69.9 us -> 0 us
  other arithmetic: 69.8 us -> 0 us
  Pallas kernels: 0 us -> 51.8 us
  starting transfers between devices: 32.6 us -> 19 us
    ppermute x14 -> x9, waiting for transfers between devices: 169 us -> 76.8 us  [the longest x1 22.5 us: on_device(): onward_1 = lax.ppermute(behind(across_1, direct), 'pipe', ONWARD)]
    dot_general x8 -> x0, matrix products: 69.9 us -> none  [the longest x4 35.8 us: attend(): jnp.einsum('ahgqk,akhd->aqhgd', rounded, valueset, preferred_element_type...]
    pallas_call x0 -> x9, Pallas kernels: none -> 51.8 us  [the longest x5 45.5 us: attend(): pl.pallas_call(kernel, out_shape=out_shape, in_specs=[HBM] * 6 + ([ANY, V...]
    slice x37 -> x0, local copies, waits for them, and re-layouts: 37.4 us -> none  [the longest x27 23.4 us: windowed(): lax.slice_in_dim(rows, (index + offset) * BLK, (index + offset) * BLK + s...]
    another operation x43 -> x0, local copies, waits for them, and re-layouts: 31.3 us -> none  [the longest x40 30.3 us: windowed(): jnp.stack([lax.slice_in_dim(rows, (index + offset) * BLK, (index + offset...]
    reduce_sum x4 -> x0, other arithmetic: 30.9 us -> none  [attend(): totals = jnp.sum(weights, axis=-1)]
    unnamed x137 -> x14, local copies, waits for them, and re-layouts: 29.3 us -> 5.69 us
    convert_element_type x4 -> x0, local copies, waits for them, and re-layouts: 22.7 us -> none  [attend(): (mixed / totals).astype(jnp.bfloat16).reshape(group_count * BLK, -1)]
  transfers between devices with their start and end apart: 14 -> 9, of which waited for: 4 -> 4; matrix products, arithmetic and copies ran while one was open for 54% -> 0% of each run, Pallas kernels for 0% -> 23%
where the time goes in v1:
time: 156 us; the launch traced here: 154 us
  waiting for transfers between devices  76.8 us (49%)
  Pallas kernels  51.8 us (33%)
  starting transfers between devices  19 us (12%)
  local copies, waits for them, and re-layouts  5.69 us (4%)
    pallas_call x5, Pallas kernels, attend(): pl.pallas_call(kernel, out_shape=out_shape, in_specs=[HBM] * 6 + ([ANY, V...  45.5 us
    ppermute x1, waiting for transfers between devices, on_device(): onward_1 = lax.ppermute(behind(across_1, direct), 'pipe', ONWARD)  22.5 us
    ppermute x1, waiting for transfers between devices, on_device(): got_2 = lax.ppermute(swap_2, 'pipe', SWAP)  22.2 us
    ppermute x1, waiting for transfers between devices, on_device(): onward_2 = lax.ppermute(behind(across_2, direct), 'pipe', ONWARD)  21.2 us
    ppermute x1, waiting for transfers between devices, on_device(): got_1 = lax.ppermute(swap_1, 'pipe', SWAP)  10.8 us
    pallas_call x2, Pallas kernels, place(): pl.pallas_call(functools.partial(place_kernel, [(kind, blocks) for kind,...  6.3 us
    unnamed x14, local copies, waits for them, and re-layouts  5.69 us
    ppermute x1, starting transfers between devices, on_device(): lax.ppermute(halo_info, 'dp', ring)  3.59 us
  transfers between devices with their start and end apart: 9, of which 4 were waited for; matrix products, arithmetic and copies ran while one was open for 0% of the time, Pallas kernels for 23%

profile of v1, /device:TPU:20, one launch (start us, length us, event | category | flops | bytes accessed | tf_op | source)
XLA Modules:
  0.0 154.0 jit_solution(14001234987086017343)
XLA Ops:
  0.6 11.1 %shard_map.77 = (bf16[256,4096]{1,0:T(8,128)(2,1)}, bf16[2,2,256,512]{3,2,1,0:T(8,128)(2,1)}, s32[2,2,256]{2,1,0:T(2,128)}) custom-call(s32[2,32]{1,0:T(2,128)} %bitcast.35, bf16[2,512,4096]{2,1,0:T(8,128)(2,1)} %bitcast.8, bf16[2,512,512]{2,1,0:T(8,128)(2,1)} %bitcast.13, bf16[2,512,512]{2,1,0:T(8,128)(2,1)} %bitcast.18, s32[2,512]{1,0:T(2,128)} %bitcast.25, ...), custom_call_target="tpu_custom_call" | custom-call | flops 1024 | bytes 1024 | tf_op jit(solution)/shard_map/pallas_call | solution.py:189
  11.7 1.6 %collective-permute-start.3 = (bf16[256,4096]{1,0:T(8,128)(2,1)}, bf16[256,4096]{1,0:T(8,128)(2,1)S(1)}, u32[]{:S(2)}, u32[]{:S(2)}) collective-permute-start(bf16[256,4096]{1,0:T(8,128)(2,1)} %get-tuple-element.11.refs_6_), channel_id=1, source_target_pairs={{0,8},{8,0},{16,24},{24,16},{1,9},{9,1},{17,25},{25,17},{2,10},{10... | collective-permute-start | bytes 6291464 | tf_op jit(solution)/shard_map/ppermute | solution.py:293
  13.3 1.9 %collective-permute-start = (bf16[2,2,256,512]{3,2,1,0:T(8,128)(2,1)}, bf16[2,2,256,512]{3,2,1,0:T(8,128)(2,1)S(1)}, u32[]{:S(2)}, u32[]{:S(2)}) collective-permute-start(bf16[2,2,256,512]{3,2,1,0:T(8,128)(2,1)} %get-tuple-element.9), channel_id=1, source_target_pairs={{0,1},{1,2},{2,3},{3,4},{4,5},{5,6},{6,7},{8,9},{9,10},{10,11},{11... | collective-permute-start | bytes 3145736 | tf_op jit(solution)/shard_map/ppermute | solution.py:294
  15.2 3.6 %collective-permute-start.1 = (s32[2,2,256]{2,1,0:T(2,128)}, s32[2,2,256]{2,1,0:T(2,128)S(1)}, u32[]{:S(2)}, u32[]{:S(2)}) collective-permute-start(s32[2,2,256]{2,1,0:T(2,128)} %get-tuple-element.10), channel_id=1, source_target_pairs={{0,1},{1,2},{2,3},{3,4},{4,5},{5,6},{6,7},{8,9},{9,10},{10,11},{11... | collective-permute-start | bytes 12296 | tf_op jit(solution)/shard_map/ppermute | solution.py:294
  18.8 6.4 %shard_map.78.refs_6_.refs_2_ = bf16[128,4096]{1,0:T(8,128)(2,1)} custom-call(s32[2,32]{1,0:T(2,128)} %bitcast.36, bf16[2,512,4096]{2,1,0:T(8,128)(2,1)} %bitcast.9, bf16[2,512,512]{2,1,0:T(8,128)(2,1)} %bitcast.14, bf16[2,512,512]{2,1,0:T(8,128)(2,1)} %bitcast.19, s32[2,512]{1,0:T(2,128)} %bitcast.26, s32[2,512]{1,0:T(2,128)} %bitcast.31, ...), custom_call_target="tpu_custom_call" | custom-call | flops 1024 | bytes 1024 | tf_op jit(solution)/shard_map/pallas_call | solution.py:189
  25.2 3.4 %collective-permute-start.5 = (bf16[128,4096]{1,0:T(8,128)(2,1)}, bf16[128,4096]{1,0:T(8,128)(2,1)}, u32[]{:S(2)}, u32[]{:S(2)}) collective-permute-start(bf16[128,4096]{1,0:T(8,128)(2,1)} %shard_map.78.refs_6_.refs_2_), channel_id=1, source_target_pairs={{8,24},{16,0},{9,25},{17,1},{10,26},{18,2},{11,27},{19,3},{12,28},... | collective-permute-start | bytes 3145736 | tf_op jit(solution)/shard_map/ppermute | solution.py:296
  28.6 6.3 %shard_map.79.refs_8_.refs_3_ = bf16[128,4096]{1,0:T(8,128)(2,1)} custom-call(s32[2,32]{1,0:T(2,128)} %bitcast.37, bf16[2,512,4096]{2,1,0:T(8,128)(2,1)} %bitcast.10, bf16[2,512,512]{2,1,0:T(8,128)(2,1)} %bitcast.15, bf16[2,512,512]{2,1,0:T(8,128)(2,1)} %bitcast.20, s32[2,512]{1,0:T(2,128)} %bitcast.27, s32[2,512]{1,0:T(2,128)} %bitcast.32, ...), custom_call_target="tpu_custom_call" | custom-call | flops 1024 | bytes 1024 | tf_op jit(solution)/shard_map/pallas_call | solution.py:189
  34.9 2.3 %collective-permute-start.7 = (bf16[128,4096]{1,0:T(8,128)(2,1)}, bf16[128,4096]{1,0:T(8,128)(2,1)}, u32[]{:S(2)}, u32[]{:S(2)}) collective-permute-start(bf16[128,4096]{1,0:T(8,128)(2,1)} %shard_map.79.refs_8_.refs_3_), channel_id=1, source_target_pairs={{8,24},{16,0},{9,25},{17,1},{10,26},{18,2},{11,27},{19,3},{12,28},... | collective-permute-start | bytes 3145736 | tf_op jit(solution)/shard_map/ppermute | solution.py:298
  37.2 0.0 collective-permute-done.1.refs_7_
  37.2 0.0 collective-permute-done.refs_6_
  37.2 0.6 copy-done.6
  37.8 1.0 copy-done.5
  38.7 10.9 %shard_map.80.refs_8_ = bf16[256,4096]{1,0:T(8,128)(2,1)} custom-call(s32[2,32]{1,0:T(2,128)} %bitcast.38, bf16[2,512,4096]{2,1,0:T(8,128)(2,1)} %bitcast.11, bf16[2,512,512]{2,1,0:T(8,128)(2,1)} %bitcast.16, bf16[2,512,512]{2,1,0:T(8,128)(2,1)} %bitcast.21, s32[2,512]{1,0:T(2,128)} %bitcast.28, s32[2,512]{1,0:T(2,128)} %bitcast.33, ...), custom_call_target="tpu_custom_call" | custom-call | flops 1024 | bytes 1024 | tf_op jit(solution)/shard_map/pallas_call | solution.py:189
  49.6 0.1 collective-permute-start.2
  49.7 10.8 %collective-permute-done.3.refs_9_.refs_0_ = bf16[256,4096]{1,0:T(8,128)(2,1)S(1)} collective-permute-done((bf16[256,4096]{1,0:T(8,128)(2,1)}, bf16[256,4096]{1,0:T(8,128)(2,1)S(1)}, u32[]{:S(2)}, u32[]{:S(2)}) %collective-permute-start.3) | collective-permute-done | bytes 2097184 | tf_op jit(solution)/shard_map/ppermute | solution.py:293
  60.5 1.3 copy-done.3
  61.8 10.8 %shard_map.81.refs_1_ = bf16[256,4096]{1,0:T(8,128)(2,1)} custom-call(s32[2,32]{1,0:T(2,128)} %bitcast.39, bf16[2,512,4096]{2,1,0:T(8,128)(2,1)} %bitcast.12, bf16[2,512,512]{2,1,0:T(8,128)(2,1)} %bitcast.17, bf16[2,512,512]{2,1,0:T(8,128)(2,1)} %bitcast.22, s32[2,512]{1,0:T(2,128)} %bitcast.29, s32[2,512]{1,0:T(2,128)} %bitcast.34, ...), custom_call_target="tpu_custom_call" | custom-call | flops 1024 | bytes 1024 | tf_op jit(solution)/shard_map/pallas_call | solution.py:189
  72.7 3.3 %collective-permute-start.4 = (bf16[256,4096]{1,0:T(8,128)(2,1)}, bf16[256,4096]{1,0:T(8,128)(2,1)}, u32[]{:S(2)}, u32[]{:S(2)}) collective-permute-start(bf16[256,4096]{1,0:T(8,128)(2,1)} %shard_map.81.refs_1_), channel_id=1, source_target_pairs={{8,16},{16,8},{9,17},{17,9},{10,18},{18,10},{11,19},{19,11},{12,20... | collective-permute-start | bytes 6291464 | tf_op jit(solution)/shard_map/ppermute | solution.py:302
  76.0 0.0 collective-permute-done.5.refs_0_
  76.1 1.6 %collective-permute-start.6 = (bf16[128,4096]{1,0:T(8,128)(2,1)}, bf16[128,4096]{1,0:T(8,128)(2,1)}, u32[]{:S(2)}, u32[]{:S(2)}) collective-permute-start(bf16[128,4096]{1,0:T(8,128)(2,1)} %shard_map.82), channel_id=1, source_target_pairs={{24,16},{0,8},{25,17},{1,9},{26,18},{2,10},{27,19},{3,11},{28,20},... | collective-permute-start | bytes 3145736 | tf_op jit(solution)/shard_map/ppermute | solution.py:303
  77.6 0.0 collective-permute-done.7.refs_0_
  77.6 1.3 collective-permute-start.8
  78.9 0.0 copy-done
  79.0 0.0 copy-done.1
  79.0 1.2 copy-done.2
  80.2 1.6 %copy-done.4 = bf16[256,4096]{1,0:T(8,128)(2,1)S(1)} copy-done((bf16[256,4096]{1,0:T(8,128)(2,1)S(1)}, bf16[256,4096]{1,0:T(8,128)(2,1)}, u32[]{:S(2)}) %copy-start.4) | copy-done | bytes 2097176
  81.8 1.6 %shard_map.84 = (bf16[512,4096]{1,0:T(8,128)(2,1)}, bf16[512,4096]{1,0:T(8,128)(2,1)}) custom-call(bf16[256,4096]{1,0:T(8,128)(2,1)S(1)} %copy-done.4, bf16[256,4096]{1,0:T(8,128)(2,1)S(1)} %copy-done, bf16[128,4096]{1,0:T(8,128)(2,1)S(1)} %copy-done.1, bf16[128,4096]{1,0:T(8,128)(2,1)S(1)} %copy-done.2), custom_call_target="tpu_custom_call" | custom-call | flops 1024 | bytes 1024 | tf_op jit(solution)/shard_map/pallas_call | solution.py:263
  83.4 22.2 %collective-permute-done.2.refs_0_ = bf16[256,4096]{1,0:T(8,128)(2,1)} collective-permute-done((bf16[256,4096]{1,0:T(8,128)(2,1)}, bf16[256,4096]{1,0:T(8,128)(2,1)}, u32[]{:S(2)}, u32[]{:S(2)}) %collective-permute-start.2) | collective-permute-done | bytes 2097184 | tf_op jit(solution)/shard_map/ppermute | solution.py:300
  105.6 22.5 %collective-permute-done.6.refs_2_ = bf16[128,4096]{1,0:T(8,128)(2,1)} collective-permute-done((bf16[128,4096]{1,0:T(8,128)(2,1)}, bf16[128,4096]{1,0:T(8,128)(2,1)}, u32[]{:S(2)}, u32[]{:S(2)}) %collective-permute-start.6) | collective-permute-done | bytes 1048608 | tf_op jit(solution)/shard_map/ppermute | solution.py:303
  128.0 21.2 %collective-permute-done.8.refs_3_ = bf16[128,4096]{1,0:T(8,128)(2,1)S(1)} collective-permute-done((bf16[128,4096]{1,0:T(8,128)(2,1)}, bf16[128,4096]{1,0:T(8,128)(2,1)S(1)}, u32[]{:S(2)}, u32[]{:S(2)}) %collective-permute-start.8) | collective-permute-done | bytes 1048608 | tf_op jit(solution)/shard_map/ppermute | solution.py:304
  149.3 0.0 collective-permute-done.4.refs_1_
  149.3 4.7 %shard_map.85 = (bf16[512,4096]{1,0:T(8,128)(2,1)}, bf16[512,4096]{1,0:T(8,128)(2,1)}) custom-call(bf16[256,4096]{1,0:T(8,128)(2,1)} %collective-permute-done.2.refs_0_, bf16[256,4096]{1,0:T(8,128)(2,1)} %collective-permute-done.4.refs_1_, bf16[128,4096]{1,0:T(8,128)(2,1)} %collective-permute-done.6.refs_2_, ...), custom_call_target="tpu_custom_call", output_to_operand_aliasing={{0}: (4, {}), {1}: (5, {})} | custom-call | flops 1024 | bytes 1024 | tf_op jit(solution)/shard_map/pallas_call | solution.py:263
  (9 shorter events, 0.0 us)
Async XLA Ops:
  11.7 48.8 %collective-permute-start.3 = (bf16[256,4096]{1,0:T(8,128)(2,1)}, bf16[256,4096]{1,0:T(8,128)(2,1)S(1)}, u32[]{:S(2)}, u32[]{:S(2)}) collective-permute-start(bf16[256,4096]{1,0:T(8,128)(2,1)} %get-tuple-element.11.refs_6_), channel_id=1, source_target_pairs={{0,8},{8,0},{16,24},{24,16},{1,9},{9,1},{17,25},{25,17},{2,10},{10... | collective-permute-start | bytes 6291464 | tf_op jit(solution)/shard_map/ppermute | solution.py:293
  13.3 23.9 %collective-permute-start = (bf16[2,2,256,512]{3,2,1,0:T(8,128)(2,1)}, bf16[2,2,256,512]{3,2,1,0:T(8,128)(2,1)S(1)}, u32[]{:S(2)}, u32[]{:S(2)}) collective-permute-start(bf16[2,2,256,512]{3,2,1,0:T(8,128)(2,1)} %get-tuple-element.9), channel_id=1, source_target_pairs={{0,1},{1,2},{2,3},{3,4},{4,5},{5,6},{6,7},{8,9},{9,10},{10,11},{11... | collective-permute-start | bytes 3145736 | tf_op jit(solution)/shard_map/ppermute | solution.py:294
  15.2 22.0 %collective-permute-start.1 = (s32[2,2,256]{2,1,0:T(2,128)}, s32[2,2,256]{2,1,0:T(2,128)S(1)}, u32[]{:S(2)}, u32[]{:S(2)}) collective-permute-start(s32[2,2,256]{2,1,0:T(2,128)} %get-tuple-element.10), channel_id=1, source_target_pairs={{0,1},{1,2},{2,3},{3,4},{4,5},{5,6},{6,7},{8,9},{9,10},{10,11},{11... | collective-permute-start | bytes 12296 | tf_op jit(solution)/shard_map/ppermute | solution.py:294
  25.2 50.9 %collective-permute-start.5 = (bf16[128,4096]{1,0:T(8,128)(2,1)}, bf16[128,4096]{1,0:T(8,128)(2,1)}, u32[]{:S(2)}, u32[]{:S(2)}) collective-permute-start(bf16[128,4096]{1,0:T(8,128)(2,1)} %shard_map.78.refs_6_.refs_2_), channel_id=1, source_target_pairs={{8,24},{16,0},{9,25},{17,1},{10,26},{18,2},{11,27},{19,3},{12,28},... | collective-permute-start | bytes 3145736 | tf_op jit(solution)/shard_map/ppermute | solution.py:296
  34.9 42.7 %collective-permute-start.7 = (bf16[128,4096]{1,0:T(8,128)(2,1)}, bf16[128,4096]{1,0:T(8,128)(2,1)}, u32[]{:S(2)}, u32[]{:S(2)}) collective-permute-start(bf16[128,4096]{1,0:T(8,128)(2,1)} %shard_map.79.refs_8_.refs_3_), channel_id=1, source_target_pairs={{8,24},{16,0},{9,25},{17,1},{10,26},{18,2},{11,27},{19,3},{12,28},... | collective-permute-start | bytes 3145736 | tf_op jit(solution)/shard_map/ppermute | solution.py:298
  37.2 0.6 copy-start.6
  37.8 1.0 copy-start.5
  49.6 55.9 %collective-permute-start.2 = (bf16[256,4096]{1,0:T(8,128)(2,1)}, bf16[256,4096]{1,0:T(8,128)(2,1)}, u32[]{:S(2)}, u32[]{:S(2)}) collective-permute-start(bf16[256,4096]{1,0:T(8,128)(2,1)} %shard_map.80.refs_8_), channel_id=1, source_target_pairs={{0,8},{8,0},{16,24},{24,16},{1,9},{9,1},{17,25},{25,17},{2,10},{10... | collective-permute-start | bytes 6291464 | tf_op jit(solution)/shard_map/ppermute | solution.py:300
  60.5 1.3 copy-start.3
  72.7 76.6 %collective-permute-start.4 = (bf16[256,4096]{1,0:T(8,128)(2,1)}, bf16[256,4096]{1,0:T(8,128)(2,1)}, u32[]{:S(2)}, u32[]{:S(2)}) collective-permute-start(bf16[256,4096]{1,0:T(8,128)(2,1)} %shard_map.81.refs_1_), channel_id=1, source_target_pairs={{8,16},{16,8},{9,17},{17,9},{10,18},{18,10},{11,19},{19,11},{12,20... | collective-permute-start | bytes 6291464 | tf_op jit(solution)/shard_map/ppermute | solution.py:302
  76.0 2.9 %copy-start = (bf16[256,4096]{1,0:T(8,128)(2,1)S(1)}, bf16[256,4096]{1,0:T(8,128)(2,1)}, u32[]{:S(2)}) copy-start(bf16[256,4096]{1,0:T(8,128)(2,1)} %shard_map.81.refs_1_) | copy-start | bytes 6291460
  76.1 2.9 %copy-start.1 = (bf16[128,4096]{1,0:T(8,128)(2,1)S(1)}, bf16[128,4096]{1,0:T(8,128)(2,1)}, u32[]{:S(2)}) copy-start(bf16[128,4096]{1,0:T(8,128)(2,1)} %shard_map.78.refs_6_.refs_2_) | copy-start | bytes 3145732
  76.1 52.0 %collective-permute-start.6 = (bf16[128,4096]{1,0:T(8,128)(2,1)}, bf16[128,4096]{1,0:T(8,128)(2,1)}, u32[]{:S(2)}, u32[]{:S(2)}) collective-permute-start(bf16[128,4096]{1,0:T(8,128)(2,1)} %shard_map.82), channel_id=1, source_target_pairs={{24,16},{0,8},{25,17},{1,9},{26,18},{2,10},{27,19},{3,11},{28,20},... | collective-permute-start | bytes 3145736 | tf_op jit(solution)/shard_map/ppermute | solution.py:303
  77.6 71.6 %collective-permute-start.8 = (bf16[128,4096]{1,0:T(8,128)(2,1)}, bf16[128,4096]{1,0:T(8,128)(2,1)S(1)}, u32[]{:S(2)}, u32[]{:S(2)}) collective-permute-start(bf16[128,4096]{1,0:T(8,128)(2,1)} %shard_map.83), channel_id=1, source_target_pairs={{24,16},{0,8},{25,17},{1,9},{26,18},{2,10},{27,19},{3,11},{28,20},... | collective-permute-start | bytes 3145736 | tf_op jit(solution)/shard_map/ppermute | solution.py:304
  79.0 1.2 copy-start.2
  80.2 1.6 %copy-start.4 = (bf16[256,4096]{1,0:T(8,128)(2,1)S(1)}, bf16[256,4096]{1,0:T(8,128)(2,1)}, u32[]{:S(2)}) copy-start(bf16[256,4096]{1,0:T(8,128)(2,1)} %copy-done.3) | copy-start | bytes 6291460

commit v2 on v0

v2 whole, which is shorter than its diff:
```python
import functools
import math

import jax
import jax.numpy as jnp
from jax import lax
from jax.experimental import pallas as pl
from jax.experimental.pallas import tpu as pltpu
from jax.sharding import PartitionSpec as P

BLK = 128
TREE_MOST = 3
KV_HEADS = 4
HEAD = 128
REACH = (TREE_MOST - 1) * BLK
SPAN = TREE_MOST * BLK
NEG = -1e30
FACTOR = math.log2(math.e) / math.sqrt(HEAD)

HALF = BLK // 2
CORNER = HALF + 16
INFO = 16
VMEM_LIMIT = 60 * 1024 * 1024

ANY = pl.BlockSpec(memory_space=pl.ANY)
HBM = pl.BlockSpec(memory_space=pltpu.HBM)


def flipped(array):
    count = array.shape[0]
    rows = lax.broadcasted_iota(jnp.int32, (count, count), 0)
    lanes = lax.broadcasted_iota(jnp.int32, (count, count), 1)
    swap = (rows + lanes == count - 1).astype(jnp.bfloat16)
    return jnp.dot(swap, array, preferred_element_type=jnp.float32).astype(jnp.bfloat16)


def stacked(array):
    return jnp.concatenate([array[:, at : at + HEAD] for at in range(0, array.shape[1], HEAD)], axis=0)


def product(left, right):
    return jnp.dot(left, right, preferred_element_type=jnp.float32)


def product_t(left, right):
    return lax.dot_general(left, right, (((1,), (1,)), ((), ())), preferred_element_type=jnp.float32)


def sides():
    lane = lax.broadcasted_iota(jnp.int32, (HALF, BLK), 1)
    gap = lax.broadcasted_iota(jnp.int32, (HALF, BLK), 0) + HALF
    return (lane < gap, lane > gap)


def plain_block(first, at):
    return at + (first <= at).astype(jnp.int32)


def attend_kernel(payload, groups, items, corner, pack, halo, *refs):
    heads = [head for group in groups for head in group]
    refs = list(refs)
    lengths_in, queries, keys, values, seg_in, par_in = refs[:6]
    refs = refs[6:]
    halo_in = refs.pop(0) if halo else None
    outs = [refs.pop(0) for _ in groups]
    pack_out = refs.pop(0) if pack else None
    kbuf, vbuf, bias, segs, pars, seg, par, lengths, marks, sems = refs[:10]
    refs = refs[10:]
    if halo:
        info = refs.pop(0)
    if corner:
        corner_q, corner_out = refs[:2]
        refs = refs[2:]
    if pack:
        packed = refs.pop(0)
    rows = keys.shape[1]
    kv_heads = keys.shape[2] // HEAD
    width = queries.shape[2] // kv_heads
    group = width // HEAD
    count = rows // BLK
    taken = len(heads)
    path = lax.rem(lax.axis_index("pipe"), 2)
    path = path if payload == 0 else 1 - path
    first_block = lax.axis_index("dp") * count
    lanes = pl.ds(heads[0] * HEAD, taken * HEAD)

    started = []

    def start(source, target):
        copy = pltpu.make_async_copy(source, target, sems.at[len(started)])
        copy.start()
        started.append(copy)
        return copy

    lengths_copy = start(lengths_in, lengths)
    row_copies = [start(seg_in, segs), start(par_in, pars)]
    kv_copies = []
    for which, (source, target) in enumerate(((keys, kbuf), (values, vbuf))):
        kv_copies.append(start(source.at[path, :, lanes], target.at[pl.ds(REACH, rows)]))
        if halo:
            kv_copies.append(start(halo_in.at[which, path, pl.ds(0, REACH), lanes], target.at[pl.ds(0, REACH)]))
    if halo:
        row_copies.append(start(halo_in.at[0, path, pl.ds(REACH, INFO)], info))
    pack_copies = []
    if pack:
        for each in range(2):
            for which, source in enumerate((keys, values)):
                source = source.at[each, pl.ds(rows - REACH, REACH)]
                pack_copies.append(start(source, packed.at[which, each, pl.ds(0, REACH)]))

    lengths_copy.wait()

    def step(entry, carry):
        end, begins = carry
        end = end + lengths[path, entry]
        return (end, tuple(jnp.where(end <= first_block + at, end, begin) for at, begin in enumerate(begins)))

    zero = jnp.int32(0)
    _, begins = lax.fori_loop(0, lengths.shape[1], step, (zero, (zero,) * count))
    first = jnp.int32(count - 1)
    for at in reversed(range(count)):
        marks[at] = begins[at]
        first = jnp.where(begins[at] == first_block + at, at, first)
    if corner:
        columns = pl.ds(heads[0] * width, taken * width)
        query_copy = start(queries.at[path, pl.ds(pl.multiple_of(first * BLK, BLK), BLK), columns], corner_q)

    for copy in row_copies:
        copy.wait()
    for source, target in ((segs, seg), (pars, par)):
        target[:, REACH:] = jnp.where(path == 0, source[0:1], source[1:2])
    if halo:
        numbers = info[...].astype(jnp.float32)
        seg[:, :REACH] = (numbers[0:1, :REACH] * 128.0 + numbers[1:2, :REACH]).astype(jnp.int32)
        par[:, :REACH] = (numbers[2:3, :REACH] * 128.0 + numbers[3:4, :REACH]).astype(jnp.int32)
    if pack:
        for each in range(2):
            at = lax.broadcasted_iota(jnp.int32, (INFO, REACH), 0)
            numbers = jnp.zeros((INFO, REACH), jnp.int32)
            for which, source in enumerate((segs, pars)):
                row = source[each : each + 1, rows - REACH :]
                numbers = jnp.where(at == 2 * which, row >> 7, numbers)
                numbers = jnp.where(at == 2 * which + 1, row & 127, numbers)
            numbers = numbers.astype(jnp.float32).astype(jnp.bfloat16)
            packed[0, each, REACH:, :REACH] = numbers
            packed[0, each, REACH:, REACH:] = jnp.zeros((INFO, keys.shape[2] - REACH), jnp.bfloat16)
            packed[1, each, REACH:, :] = jnp.zeros((INFO, keys.shape[2]), jnp.bfloat16)
        for copy in pack_copies:
            copy.wait()
        pack_store = start(packed, pack_out)
    for copy in kv_copies:
        copy.wait()

    def column(row):
        return jnp.transpose(jnp.broadcast_to(row, (BLK, BLK)))

    def related(block, back):
        ours = pl.ds(pl.multiple_of(REACH + block * BLK, BLK), BLK)
        theirs = pl.ds(pl.multiple_of(REACH + (block - back) * BLK, BLK), BLK)
        key_seg = seg[:, theirs]
        query_seg, query_par = (column(seg[:, ours]), column(par[:, ours]))
        found = (key_seg == query_seg) | (key_seg == query_par) | (par[:, theirs] == key_seg)
        if back:
            return found & (first_block + block - back >= marks[block])
        lane = lax.broadcasted_iota(jnp.int32, (BLK, BLK), 1)
        return found & (lane <= lax.broadcasted_iota(jnp.int32, (BLK, BLK), 0))

    if corner:
        query_copy.wait()
        seen = related(first, 0).astype(jnp.float32).astype(jnp.bfloat16)
        turned = jnp.transpose(flipped(jnp.transpose(flipped(seen[:HALF]).astype(jnp.float32)).astype(jnp.bfloat16)).astype(jnp.float32))
        low_bias = jnp.where(seen[HALF:].astype(jnp.float32) > 0.5, 0.0, NEG)
        high_bias = jnp.where(turned > 0.5, 0.0, NEG)
        own_rows = pl.ds(pl.multiple_of(REACH + first * BLK, BLK), BLK)
        left, right = sides()

        def shares(query, key, mask):
            scores = product_t(query, key).reshape(group, HALF, BLK) + mask[None]
            top = jnp.max(scores, axis=-1, keepdims=True)
            weights = jnp.exp2((scores - top) * FACTOR)
            return weights / jnp.sum(weights, axis=-1, keepdims=True)

        for at in range(taken):
            key = kbuf[own_rows, at * HEAD : (at + 1) * HEAD]
            query = corner_q[:, at * width : (at + 1) * width]
            low = shares(stacked(query[HALF:]), key, low_bias)
            high = shares(stacked(flipped(query[:HALF])), flipped(key), high_bias)
            mixed = jnp.where(right[None], high, first.astype(jnp.float32))
            mixed = jnp.where(left[None], low, mixed).astype(jnp.bfloat16)
            value = vbuf[own_rows, at * HEAD : (at + 1) * HEAD]
            for g in range(group):
                place = slice(at * width + g * HEAD, at * width + (g + 1) * HEAD)
                corner_out[:HALF, place] = mixed[g]
                corner_out[HALF:, place] = value[g * 16 : (g + 1) * 16]
        corner_stores = []
        for out, heads_here in zip(outs, groups):
            columns = pl.ds((heads_here[0] - heads[0]) * width, len(heads_here) * width)
            corner_stores.append(start(corner_out.at[:, columns], out.at[pl.ds(len(items) * BLK, CORNER)]))

    def block_of(place):
        at = jnp.int32(items[-1])
        for other in range(len(items) - 1):
            at = jnp.where(place == other, jnp.int32(items[other]), at)
        return at + (first <= at).astype(jnp.int32)

    def body(skipped, taken, query_ref, out_ref):
        step = marks[count]
        marks[count] = step + 1
        block, head = (block_of(lax.div(step, taken)), lax.rem(step, taken))

        @pl.when(head == 0)
        def _():
            for back in range(TREE_MOST):
                at = (TREE_MOST - 1 - back) * BLK
                bias[:, at : at + BLK] = jnp.where(related(block, back), 0.0, NEG)

        window = pl.ds(pl.multiple_of(block * BLK, BLK), SPAN)
        at = pl.ds(pl.multiple_of((skipped + head) * HEAD, HEAD), HEAD)
        scores = product_t(stacked(query_ref[0]), kbuf[window, at])
        scores = scores.reshape(group, BLK, SPAN) + bias[...][None]
        top = jnp.max(scores, axis=-1, keepdims=True)
        weights = jnp.exp2((scores - top) * FACTOR)
        totals = jnp.sum(weights, axis=-1, keepdims=True)
        rounded = weights.astype(jnp.bfloat16).reshape(group * BLK, SPAN)
        mixed = product(rounded, vbuf[window, at])
        mixed = (mixed.reshape(group, BLK, HEAD) / totals).astype(jnp.bfloat16)
        for g in range(group):
            out_ref[:, g * HEAD : (g + 1) * HEAD] = mixed[g]

    for out, heads_here in zip(outs, groups):
        if items:
            marks[count] = 0
            pltpu.emit_pipeline(
                functools.partial(body, heads_here[0] - heads[0], len(heads_here)),
                grid=(len(items), len(heads_here)),
                in_specs=[
                    pl.BlockSpec((1, BLK, width), lambda i, h, at=heads_here[0]: (path, block_of(i), at + h))
                ],
                out_specs=[pl.BlockSpec((BLK, width), lambda i, h: (i, h))],
            )(queries, out.at[pl.ds(0, len(items) * BLK)])
    if corner:
        for copy in corner_stores:
            copy.wait()
    if pack:
        pack_store.wait()


def attend(payload, groups, items, operands, after=(), halo=None, corner=False, pack=False):
    lengths, queries, keys, values, seg, par = operands
    rows, columns = queries.shape[1:]
    width = columns // (keys.shape[2] // HEAD)
    count = rows // BLK
    heads = [head for group in groups for head in group]
    height = len(items) * BLK + (CORNER if corner else 0)
    out_shape = [jax.ShapeDtypeStruct((height, len(group) * width), jnp.bfloat16) for group in groups]
    scratch = [
        pltpu.VMEM((REACH + rows, len(heads) * HEAD), jnp.bfloat16),
        pltpu.VMEM((REACH + rows, len(heads) * HEAD), jnp.bfloat16),
        pltpu.VMEM((BLK, SPAN), jnp.float32),
        pltpu.VMEM(seg.shape, jnp.int32),
        pltpu.VMEM(par.shape, jnp.int32),
        pltpu.VMEM((1, REACH + rows), jnp.int32),
        pltpu.VMEM((1, REACH + rows), jnp.int32),
        pltpu.SMEM(lengths.shape, jnp.int32),
        pltpu.SMEM((count + 1,), jnp.int32),
        pltpu.SemaphoreType.DMA((16,)),
    ]
    if halo is not None:
        scratch.append(pltpu.VMEM((INFO, keys.shape[2]), jnp.bfloat16))
    if corner:
        scratch.append(pltpu.VMEM((BLK, len(heads) * width), jnp.bfloat16))
        scratch.append(pltpu.VMEM((CORNER, len(heads) * width), jnp.bfloat16))
    if pack:
        packed = (2, 2, REACH + INFO, keys.shape[2])
        out_shape.append(jax.ShapeDtypeStruct(packed, jnp.bfloat16))
        scratch.append(pltpu.VMEM(packed, jnp.bfloat16))
    inputs = [lengths, queries, keys, values, seg, par] + ([] if halo is None else [halo])

    def kernel(*refs):
        refs = refs[: len(inputs)] + refs[len(inputs) + len(after) :]
        attend_kernel(payload, groups, items, corner, pack, halo is not None, *refs)

    return pl.pallas_call(
        kernel,
        out_shape=out_shape,
        in_specs=[HBM] * 6 + [ANY] * (len(inputs) - 6 + len(after)),
        out_specs=[ANY] * len(out_shape),
        scratch_shapes=scratch,
        compiler_params=pltpu.CompilerParams(vmem_limit_bytes=VMEM_LIMIT),
        cost_estimate=COST,
    )(*inputs, *after)


def behind(value, *after):
    return pl.pallas_call(
        lambda *refs: None,
        out_shape=jax.ShapeDtypeStruct(value.shape, value.dtype),
        in_specs=[ANY] * (1 + len(after)),
        out_specs=ANY,
        input_output_aliases={0: 0},
        cost_estimate=COST,
    )(value, *after)


def place_kernel(pieces, aliased, *refs):
    refs = list(refs)
    sources = [[refs.pop(0)] if swap else [refs.pop(0), refs.pop(0)] for swap, _, _, _ in pieces]
    refs = refs[aliased:]
    forward, back = refs[:2]
    stages, blocks = (refs[2 : 2 + len(pieces)], refs[2 + len(pieces) : 2 + 2 * len(pieces)])
    in_sems, out_sems = refs[2 + 2 * len(pieces) :]
    width = forward.shape[1] // KV_HEADS
    group = width // HEAD
    where = lax.axis_index("pipe")
    even = lax.rem(where, 2) == 0
    edge = (where == 0) | (where == lax.axis_size("pipe") - 1)

    for at, source in enumerate(sources):
        if len(source) == 1:
            pltpu.make_async_copy(source[0], stages[at], in_sems.at[at]).start()
        else:
            for own, mine in ((edge, source[1]), (jnp.logical_not(edge), source[0])):

                @pl.when(own)
                def _():
                    pltpu.make_async_copy(mine, stages[at], in_sems.at[at]).start()

    left, right = sides()
    first = {}
    stores = []
    for at, (swap, heads, items, corner) in enumerate(pieces):
        pltpu.make_async_copy(sources[at][0], stages[at], in_sems.at[at]).wait()
        stage = stages[at]
        top = len(items) * BLK
        if corner:
            tile = stage[top : top + 16, HALF : HALF + HEAD // 2].astype(jnp.float32)
            spot = (lax.broadcasted_iota(jnp.int32, tile.shape, 0) == 0) & (lax.broadcasted_iota(jnp.int32, tile.shape, 1) == 0)
            first[swap] = jnp.sum(jnp.where(spot, tile, 0.0)).astype(jnp.int32)
        columns = pl.ds(heads[0] * width, len(heads) * width)

        def store(source, block):
            rows = pl.ds(pl.multiple_of(block * BLK, BLK), BLK)
            for to_forward, target in ((even != swap, forward), (even == swap, back)):

                @pl.when(to_forward)
                def _():
                    pltpu.make_async_copy(source, target.at[rows, columns], out_sems.at[len(stores)]).start()

            stores.append(pltpu.make_async_copy(source, forward.at[rows, columns], out_sems.at[len(stores)]))

        for item, index in enumerate(items):
            store(stage.at[pl.ds(item * BLK, BLK)], plain_block(first[swap], index))
        if corner:
            for head in range(len(heads)):
                lanes = slice(head * width, (head + 1) * width)
                tiles = stage[top + HALF : top + CORNER, lanes]
                value = stacked(tiles)
                turned = flipped(value)
                shares = stage[top : top + HALF, lanes].astype(jnp.float32)
                shares = stacked(shares).reshape(group, HALF, BLK)

                def context(side, basis):
                    kept = jnp.where(side[None], shares, 0.0)
                    rest = 1.0 - jnp.sum(kept, axis=-1, keepdims=True)
                    mixed = product(kept.astype(jnp.bfloat16).reshape(group * HALF, BLK), basis)
                    mixed = mixed.reshape(group, HALF, HEAD) + rest * basis[HALF:].astype(jnp.float32)[None]
                    mixed = mixed.astype(jnp.bfloat16)
                    return jnp.concatenate([mixed[g] for g in range(group)], axis=1)

                blocks[at][HALF:, lanes] = context(left, value)
                blocks[at][:HALF, lanes] = flipped(context(right, turned))
            store(blocks[at], first[swap])
    for copy in stores:
        copy.wait()


def place(pieces, rows, outs=()):
    arrays = [array for piece in pieces for array in piece[0]]
    width = pieces[0][0][0].shape[1] // len(pieces[0][2])
    shape = jax.ShapeDtypeStruct((rows, width * KV_HEADS), jnp.bfloat16)
    held = [piece[0][0].shape for piece in pieces]
    return pl.pallas_call(
        functools.partial(place_kernel, [piece[1:] for piece in pieces], len(outs)),
        out_shape=[shape, shape],
        in_specs=[ANY] * len(arrays) + [HBM] * len(outs),
        out_specs=[HBM, HBM],
        scratch_shapes=[pltpu.VMEM(size, jnp.bfloat16) for size in held]
        + [pltpu.VMEM((BLK, size[1]), jnp.bfloat16) for size in held]
        + [pltpu.SemaphoreType.DMA((len(pieces),)), pltpu.SemaphoreType.DMA((4 * len(pieces),))],
        input_output_aliases={len(arrays) + i: i for i in range(len(outs))},
        compiler_params=pltpu.CompilerParams(vmem_limit_bytes=24 * 1024 * 1024),
        cost_estimate=COST,
    )(*arrays, *outs)


COST = pl.CostEstimate(flops=1024, bytes_accessed=1024, transcendentals=0)

SWAP = [(0, 1), (1, 0), (2, 3), (3, 2)]
DIAGONAL = [(1, 2), (2, 1)]
ACROSS = [(1, 3), (2, 0)]
ONWARD = [(3, 2), (0, 1)]


def on_device(queries, keys, values, segment, parent, tree_lengths):
    rows = queries.shape[2]
    operands = (tree_lengths[0], queries[0], keys[0], values[0], segment[0], parent[0])
    ring = [(source, source + 1) for source in range(lax.axis_size("dp") - 1)]
    every = tuple(range(KV_HEADS))

    corner, halo = attend(0, (every,), (), operands, corner=True, pack=True)
    got_0 = lax.ppermute(corner, "pipe", SWAP)
    halo = lax.ppermute(halo, "dp", ring)
    swap_1, swap_2 = attend(0, ((0, 1), (2, 3)), (2,), operands, after=(corner,))
    got_1 = lax.ppermute(swap_1, "pipe", SWAP)
    got_2 = lax.ppermute(swap_2, "pipe", SWAP)
    (swap_3,) = attend(0, (every,), (0, 1), operands, after=(swap_1,), halo=halo)
    got_3 = lax.ppermute(swap_3, "pipe", SWAP)
    routed_1, routed_2 = attend(1, ((0,), (1,)), (0, 1, 2), operands, after=(swap_3,), halo=halo, corner=True)
    across_1 = lax.ppermute(routed_1, "pipe", ACROSS)
    across_2 = lax.ppermute(routed_2, "pipe", ACROSS)
    (direct,) = attend(
        1, ((2, 3),), (0, 1, 2), operands, after=(routed_1, got_0, got_1, got_2), halo=halo, corner=True
    )
    diagonal = lax.ppermute(direct, "pipe", DIAGONAL)
    onward_1 = lax.ppermute(behind(across_1, direct), "pipe", ONWARD)
    onward_2 = lax.ppermute(behind(across_2, direct), "pipe", ONWARD)
    outs = place(
        [
            ((got_0,), True, every, (), True),
            ((got_1,), True, (0, 1), (2,), False),
            ((got_2,), True, (2, 3), (2,), False),
            ((got_3,), True, every, (0, 1), False),
        ],
        rows,
    )
    forward, back = place(
        [
            ((onward_1, routed_1), False, (0,), (0, 1, 2), True),
            ((onward_2, routed_2), False, (1,), (0, 1, 2), True),
            ((diagonal, direct), False, (2, 3), (0, 1, 2), True),
        ],
        rows,
        outs,
    )
    return (forward[None], back[None])


def solution(mesh):
    return jax.shard_map(
        on_device,
        mesh=mesh,
        in_specs=(
            P("pipe", None, "dp", None),
            P("pipe", None, "dp", None),
            P("pipe", None, "dp", None),
            P("pipe", None, "dp"),
            P("pipe", None, "dp"),
            P("pipe", None, None),
        ),
        out_specs=(P("pipe", "dp", None), P("pipe", "dp", None)),
        check_vma=False,
    )
```

time: 496 us -> 140 us (0.28); the launches traced: 487 us -> 138 us
  local copies, waits for them, and re-layouts: 144 us -> 3.75 us
  waiting for transfers between devices: 169 us -> 59.4 us
  matrix products: 69.9 us -> 0 us
  other arithmetic: 69.8 us -> 0 us
  Pallas kernels: 0 us -> 54.6 us
  starting transfers between devices: 32.6 us -> 19.2 us
    ppermute x14 -> x10, waiting for transfers between devices: 169 us -> 59.4 us  [the longest x1 20.3 us: on_device(): onward_1 = lax.ppermute(behind(across_1, direct), 'pipe', ONWARD)]
    dot_general x8 -> x0, matrix products: 69.9 us -> none  [the longest x4 35.8 us: attend(): jnp.einsum('ahgqk,akhd->aqhgd', rounded, valueset, preferred_element_type...]
    pallas_call x0 -> x9, Pallas kernels: none -> 54.6 us  [the longest x5 46 us: attend(): pl.pallas_call(kernel, out_shape=out_shape, in_specs=[HBM] * 6 + [ANY] *...]
    slice x37 -> x0, local copies, waits for them, and re-layouts: 37.4 us -> none  [the longest x27 23.4 us: windowed(): lax.slice_in_dim(rows, (index + offset) * BLK, (index + offset) * BLK + s...]
    another operation x43 -> x0, local copies, waits for them, and re-layouts: 31.3 us -> none  [the longest x40 30.3 us: windowed(): jnp.stack([lax.slice_in_dim(rows, (index + offset) * BLK, (index + offset...]
    reduce_sum x4 -> x0, other arithmetic: 30.9 us -> none  [attend(): totals = jnp.sum(weights, axis=-1)]
    unnamed x137 -> x20, local copies, waits for them, and re-layouts: 29.3 us -> 3.75 us
    convert_element_type x4 -> x0, local copies, waits for them, and re-layouts: 22.7 us -> none  [attend(): (mixed / totals).astype(jnp.bfloat16).reshape(group_count * BLK, -1)]
  transfers between devices with their start and end apart: 14 -> 10, of which waited for: 4 -> 7; matrix products, arithmetic and copies ran while one was open for 54% -> 0% of each run, Pallas kernels for 0% -> 33%
where the time goes in v2:
time: 140 us; the launch traced here: 138 us
  waiting for transfers between devices  59.4 us (42%)
  Pallas kernels  54.6 us (39%)
  starting transfers between devices  19.2 us (14%)
  local copies, waits for them, and re-layouts  3.75 us (3%)
    pallas_call x5, Pallas kernels, attend(): pl.pallas_call(kernel, out_shape=out_shape, in_specs=[HBM] * 6 + [ANY] *...  46 us
    ppermute x1, waiting for transfers between devices, on_device(): onward_1 = lax.ppermute(behind(across_1, direct), 'pipe', ONWARD)  20.3 us
    ppermute x1, waiting for transfers between devices, on_device(): across_1 = lax.ppermute(routed_1, 'pipe', ACROSS)  16.9 us
    ppermute x1, waiting for transfers between devices, on_device(): onward_2 = lax.ppermute(behind(across_2, direct), 'pipe', ONWARD)  15.3 us
    pallas_call x2, Pallas kernels, place(): pl.pallas_call(functools.partial(place_kernel, [piece[1:] for piece in pi...  8.53 us
    unnamed x20, local copies, waits for them, and re-layouts  3.75 us
    ppermute x1, waiting for transfers between devices, on_device(): halo = lax.ppermute(halo, 'dp', ring)  3.56 us
    ppermute x1, starting transfers between devices, on_device(): across_2 = lax.ppermute(routed_2, 'pipe', ACROSS)  3.47 us
  transfers between devices with their start and end apart: 10, of which 7 were waited for; matrix products, arithmetic and copies ran while one was open for 0% of the time, Pallas kernels for 33%

profile of v2, /device:TPU:20, one launch (start us, length us, event | category | flops | bytes accessed | tf_op | source)
XLA Modules:
  0.0 137.7 jit_solution(1705424925941266988)
XLA Ops:
  0.6 5.2 %shard_map.77 = (bf16[80,4096]{1,0:T(8,128)(2,1)}, bf16[2,2,272,512]{3,2,1,0:T(8,128)(2,1)}) custom-call(s32[2,32]{1,0:T(2,128)} %bitcast.35, bf16[2,512,4096]{2,1,0:T(8,128)(2,1)} %bitcast.8, bf16[2,512,512]{2,1,0:T(8,128)(2,1)} %bitcast.13, bf16[2,512,512]{2,1,0:T(8,128)(2,1)} %bitcast.18, s32[2,512]{1,0:T(2,128)} %bitcast.25, s32[2,512]{1,0:T(2,128)} %bitcast.30), custom_call_target="tpu_custom_call" | custom-call | flops 1024 | bytes 1024 | tf_op jit(solution)/shard_map/pallas_call | solution.py:283
  5.8 1.9 %collective-permute-start = (bf16[2,2,272,512]{3,2,1,0:T(8,128)(2,1)}, bf16[2,2,272,512]{3,2,1,0:T(8,128)(2,1)S(1)}, u32[]{:S(2)}, u32[]{:S(2)}) collective-permute-start(bf16[2,2,272,512]{3,2,1,0:T(8,128)(2,1)} %get-tuple-element.12), channel_id=1, source_target_pairs={{0,1},{1,2},{2,3},{3,4},{4,5},{5,6},{6,7},{8,9},{9,10},{10,11},{11... | collective-permute-start | bytes 3342344 | tf_op jit(solution)/shard_map/ppermute | solution.py:412
  7.8 1.6 %collective-permute-start.2 = (bf16[80,4096]{1,0:T(8,128)(2,1)}, bf16[80,4096]{1,0:T(8,128)(2,1)S(1)}, u32[]{:S(2)}, u32[]{:S(2)}) collective-permute-start(bf16[80,4096]{1,0:T(8,128)(2,1)} %get-tuple-element.13.refs_6_), channel_id=1, source_target_pairs={{0,8},{8,0},{16,24},{24,16},{1,9},{9,1},{17,25},{25,17},{2,10},{10... | collective-permute-start | bytes 1966088 | tf_op jit(solution)/shard_map/ppermute | solution.py:411
  9.3 7.9 %shard_map.78 = (bf16[128,2048]{1,0:T(8,128)(2,1)}, bf16[128,2048]{1,0:T(8,128)(2,1)}) custom-call(s32[2,32]{1,0:T(2,128)} %bitcast.36, bf16[2,512,4096]{2,1,0:T(8,128)(2,1)} %bitcast.9, bf16[2,512,512]{2,1,0:T(8,128)(2,1)} %bitcast.14, bf16[2,512,512]{2,1,0:T(8,128)(2,1)} %bitcast.19, s32[2,512]{1,0:T(2,128)} %bitcast.26, s32[2,512]{1,0:T(2,128)} %bitcast.31, ...), custom_call_target="tpu_custom_call" | custom-call | flops 1024 | bytes 1024 | tf_op jit(solution)/shard_map/pallas_call | solution.py:283
  17.2 0.6 collective-permute-start.4
  17.8 1.5 %collective-permute-start.3 = (bf16[128,2048]{1,0:T(8,128)(2,1)}, bf16[128,2048]{1,0:T(8,128)(2,1)S(1)}, u32[]{:S(2)}, u32[]{:S(2)}) collective-permute-start(bf16[128,2048]{1,0:T(8,128)(2,1)} %get-tuple-element.14.refs_7_), channel_id=1, source_target_pairs={{0,8},{8,0},{16,24},{24,16},{1,9},{9,1},{17,25},{25,17},{2,10},{10... | collective-permute-start | bytes 1572872 | tf_op jit(solution)/shard_map/ppermute | solution.py:414
  19.3 3.6 %collective-permute-done.refs_6_ = bf16[2,2,272,512]{3,2,1,0:T(8,128)(2,1)S(1)} collective-permute-done((bf16[2,2,272,512]{3,2,1,0:T(8,128)(2,1)}, bf16[2,2,272,512]{3,2,1,0:T(8,128)(2,1)S(1)}, u32[]{:S(2)}, u32[]{:S(2)}) %collective-permute-start) | collective-permute-done | bytes 1114144 | tf_op jit(solution)/shard_map/ppermute | solution.py:412
  22.9 1.0 copy-done.9
  23.9 10.3 %shard_map.79.refs_7_ = bf16[256,4096]{1,0:T(8,128)(2,1)} custom-call(s32[2,32]{1,0:T(2,128)} %bitcast.37, bf16[2,512,4096]{2,1,0:T(8,128)(2,1)} %bitcast.10, bf16[2,512,512]{2,1,0:T(8,128)(2,1)} %bitcast.15, bf16[2,512,512]{2,1,0:T(8,128)(2,1)} %bitcast.20, s32[2,512]{1,0:T(2,128)} %bitcast.27, s32[2,512]{1,0:T(2,128)} %bitcast.32, ...), custom_call_target="tpu_custom_call" | custom-call | flops 1024 | bytes 1024 | tf_op jit(solution)/shard_map/pallas_call | solution.py:283
  34.1 1.6 %collective-permute-start.9 = (bf16[256,4096]{1,0:T(8,128)(2,1)}, bf16[256,4096]{1,0:T(8,128)(2,1)S(1)}, u32[]{:S(2)}, u32[]{:S(2)}) collective-permute-start(bf16[256,4096]{1,0:T(8,128)(2,1)} %shard_map.79.refs_7_), channel_id=1, source_target_pairs={{0,8},{8,0},{16,24},{24,16},{1,9},{9,1},{17,25},{25,17},{2,10},{10... | collective-permute-start | bytes 6291464 | tf_op jit(solution)/shard_map/ppermute | solution.py:417
  35.7 11.9 %shard_map.80 = (bf16[464,1024]{1,0:T(8,128)(2,1)}, bf16[464,1024]{1,0:T(8,128)(2,1)}) custom-call(s32[2,32]{1,0:T(2,128)} %bitcast.38, bf16[2,512,4096]{2,1,0:T(8,128)(2,1)} %bitcast.11, bf16[2,512,512]{2,1,0:T(8,128)(2,1)} %bitcast.16, bf16[2,512,512]{2,1,0:T(8,128)(2,1)} %bitcast.21, s32[2,512]{1,0:T(2,128)} %bitcast.28, s32[2,512]{1,0:T(2,128)} %bitcast.33, ...), custom_call_target="tpu_custom_call" | custom-call | flops 1024 | bytes 1024 | tf_op jit(solution)/shard_map/pallas_call | solution.py:283
  47.6 3.5 %collective-permute-start.6 = (bf16[464,1024]{1,0:T(8,128)(2,1)}, bf16[464,1024]{1,0:T(8,128)(2,1)}, u32[]{:S(2)}, u32[]{:S(2)}) collective-permute-start(bf16[464,1024]{1,0:T(8,128)(2,1)} %get-tuple-element.17.refs_3_), channel_id=1, source_target_pairs={{8,24},{16,0},{9,25},{17,1},{10,26},{18,2},{11,27},{19,3},{12,28},... | collective-permute-start | bytes 2850824 | tf_op jit(solution)/shard_map/ppermute | solution.py:420
  51.1 0.0 collective-permute-done.4.refs_10_.refs_2_
  51.1 2.2 %collective-permute-start.1 = (bf16[464,1024]{1,0:T(8,128)(2,1)}, bf16[464,1024]{1,0:T(8,128)(2,1)}, u32[]{:S(2)}, u32[]{:S(2)}) collective-permute-start(bf16[464,1024]{1,0:T(8,128)(2,1)} %get-tuple-element.15.refs_7_.refs_1_), channel_id=1, source_target_pairs={{8,24},{16,0},{9,25},{17,1},{10,26},{18,2},{11,27},{19,3},{12,28},... | collective-permute-start | bytes 2850824 | tf_op jit(solution)/shard_map/ppermute | solution.py:419
  53.3 0.0 collective-permute-done.3.refs_9_.refs_1_
  53.3 0.0 collective-permute-done.2.refs_8_.refs_0_
  53.3 0.0 copy-done.4
  53.3 0.8 copy-done.6
  54.1 0.9 copy-done.2
  55.0 10.8 %shard_map.81.refs_1_.refs_5_ = bf16[464,2048]{1,0:T(8,128)(2,1)} custom-call(s32[2,32]{1,0:T(2,128)} %bitcast.39, bf16[2,512,4096]{2,1,0:T(8,128)(2,1)} %bitcast.12, bf16[2,512,512]{2,1,0:T(8,128)(2,1)} %bitcast.17, bf16[2,512,512]{2,1,0:T(8,128)(2,1)} %bitcast.22, s32[2,512]{1,0:T(2,128)} %bitcast.29, s32[2,512]{1,0:T(2,128)} %bitcast.34, ...), custom_call_target="tpu_custom_call" | custom-call | flops 1024 | bytes 1024 | tf_op jit(solution)/shard_map/pallas_call | solution.py:283
  65.8 3.4 %collective-permute-start.8 = (bf16[464,2048]{1,0:T(8,128)(2,1)}, bf16[464,2048]{1,0:T(8,128)(2,1)}, u32[]{:S(2)}, u32[]{:S(2)}) collective-permute-start(bf16[464,2048]{1,0:T(8,128)(2,1)} %shard_map.81.refs_1_.refs_5_), channel_id=1, source_target_pairs={{8,16},{16,8},{9,17},{17,9},{10,18},{18,10},{11,19},{19,11},{12,20... | collective-permute-start | bytes 5701640 | tf_op jit(solution)/shard_map/ppermute | solution.py:424
  69.2 2.7 %collective-permute-done.6.refs_0_ = bf16[464,1024]{1,0:T(8,128)(2,1)} collective-permute-done((bf16[464,1024]{1,0:T(8,128)(2,1)}, bf16[464,1024]{1,0:T(8,128)(2,1)}, u32[]{:S(2)}, u32[]{:S(2)}) %collective-permute-start.6) | collective-permute-done | bytes 950304 | tf_op jit(solution)/shard_map/ppermute | solution.py:420
  71.9 1.4 %collective-permute-start.7 = (bf16[464,1024]{1,0:T(8,128)(2,1)}, bf16[464,1024]{1,0:T(8,128)(2,1)}, u32[]{:S(2)}, u32[]{:S(2)}) collective-permute-start(bf16[464,1024]{1,0:T(8,128)(2,1)} %shard_map.83), channel_id=1, source_target_pairs={{24,16},{0,8},{25,17},{1,9},{26,18},{2,10},{27,19},{3,11},{28,20},... | collective-permute-start | bytes 2850824 | tf_op jit(solution)/shard_map/ppermute | solution.py:426
  73.3 16.9 %collective-permute-done.1.refs_0_ = bf16[464,1024]{1,0:T(8,128)(2,1)} collective-permute-done((bf16[464,1024]{1,0:T(8,128)(2,1)}, bf16[464,1024]{1,0:T(8,128)(2,1)}, u32[]{:S(2)}, u32[]{:S(2)}) %collective-permute-start.1) | collective-permute-done | bytes 950304 | tf_op jit(solution)/shard_map/ppermute | solution.py:419
  90.2 1.5 %collective-permute-start.5 = (bf16[464,1024]{1,0:T(8,128)(2,1)}, bf16[464,1024]{1,0:T(8,128)(2,1)S(1)}, u32[]{:S(2)}, u32[]{:S(2)}) collective-permute-start(bf16[464,1024]{1,0:T(8,128)(2,1)} %shard_map.82), channel_id=1, source_target_pairs={{24,16},{0,8},{25,17},{1,9},{26,18},{2,10},{27,19},{3,11},{28,20},... | collective-permute-start | bytes 2850824 | tf_op jit(solution)/shard_map/ppermute | solution.py:425
  91.8 0.6 collective-permute-done.9.refs_3_
  92.4 1.0 copy-done.7
  93.5 4.1 %shard_map.84 = (bf16[512,4096]{1,0:T(8,128)(2,1)}, bf16[512,4096]{1,0:T(8,128)(2,1)}) custom-call(bf16[80,4096]{1,0:T(8,128)(2,1)S(1)} %copy-done.3, bf16[128,2048]{1,0:T(8,128)(2,1)S(1)} %copy-done.7, bf16[128,2048]{1,0:T(8,128)(2,1)S(1)} %copy-done.5, bf16[256,4096]{1,0:T(8,128)(2,1)S(1)} %collective-permute-done.9.refs_3_), custom_call_target="tpu_custom_call" | custom-call | flops 1024 | bytes 1024 | tf_op jit(solution)/shard_map/pallas_call | solution.py:382
  97.5 15.3 %collective-permute-done.7.refs_2_ = bf16[464,1024]{1,0:T(8,128)(2,1)} collective-permute-done((bf16[464,1024]{1,0:T(8,128)(2,1)}, bf16[464,1024]{1,0:T(8,128)(2,1)}, u32[]{:S(2)}, u32[]{:S(2)}) %collective-permute-start.7) | collective-permute-done | bytes 950304 | tf_op jit(solution)/shard_map/ppermute | solution.py:426
  112.9 20.3 %collective-permute-done.5.refs_0_ = bf16[464,1024]{1,0:T(8,128)(2,1)S(1)} collective-permute-done((bf16[464,1024]{1,0:T(8,128)(2,1)}, bf16[464,1024]{1,0:T(8,128)(2,1)S(1)}, u32[]{:S(2)}, u32[]{:S(2)}) %collective-permute-start.5) | collective-permute-done | bytes 950304 | tf_op jit(solution)/shard_map/ppermute | solution.py:425
  133.1 0.1 collective-permute-done.8.refs_4_
  133.2 4.5 %shard_map.85 = (bf16[512,4096]{1,0:T(8,128)(2,1)}, bf16[512,4096]{1,0:T(8,128)(2,1)}) custom-call(bf16[464,1024]{1,0:T(8,128)(2,1)S(1)} %collective-permute-done.5.refs_0_, bf16[464,1024]{1,0:T(8,128)(2,1)S(1)} %copy-done.1, bf16[464,1024]{1,0:T(8,128)(2,1)} %collective-permute-done.7.refs_2_, ...), custom_call_target="tpu_custom_call", output_to_operand_aliasing={{0}: (6, {}), {1}: (7, {})} | custom-call | flops 1024 | bytes 1024 | tf_op jit(solution)/shard_map/pallas_call | solution.py:382
  (17 shorter events, 0.0 us)
Async XLA Ops:
  5.8 17.0 %collective-permute-start = (bf16[2,2,272,512]{3,2,1,0:T(8,128)(2,1)}, bf16[2,2,272,512]{3,2,1,0:T(8,128)(2,1)S(1)}, u32[]{:S(2)}, u32[]{:S(2)}) collective-permute-start(bf16[2,2,272,512]{3,2,1,0:T(8,128)(2,1)} %get-tuple-element.12), channel_id=1, source_target_pairs={{0,1},{1,2},{2,3},{3,4},{4,5},{5,6},{6,7},{8,9},{9,10},{10,11},{11... | collective-permute-start | bytes 3342344 | tf_op jit(solution)/shard_map/ppermute | solution.py:412
  7.8 45.5 %collective-permute-start.2 = (bf16[80,4096]{1,0:T(8,128)(2,1)}, bf16[80,4096]{1,0:T(8,128)(2,1)S(1)}, u32[]{:S(2)}, u32[]{:S(2)}) collective-permute-start(bf16[80,4096]{1,0:T(8,128)(2,1)} %get-tuple-element.13.refs_6_), channel_id=1, source_target_pairs={{0,8},{8,0},{16,24},{24,16},{1,9},{9,1},{17,25},{25,17},{2,10},{10... | collective-permute-start | bytes 1966088 | tf_op jit(solution)/shard_map/ppermute | solution.py:411
  17.2 33.9 %collective-permute-start.4 = (bf16[128,2048]{1,0:T(8,128)(2,1)}, bf16[128,2048]{1,0:T(8,128)(2,1)S(1)}, u32[]{:S(2)}, u32[]{:S(2)}) collective-permute-start(bf16[128,2048]{1,0:T(8,128)(2,1)} %get-tuple-element.16), channel_id=1, source_target_pairs={{0,8},{8,0},{16,24},{24,16},{1,9},{9,1},{17,25},{25,17},{2,10},{10... | collective-permute-start | bytes 1572872 | tf_op jit(solution)/shard_map/ppermute | solution.py:415
  17.8 35.5 %collective-permute-start.3 = (bf16[128,2048]{1,0:T(8,128)(2,1)}, bf16[128,2048]{1,0:T(8,128)(2,1)S(1)}, u32[]{:S(2)}, u32[]{:S(2)}) collective-permute-start(bf16[128,2048]{1,0:T(8,128)(2,1)} %get-tuple-element.14.refs_7_), channel_id=1, source_target_pairs={{0,8},{8,0},{16,24},{24,16},{1,9},{9,1},{17,25},{25,17},{2,10},{10... | collective-permute-start | bytes 1572872 | tf_op jit(solution)/shard_map/ppermute | solution.py:414
  22.9 1.0 copy-start.9
  34.1 58.3 %collective-permute-start.9 = (bf16[256,4096]{1,0:T(8,128)(2,1)}, bf16[256,4096]{1,0:T(8,128)(2,1)S(1)}, u32[]{:S(2)}, u32[]{:S(2)}) collective-permute-start(bf16[256,4096]{1,0:T(8,128)(2,1)} %shard_map.79.refs_7_), channel_id=1, source_target_pairs={{0,8},{8,0},{16,24},{24,16},{1,9},{9,1},{17,25},{25,17},{2,10},{10... | collective-permute-start | bytes 6291464 | tf_op jit(solution)/shard_map/ppermute | solution.py:417
  47.6 24.2 %collective-permute-start.6 = (bf16[464,1024]{1,0:T(8,128)(2,1)}, bf16[464,1024]{1,0:T(8,128)(2,1)}, u32[]{:S(2)}, u32[]{:S(2)}) collective-permute-start(bf16[464,1024]{1,0:T(8,128)(2,1)} %get-tuple-element.17.refs_3_), channel_id=1, source_target_pairs={{8,24},{16,0},{9,25},{17,1},{10,26},{18,2},{11,27},{19,3},{12,28},... | collective-permute-start | bytes 2850824 | tf_op jit(solution)/shard_map/ppermute | solution.py:420
  51.1 2.2 %copy-start.4 = (bf16[128,2048]{1,0:T(8,128)(2,1)}, bf16[128,2048]{1,0:T(8,128)(2,1)S(1)}, u32[]{:S(2)}) copy-start(bf16[128,2048]{1,0:T(8,128)(2,1)S(1)} %collective-permute-done.4.refs_10_.refs_2_) | copy-start | bytes 1572868
  51.1 39.1 %collective-permute-start.1 = (bf16[464,1024]{1,0:T(8,128)(2,1)}, bf16[464,1024]{1,0:T(8,128)(2,1)}, u32[]{:S(2)}, u32[]{:S(2)}) collective-permute-start(bf16[464,1024]{1,0:T(8,128)(2,1)} %get-tuple-element.15.refs_7_.refs_1_), channel_id=1, source_target_pairs={{8,24},{16,0},{9,25},{17,1},{10,26},{18,2},{11,27},{19,3},{12,28},... | collective-permute-start | bytes 2850824 | tf_op jit(solution)/shard_map/ppermute | solution.py:419
  53.3 0.8 copy-start.6
  54.1 0.9 copy-start.2
  65.8 67.4 %collective-permute-start.8 = (bf16[464,2048]{1,0:T(8,128)(2,1)}, bf16[464,2048]{1,0:T(8,128)(2,1)}, u32[]{:S(2)}, u32[]{:S(2)}) collective-permute-start(bf16[464,2048]{1,0:T(8,128)(2,1)} %shard_map.81.refs_1_.refs_5_), channel_id=1, source_target_pairs={{8,16},{16,8},{9,17},{17,9},{10,18},{18,10},{11,19},{19,11},{12,20... | collective-permute-start | bytes 5701640 | tf_op jit(solution)/shard_map/ppermute | solution.py:424
  71.9 20.6 %copy-start.3 = (bf16[80,4096]{1,0:T(8,128)(2,1)S(1)}, bf16[80,4096]{1,0:T(8,128)(2,1)}, u32[]{:S(2)}) copy-start(bf16[80,4096]{1,0:T(8,128)(2,1)} %copy-done.2) | copy-start | bytes 1966084
  71.9 20.6 %copy-start.5 = (bf16[128,2048]{1,0:T(8,128)(2,1)S(1)}, bf16[128,2048]{1,0:T(8,128)(2,1)}, u32[]{:S(2)}) copy-start(bf16[128,2048]{1,0:T(8,128)(2,1)} %copy-done.4) | copy-start | bytes 1572868
  71.9 41.0 %collective-permute-start.7 = (bf16[464,1024]{1,0:T(8,128)(2,1)}, bf16[464,1024]{1,0:T(8,128)(2,1)}, u32[]{:S(2)}, u32[]{:S(2)}) collective-permute-start(bf16[464,1024]{1,0:T(8,128)(2,1)} %shard_map.83), channel_id=1, source_target_pairs={{24,16},{0,8},{25,17},{1,9},{26,18},{2,10},{27,19},{3,11},{28,20},... | collective-permute-start | bytes 2850824 | tf_op jit(solution)/shard_map/ppermute | solution.py:426
  90.2 43.0 %copy-start = (bf16[464,2048]{1,0:T(8,128)(2,1)S(1)}, bf16[464,2048]{1,0:T(8,128)(2,1)}, u32[]{:S(2)}) copy-start(bf16[464,2048]{1,0:T(8,128)(2,1)} %shard_map.81.refs_1_.refs_5_) | copy-start | bytes 5701636
  90.2 43.0 %copy-start.1 = (bf16[464,1024]{1,0:T(8,128)(2,1)S(1)}, bf16[464,1024]{1,0:T(8,128)(2,1)}, u32[]{:S(2)}) copy-start(bf16[464,1024]{1,0:T(8,128)(2,1)} %get-tuple-element.15.refs_7_.refs_1_) | copy-start | bytes 2850820
  90.2 42.9 %collective-permute-start.5 = (bf16[464,1024]{1,0:T(8,128)(2,1)}, bf16[464,1024]{1,0:T(8,128)(2,1)S(1)}, u32[]{:S(2)}, u32[]{:S(2)}) collective-permute-start(bf16[464,1024]{1,0:T(8,128)(2,1)} %shard_map.82), channel_id=1, source_target_pairs={{24,16},{0,8},{25,17},{1,9},{26,18},{2,10},{27,19},{3,11},{28,20},... | collective-permute-start | bytes 2850824 | tf_op jit(solution)/shard_map/ppermute | solution.py:425
  92.4 1.0 copy-start.7
  93.5 39.7 %copy-start.8 = (bf16[464,1024]{1,0:T(8,128)(2,1)S(1)}, bf16[464,1024]{1,0:T(8,128)(2,1)}, u32[]{:S(2)}) copy-start(bf16[464,1024]{1,0:T(8,128)(2,1)} %get-tuple-element.17.refs_3_) | copy-start | bytes 2850820

commit v3 on v2

--- a/solution.py
+++ b/solution.py
@@ -63,7 +63,7 @@
     refs = refs[6:]
     halo_in = refs.pop(0) if halo else None
     outs = [refs.pop(0) for _ in groups]
-    pack_out = refs.pop(0) if pack else None
+    pack_outs = [refs.pop(0), refs.pop(0)] if pack else None
     kbuf, vbuf, bias, segs, pars, seg, par, lengths, marks, sems = refs[:10]
     refs = refs[10:]
     if halo:
@@ -98,15 +98,15 @@
     for which, (source, target) in enumerate(((keys, kbuf), (values, vbuf))):
         kv_copies.append(start(source.at[path, :, lanes], target.at[pl.ds(REACH, rows)]))
         if halo:
-            kv_copies.append(start(halo_in.at[which, path, pl.ds(0, REACH), lanes], target.at[pl.ds(0, REACH)]))
+            kv_copies.append(start(halo_in.at[which, pl.ds(0, REACH), lanes], target.at[pl.ds(0, REACH)]))
     if halo:
-        row_copies.append(start(halo_in.at[0, path, pl.ds(REACH, INFO)], info))
+        row_copies.append(start(halo_in.at[0, pl.ds(REACH, INFO)], info))
     pack_copies = []
     if pack:
         for each in range(2):
             for which, source in enumerate((keys, values)):
                 source = source.at[each, pl.ds(rows - REACH, REACH)]
-                pack_copies.append(start(source, packed.at[which, each, pl.ds(0, REACH)]))
+                pack_copies.append(start(source, packed.at[each, which, pl.ds(0, REACH)]))
 
     lengths_copy.wait()
 
@@ -116,23 +116,30 @@
         return (end, tuple(jnp.where(end <= first_block + at, end, begin) for at, begin in enumerate(begins)))
 
     zero = jnp.int32(0)
-    _, begins = lax.fori_loop(0, lengths.shape[1], step, (zero, (zero,) * count))
-    first = jnp.int32(count - 1)
+    _, begins = lax.fori_loop(0, lengths.shape[1], step, (zero, (zero,) * count), unroll=8)
+    first = jnp.int32(TREE_MOST - 1)
     for at in reversed(range(count)):
         marks[at] = begins[at]
-        first = jnp.where(begins[at] == first_block + at, at, first)
+        if at < TREE_MOST - 1:
+            first = jnp.where(begins[at] == first_block + at, at, first)
     if corner:
         columns = pl.ds(heads[0] * width, taken * width)
         query_copy = start(queries.at[path, pl.ds(pl.multiple_of(first * BLK, BLK), BLK), columns], corner_q)
 
-    for copy in row_copies:
-        copy.wait()
-    for source, target in ((segs, seg), (pars, par)):
-        target[:, REACH:] = jnp.where(path == 0, source[0:1], source[1:2])
-    if halo:
-        numbers = info[...].astype(jnp.float32)
-        seg[:, :REACH] = (numbers[0:1, :REACH] * 128.0 + numbers[1:2, :REACH]).astype(jnp.int32)
-        par[:, :REACH] = (numbers[2:3, :REACH] * 128.0 + numbers[3:4, :REACH]).astype(jnp.int32)
+    def rows_ready():
+        for copy in row_copies:
+            copy.wait()
+        for source, target in ((segs, seg), (pars, par)):
+            target[:, REACH:] = jnp.where(path == 0, source[0:1], source[1:2])
+        if halo:
+            numbers = info[...].astype(jnp.float32)
+            seg[:, :REACH] = (numbers[0:1, :REACH] * 128.0 + numbers[1:2, :REACH]).astype(jnp.int32)
+            par[:, :REACH] = (numbers[2:3, :REACH] * 128.0 + numbers[3:4, :REACH]).astype(jnp.int32)
+        for copy in kv_copies:
+            copy.wait()
+
+    if corner:
+        rows_ready()
     if pack:
         for each in range(2):
             at = lax.broadcasted_iota(jnp.int32, (INFO, REACH), 0)
@@ -142,14 +149,12 @@
                 numbers = jnp.where(at == 2 * which, row >> 7, numbers)
                 numbers = jnp.where(at == 2 * which + 1, row & 127, numbers)
             numbers = numbers.astype(jnp.float32).astype(jnp.bfloat16)
-            packed[0, each, REACH:, :REACH] = numbers
-            packed[0, each, REACH:, REACH:] = jnp.zeros((INFO, keys.shape[2] - REACH), jnp.bfloat16)
-            packed[1, each, REACH:, :] = jnp.zeros((INFO, keys.shape[2]), jnp.bfloat16)
+            packed[each, 0, REACH:, :REACH] = numbers
+            packed[each, 0, REACH:, REACH:] = jnp.zeros((INFO, keys.shape[2] - REACH), jnp.bfloat16)
+            packed[each, 1, REACH:, :] = jnp.zeros((INFO, keys.shape[2]), jnp.bfloat16)
         for copy in pack_copies:
             copy.wait()
-        pack_store = start(packed, pack_out)
-    for copy in kv_copies:
-        copy.wait()
+        pack_stores = [start(packed.at[path], pack_outs[0]), start(packed.at[1 - path], pack_outs[1])]
 
     def column(row):
         return jnp.transpose(jnp.broadcast_to(row, (BLK, BLK)))
@@ -201,12 +206,17 @@
         at = jnp.int32(items[-1])
         for other in range(len(items) - 1):
             at = jnp.where(place == other, jnp.int32(items[other]), at)
+        if min(items) >= TREE_MOST - 1:
+            return at + 1
         return at + (first <= at).astype(jnp.int32)
 
     def body(skipped, taken, query_ref, out_ref):
         step = marks[count]
         marks[count] = step + 1
         block, head = (block_of(lax.div(step, taken)), lax.rem(step, taken))
+
+        if not corner:
+            pl.when(step == 0)(rows_ready)
 
         @pl.when(head == 0)
         def _():
@@ -242,7 +252,8 @@
         for copy in corner_stores:
             copy.wait()
     if pack:
-        pack_store.wait()
+        for copy in pack_stores:
+            copy.wait()
 
 
 def attend(payload, groups, items, operands, after=(), halo=None, corner=False, pack=False):
@@ -272,7 +283,7 @@
         scratch.append(pltpu.VMEM((CORNER, len(heads) * width), jnp.bfloat16))
     if pack:
         packed = (2, 2, REACH + INFO, keys.shape[2])
-        out_shape.append(jax.ShapeDtypeStruct(packed, jnp.bfloat16))
+        out_shape += [jax.ShapeDtypeStruct(packed[1:], jnp.bfloat16)] * 2
         scratch.append(pltpu.VMEM(packed, jnp.bfloat16))
     inputs = [lengths, queries, keys, values, seg, par] + ([] if halo is None else [halo])
 
@@ -407,37 +418,47 @@
     ring = [(source, source + 1) for source in range(lax.axis_size("dp") - 1)]
     every = tuple(range(KV_HEADS))
 
-    corner, halo = attend(0, (every,), (), operands, corner=True, pack=True)
-    got_0 = lax.ppermute(corner, "pipe", SWAP)
+    (swap_0,) = attend(0, ((0,),), (2,), operands)
+    got_0 = lax.ppermute(swap_0, "pipe", SWAP)
+    (swap_1,) = attend(0, ((1, 2, 3),), (2,), operands, after=(swap_0,))
+    got_1 = lax.ppermute(swap_1, "pipe", SWAP)
+    corner, halo, far_halo = attend(0, (every,), (), operands, after=(swap_1, got_0), corner=True, pack=True)
+    got_corner = lax.ppermute(corner, "pipe", SWAP)
     halo = lax.ppermute(halo, "dp", ring)
-    swap_1, swap_2 = attend(0, ((0, 1), (2, 3)), (2,), operands, after=(corner,))
-    got_1 = lax.ppermute(swap_1, "pipe", SWAP)
+    far_halo = lax.ppermute(far_halo, "dp", ring)
+    (swap_2,) = attend(0, (every,), (0, 1), operands, after=(corner,), halo=halo)
     got_2 = lax.ppermute(swap_2, "pipe", SWAP)
-    (swap_3,) = attend(0, (every,), (0, 1), operands, after=(swap_1,), halo=halo)
-    got_3 = lax.ppermute(swap_3, "pipe", SWAP)
-    routed_1, routed_2 = attend(1, ((0,), (1,)), (0, 1, 2), operands, after=(swap_3,), halo=halo, corner=True)
+    routed_1, routed_2 = attend(1, ((0,), (1,)), (0, 1, 2), operands, after=(swap_2,), halo=far_halo, corner=True)
     across_1 = lax.ppermute(routed_1, "pipe", ACROSS)
-    across_2 = lax.ppermute(routed_2, "pipe", ACROSS)
-    (direct,) = attend(
-        1, ((2, 3),), (0, 1, 2), operands, after=(routed_1, got_0, got_1, got_2), halo=halo, corner=True
+    direct_1, direct_2 = attend(
+        1, ((2,), (3,)), (0, 1, 2), operands, after=(routed_1, got_1, got_corner), halo=far_halo, corner=True
     )
-    diagonal = lax.ppermute(direct, "pipe", DIAGONAL)
-    onward_1 = lax.ppermute(behind(across_1, direct), "pipe", ONWARD)
-    onward_2 = lax.ppermute(behind(across_2, direct), "pipe", ONWARD)
+    diagonal_1 = lax.ppermute(direct_1, "pipe", DIAGONAL)
+    across_2 = lax.ppermute(behind(routed_2, direct_1), "pipe", ACROSS)
+    diagonal_2 = lax.ppermute(behind(direct_2, across_2), "pipe", DIAGONAL)
+    onward_1 = lax.ppermute(behind(across_1, direct_1), "pipe", ONWARD)
+    onward_2 = lax.ppermute(behind(across_2, direct_1), "pipe", ONWARD)
     outs = place(
         [
-            ((got_0,), True, every, (), True),
-            ((got_1,), True, (0, 1), (2,), False),
-            ((got_2,), True, (2, 3), (2,), False),
-            ((got_3,), True, every, (0, 1), False),
+            ((got_corner,), True, every, (), True),
+            ((got_0,), True, (0,), (2,), False),
+            ((got_1,), True, (1, 2, 3), (2,), False),
+            ((got_2,), True, every, (0, 1), False),
         ],
         rows,
     )
+    outs = place(
+        [
+            ((onward_1, routed_1), False, (0,), (0, 1, 2), True),
+            ((diagonal_1, direct_1), False, (2,), (0, 1, 2), True),
+        ],
+        rows,
+        outs,
+    )
     forward, back = place(
         [
-            ((onward_1, routed_1), False, (0,), (0, 1, 2), True),
             ((onward_2, routed_2), False, (1,), (0, 1, 2), True),
-            ((diagonal, direct), False, (2, 3), (0, 1, 2), True),
+            ((diagonal_2, direct_2), False, (3,), (0, 1, 2), True),
         ],
         rows,
         outs,

time: 140 us -> 134 us (0.957)
  waiting for transfers between devices: 59.4 us -> 39.5 us
  local copies, waits for them, and re-layouts: 3.75 us -> 10.4 us
  starting transfers between devices: 19.2 us -> 24.9 us
  Pallas kernels: 54.6 us -> 56.9 us
    ppermute x1, waiting for transfers between devices: 16.9 us -> 0.01 us  [on_device(): across_1 = lax.ppermute(routed_1, 'pipe', ACROSS)]
    unnamed x20 -> x28, local copies, waits for them, and re-layouts: 3.75 us -> 10.4 us
    ppermute x6 -> x8, starting transfers between devices: 12.9 us -> 18.4 us  [the longest x1 3.58 us: on_device(): diagonal_2 = lax.ppermute(behind(direct_2, across_2), 'pipe', DIAGONAL)]
    ppermute x6 -> x8, waiting for transfers between devices: 38.9 us -> 35.2 us  [the longest x1 15.6 us: on_device(): onward_2 = lax.ppermute(behind(across_2, direct_1), 'pipe', ONWARD)]
    pallas_call x5 -> x6, Pallas kernels: 46 us -> 47.3 us  [attend(): pl.pallas_call(kernel, out_shape=out_shape, in_specs=[HBM] * 6 + [ANY] *...]
    pallas_call x2 -> x3, Pallas kernels: 8.53 us -> 9.57 us  [place(): pl.pallas_call(functools.partial(place_kernel, [piece[1:] for piece in pi...]
  transfers between devices with their start and end apart: 10 -> 12, of which waited for: 7 -> 6; matrix products, arithmetic and copies ran while one was open for 0% -> 3% of each run, Pallas kernels for 33% -> 38%
where the time goes in v3:
time: 134 us; the launch traced here: 133 us
  Pallas kernels  56.9 us (42%)
  waiting for transfers between devices  39.5 us (29%)
  starting transfers between devices  24.9 us (19%)
  local copies, waits for them, and re-layouts  10.4 us (8%)
    pallas_call x6, Pallas kernels, attend(): pl.pallas_call(kernel, out_shape=out_shape, in_specs=[HBM] * 6 + [ANY] *...  47.3 us
    ppermute x1, waiting for transfers between devices, on_device(): onward_2 = lax.ppermute(behind(across_2, direct_1), 'pipe', ONWARD)  15.6 us
    ppermute x1, waiting for transfers between devices, on_device(): across_2 = lax.ppermute(behind(routed_2, direct_1), 'pipe', ACROSS)  14.1 us
    unnamed x28, local copies, waits for them, and re-layouts  10.4 us
    pallas_call x3, Pallas kernels, place(): pl.pallas_call(functools.partial(place_kernel, [piece[1:] for piece in pi...  9.57 us
    ppermute x1, waiting for transfers between devices, on_device(): diagonal_1 = lax.ppermute(direct_1, 'pipe', DIAGONAL)  4.7 us
    ppermute x1, waiting for transfers between devices, on_device(): halo = lax.ppermute(halo, 'dp', ring)  4.27 us
    ppermute x1, starting transfers between devices, on_device(): diagonal_2 = lax.ppermute(behind(direct_2, across_2), 'pipe', DIAGONAL)  3.58 us
  transfers between devices with their start and end apart: 12, of which 6 were waited for; matrix products, arithmetic and copies ran while one was open for 3% of the time, Pallas kernels for 38%

profile of v3, /device:TPU:20, one launch (start us, length us, event | category | flops | bytes accessed | tf_op | source)
XLA Modules:
  0.0 132.6 jit_solution(4495665621084348193)
XLA Ops:
  0.6 3.5 %shard_map.77.refs_6_ = bf16[128,1024]{1,0:T(8,128)(2,1)} custom-call(s32[2,32]{1,0:T(2,128)} %bitcast.40, bf16[2,512,4096]{2,1,0:T(8,128)(2,1)} %bitcast.8, bf16[2,512,512]{2,1,0:T(8,128)(2,1)} %bitcast.14, bf16[2,512,512]{2,1,0:T(8,128)(2,1)} %bitcast.20, s32[2,512]{1,0:T(2,128)} %bitcast.28, s32[2,512]{1,0:T(2,128)} %bitcast.34), custom_call_target="tpu_custom_call" | custom-call | flops 1024 | bytes 1024 | tf_op jit(solution)/shard_map/pallas_call | solution.py:294
  4.1 1.6 %collective-permute-start = (bf16[128,1024]{1,0:T(8,128)(2,1)}, bf16[128,1024]{1,0:T(8,128)(2,1)S(1)}, u32[]{:S(2)}, u32[]{:S(2)}) collective-permute-start(bf16[128,1024]{1,0:T(8,128)(2,1)} %shard_map.77.refs_6_), channel_id=1, source_target_pairs={{0,8},{8,0},{16,24},{24,16},{1,9},{9,1},{17,25},{25,17},{2,10},{10... | collective-permute-start | bytes 786440 | tf_op jit(solution)/shard_map/ppermute | solution.py:422
  5.6 5.4 %shard_map.78.refs_6_ = bf16[128,3072]{1,0:T(8,128)(2,1)} custom-call(s32[2,32]{1,0:T(2,128)} %bitcast.41, bf16[2,512,4096]{2,1,0:T(8,128)(2,1)} %bitcast.9, bf16[2,512,512]{2,1,0:T(8,128)(2,1)} %bitcast.15, bf16[2,512,512]{2,1,0:T(8,128)(2,1)} %bitcast.21, s32[2,512]{1,0:T(2,128)} %bitcast.29, s32[2,512]{1,0:T(2,128)} %bitcast.35, ...), custom_call_target="tpu_custom_call" | custom-call | flops 1024 | bytes 1024 | tf_op jit(solution)/shard_map/pallas_call | solution.py:294
  13.1 5.1 %shard_map.79 = (bf16[80,4096]{1,0:T(8,128)(2,1)}, bf16[2,272,512]{2,1,0:T(8,128)(2,1)}, bf16[2,272,512]{2,1,0:T(8,128)(2,1)}) custom-call(s32[2,32]{1,0:T(2,128)} %bitcast.42, bf16[2,512,4096]{2,1,0:T(8,128)(2,1)} %bitcast.10, bf16[2,512,512]{2,1,0:T(8,128)(2,1)} %bitcast.16, bf16[2,512,512]{2,1,0:T(8,128)(2,1)} %bitcast.22, s32[2,512]{1,0:T(2,128)} %bitcast.30, ...), custom_call_target="tpu_custom_call" | custom-call | flops 1024 | bytes 1024 | tf_op jit(solution)/shard_map/pallas_call | solution.py:294
  18.2 1.9 %collective-permute-start.2 = (bf16[2,272,512]{2,1,0:T(8,128)(2,1)}, bf16[2,272,512]{2,1,0:T(8,128)(2,1)S(1)}, u32[]{:S(2)}, u32[]{:S(2)}) collective-permute-start(bf16[2,272,512]{2,1,0:T(8,128)(2,1)} %get-tuple-element.16), channel_id=1, source_target_pairs={{0,1},{1,2},{2,3},{3,4},{4,5},{5,6},{6,7},{8,9},{9,10},{10,11},{11... | collective-permute-start | bytes 1671176 | tf_op jit(solution)/shard_map/ppermute | solution.py:427
  20.1 1.6 %collective-permute-start.4 = (bf16[80,4096]{1,0:T(8,128)(2,1)}, bf16[80,4096]{1,0:T(8,128)(2,1)S(1)}, u32[]{:S(2)}, u32[]{:S(2)}) collective-permute-start(bf16[80,4096]{1,0:T(8,128)(2,1)} %get-tuple-element.17.refs_7_), channel_id=1, source_target_pairs={{0,8},{8,0},{16,24},{24,16},{1,9},{9,1},{17,25},{25,17},{2,10},{10... | collective-permute-start | bytes 1966088 | tf_op jit(solution)/shard_map/ppermute | solution.py:426
  21.7 3.3 %collective-permute-start.1 = (bf16[2,272,512]{2,1,0:T(8,128)(2,1)}, bf16[2,272,512]{2,1,0:T(8,128)(2,1)S(1)}, u32[]{:S(2)}, u32[]{:S(2)}) collective-permute-start(bf16[2,272,512]{2,1,0:T(8,128)(2,1)} %get-tuple-element.15), channel_id=1, source_target_pairs={{0,1},{1,2},{2,3},{3,4},{4,5},{5,6},{6,7},{8,9},{9,10},{10,11},{11... | collective-permute-start | bytes 1671176 | tf_op jit(solution)/shard_map/ppermute | solution.py:428
  25.0 4.3 %collective-permute-done.2.refs_6_ = bf16[2,272,512]{2,1,0:T(8,128)(2,1)S(1)} collective-permute-done((bf16[2,272,512]{2,1,0:T(8,128)(2,1)}, bf16[2,272,512]{2,1,0:T(8,128)(2,1)S(1)}, u32[]{:S(2)}, u32[]{:S(2)}) %collective-permute-start.2) | collective-permute-done | bytes 557088 | tf_op jit(solution)/shard_map/ppermute | solution.py:427
  29.2 0.8 copy-done.12
  30.1 9.9 %shard_map.80.refs_7_ = bf16[256,4096]{1,0:T(8,128)(2,1)} custom-call(s32[2,32]{1,0:T(2,128)} %bitcast.43, bf16[2,512,4096]{2,1,0:T(8,128)(2,1)} %bitcast.11, bf16[2,512,512]{2,1,0:T(8,128)(2,1)} %bitcast.17, bf16[2,512,512]{2,1,0:T(8,128)(2,1)} %bitcast.23, s32[2,512]{1,0:T(2,128)} %bitcast.31, s32[2,512]{1,0:T(2,128)} %bitcast.37, ...), custom_call_target="tpu_custom_call" | custom-call | flops 1024 | bytes 1024 | tf_op jit(solution)/shard_map/pallas_call | solution.py:294
  40.0 1.6 %collective-permute-start.11 = (bf16[256,4096]{1,0:T(8,128)(2,1)}, bf16[256,4096]{1,0:T(8,128)(2,1)}, u32[]{:S(2)}, u32[]{:S(2)}) collective-permute-start(bf16[256,4096]{1,0:T(8,128)(2,1)} %shard_map.80.refs_7_), channel_id=1, source_target_pairs={{0,8},{8,0},{16,24},{24,16},{1,9},{9,1},{17,25},{25,17},{2,10},{10... | collective-permute-start | bytes 6291464 | tf_op jit(solution)/shard_map/ppermute | solution.py:430
  41.6 0.8 copy-done.10
  42.4 11.7 %shard_map.81 = (bf16[464,1024]{1,0:T(8,128)(2,1)}, bf16[464,1024]{1,0:T(8,128)(2,1)}) custom-call(s32[2,32]{1,0:T(2,128)} %bitcast.44, bf16[2,512,4096]{2,1,0:T(8,128)(2,1)} %bitcast.12, bf16[2,512,512]{2,1,0:T(8,128)(2,1)} %bitcast.18, bf16[2,512,512]{2,1,0:T(8,128)(2,1)} %bitcast.24, s32[2,512]{1,0:T(2,128)} %bitcast.32, s32[2,512]{1,0:T(2,128)} %bitcast.38, ...), custom_call_target="tpu_custom_call" | custom-call | flops 1024 | bytes 1024 | tf_op jit(solution)/shard_map/pallas_call | solution.py:294
  54.1 2.5 %collective-permute-start.8 = (bf16[464,1024]{1,0:T(8,128)(2,1)}, bf16[464,1024]{1,0:T(8,128)(2,1)S(1)}, u32[]{:S(2)}, u32[]{:S(2)}) collective-permute-start(bf16[464,1024]{1,0:T(8,128)(2,1)} %get-tuple-element.19.refs_7_.refs_1_), channel_id=1, source_target_pairs={{8,24},{16,0},{9,25},{17,1},{10,26},{18,2},{11,27},{19,3},{12,28},... | collective-permute-start | bytes 2850824 | tf_op jit(solution)/shard_map/ppermute | solution.py:432
  56.6 2.2 %copy.16.refs_0_ = bf16[464,1024]{1,0:T(8,128)(2,1)} copy(bf16[464,1024]{1,0:T(8,128)(2,1)} %get-tuple-element.18.refs_1_) | data formatting | bytes 1900544
  58.8 0.9 copy-done.4
  59.7 0.8 copy-done.6
  60.5 11.7 %shard_map.82 = (bf16[464,1024]{1,0:T(8,128)(2,1)}, bf16[464,1024]{1,0:T(8,128)(2,1)}) custom-call(s32[2,32]{1,0:T(2,128)} %bitcast.45, bf16[2,512,4096]{2,1,0:T(8,128)(2,1)} %bitcast.13, bf16[2,512,512]{2,1,0:T(8,128)(2,1)} %bitcast.19, bf16[2,512,512]{2,1,0:T(8,128)(2,1)} %bitcast.25, s32[2,512]{1,0:T(2,128)} %bitcast.33, s32[2,512]{1,0:T(2,128)} %bitcast.39, ...), custom_call_target="tpu_custom_call" | custom-call | flops 1024 | bytes 1024 | tf_op jit(solution)/shard_map/pallas_call | solution.py:294
  72.3 2.3 %collective-permute-start.5 = (bf16[464,1024]{1,0:T(8,128)(2,1)}, bf16[464,1024]{1,0:T(8,128)(2,1)}, u32[]{:S(2)}, u32[]{:S(2)}) collective-permute-start(bf16[464,1024]{1,0:T(8,128)(2,1)} %shard_map.83), channel_id=1, source_target_pairs={{8,24},{16,0},{9,25},{17,1},{10,26},{18,2},{11,27},{19,3},{12,28},... | collective-permute-start | bytes 2850824 | tf_op jit(solution)/shard_map/ppermute | solution.py:437
  74.6 3.4 %collective-permute-start.10 = (bf16[464,1024]{1,0:T(8,128)(2,1)}, bf16[464,1024]{1,0:T(8,128)(2,1)}, u32[]{:S(2)}, u32[]{:S(2)}) collective-permute-start(bf16[464,1024]{1,0:T(8,128)(2,1)} %get-tuple-element.20.refs_1_.refs_3_), channel_id=1, source_target_pairs={{8,16},{16,8},{9,17},{17,9},{10,18},{18,10},{11,19},{19,11},{12,20... | collective-permute-start | bytes 2850824 | tf_op jit(solution)/shard_map/ppermute | solution.py:436
  78.0 2.2 %copy.18.refs_0_ = bf16[464,1024]{1,0:T(8,128)(2,1)} copy(bf16[464,1024]{1,0:T(8,128)(2,1)} %get-tuple-element.21.refs_3_) | data formatting | bytes 1900544
  80.2 1.0 copy-done.11
  81.1 1.4 %collective-permute-start.9 = (bf16[464,1024]{1,0:T(8,128)(2,1)}, bf16[464,1024]{1,0:T(8,128)(2,1)}, u32[]{:S(2)}, u32[]{:S(2)}) collective-permute-start(bf16[464,1024]{1,0:T(8,128)(2,1)} %shard_map.86), channel_id=1, source_target_pairs={{24,16},{0,8},{25,17},{1,9},{26,18},{2,10},{27,19},{3,11},{28,20},... | collective-permute-start | bytes 2850824 | tf_op jit(solution)/shard_map/ppermute | solution.py:439
  82.5 14.1 %collective-permute-done.5.refs_0_.refs_1_ = bf16[464,1024]{1,0:T(8,128)(2,1)} collective-permute-done((bf16[464,1024]{1,0:T(8,128)(2,1)}, bf16[464,1024]{1,0:T(8,128)(2,1)}, u32[]{:S(2)}, u32[]{:S(2)}) %collective-permute-start.5) | collective-permute-done | bytes 950304 | tf_op jit(solution)/shard_map/ppermute | solution.py:437
  96.7 1.3 collective-permute-start.6
  98.0 3.6 %collective-permute-start.7 = (bf16[464,1024]{1,0:T(8,128)(2,1)}, bf16[464,1024]{1,0:T(8,128)(2,1)S(1)}, u32[]{:S(2)}, u32[]{:S(2)}) collective-permute-start(bf16[464,1024]{1,0:T(8,128)(2,1)} %shard_map.85), channel_id=1, source_target_pairs={{8,16},{16,8},{9,17},{17,9},{10,18},{18,10},{11,19},{19,11},{12,20... | collective-permute-start | bytes 2850824 | tf_op jit(solution)/shard_map/ppermute | solution.py:438
  101.6 0.9 copy-done.9
  102.6 3.9 %shard_map.87 = (bf16[512,4096]{1,0:T(8,128)(2,1)}, bf16[512,4096]{1,0:T(8,128)(2,1)}) custom-call(bf16[80,4096]{1,0:T(8,128)(2,1)S(1)} %copy-done.7, bf16[128,1024]{1,0:T(8,128)(2,1)S(1)} %copy-done.9, bf16[128,3072]{1,0:T(8,128)(2,1)S(1)} %copy-done.5, bf16[256,4096]{1,0:T(8,128)(2,1)} %collective-permute-done.11.refs_3_), custom_call_target="tpu_custom_call" | custom-call | flops 1024 | bytes 1024 | tf_op jit(solution)/shard_map/pallas_call | solution.py:393
  106.5 4.7 %collective-permute-done.10.refs_2_ = bf16[464,1024]{1,0:T(8,128)(2,1)} collective-permute-done((bf16[464,1024]{1,0:T(8,128)(2,1)}, bf16[464,1024]{1,0:T(8,128)(2,1)}, u32[]{:S(2)}, u32[]{:S(2)}) %collective-permute-start.10) | collective-permute-done | bytes 950304 | tf_op jit(solution)/shard_map/ppermute | solution.py:436
  111.3 3.2 %shard_map.88 = (bf16[512,4096]{1,0:T(8,128)(2,1)}, bf16[512,4096]{1,0:T(8,128)(2,1)}) custom-call(bf16[464,1024]{1,0:T(8,128)(2,1)} %collective-permute-done.9.refs_0_, bf16[464,1024]{1,0:T(8,128)(2,1)S(1)} %copy-done.3, bf16[464,1024]{1,0:T(8,128)(2,1)} %collective-permute-done.10.refs_2_, ...), custom_call_target="tpu_custom_call", output_to_operand_aliasing={{0}: (4, {}), {1}: (5, {})} | custom-call | flops 1024 | bytes 1024 | tf_op jit(solution)/shard_map/pallas_call | solution.py:393
  114.5 15.6 %collective-permute-done.6.refs_0_ = bf16[464,1024]{1,0:T(8,128)(2,1)S(1)} collective-permute-done((bf16[464,1024]{1,0:T(8,128)(2,1)}, bf16[464,1024]{1,0:T(8,128)(2,1)S(1)}, u32[]{:S(2)}, u32[]{:S(2)}) %collective-permute-start.6) | collective-permute-done | bytes 950304 | tf_op jit(solution)/shard_map/ppermute | solution.py:440
  130.1 2.4 %shard_map.89 = (bf16[512,4096]{1,0:T(8,128)(2,1)}, bf16[512,4096]{1,0:T(8,128)(2,1)}) custom-call(bf16[464,1024]{1,0:T(8,128)(2,1)S(1)} %collective-permute-done.6.refs_0_, bf16[464,1024]{1,0:T(8,128)(2,1)S(1)} %copy-done.1, bf16[464,1024]{1,0:T(8,128)(2,1)S(1)} %collective-permute-done.7.refs_2_, ...), custom_call_target="tpu_custom_call", output_to_operand_aliasing={{0}: (4, {}), {1}: (5, {})} | custom-call | flops 1024 | bytes 1024 | tf_op jit(solution)/shard_map/pallas_call | solution.py:393
  (33 shorter events, 2.2 us)
Async XLA Ops:
  4.1 8.3 %collective-permute-start = (bf16[128,1024]{1,0:T(8,128)(2,1)}, bf16[128,1024]{1,0:T(8,128)(2,1)S(1)}, u32[]{:S(2)}, u32[]{:S(2)}) collective-permute-start(bf16[128,1024]{1,0:T(8,128)(2,1)} %shard_map.77.refs_6_), channel_id=1, source_target_pairs={{0,8},{8,0},{16,24},{24,16},{1,9},{9,1},{17,25},{25,17},{2,10},{10... | collective-permute-start | bytes 786440 | tf_op jit(solution)/shard_map/ppermute | solution.py:422
  11.1 47.7 %collective-permute-start.3 = (bf16[128,3072]{1,0:T(8,128)(2,1)}, bf16[128,3072]{1,0:T(8,128)(2,1)S(1)}, u32[]{:S(2)}, u32[]{:S(2)}) collective-permute-start(bf16[128,3072]{1,0:T(8,128)(2,1)} %shard_map.78.refs_6_), channel_id=1, source_target_pairs={{0,8},{8,0},{16,24},{24,16},{1,9},{9,1},{17,25},{25,17},{2,10},{10... | collective-permute-start | bytes 2359304 | tf_op jit(solution)/shard_map/ppermute | solution.py:424
  12.4 0.7 copy-start.8
  18.2 11.1 %collective-permute-start.2 = (bf16[2,272,512]{2,1,0:T(8,128)(2,1)}, bf16[2,272,512]{2,1,0:T(8,128)(2,1)S(1)}, u32[]{:S(2)}, u32[]{:S(2)}) collective-permute-start(bf16[2,272,512]{2,1,0:T(8,128)(2,1)} %get-tuple-element.16), channel_id=1, source_target_pairs={{0,1},{1,2},{2,3},{3,4},{4,5},{5,6},{6,7},{8,9},{9,10},{10,11},{11... | collective-permute-start | bytes 1671176 | tf_op jit(solution)/shard_map/ppermute | solution.py:427
  20.1 38.7 %collective-permute-start.4 = (bf16[80,4096]{1,0:T(8,128)(2,1)}, bf16[80,4096]{1,0:T(8,128)(2,1)S(1)}, u32[]{:S(2)}, u32[]{:S(2)}) collective-permute-start(bf16[80,4096]{1,0:T(8,128)(2,1)} %get-tuple-element.17.refs_7_), channel_id=1, source_target_pairs={{0,8},{8,0},{16,24},{24,16},{1,9},{9,1},{17,25},{25,17},{2,10},{10... | collective-permute-start | bytes 1966088 | tf_op jit(solution)/shard_map/ppermute | solution.py:426
  21.7 19.9 %collective-permute-start.1 = (bf16[2,272,512]{2,1,0:T(8,128)(2,1)}, bf16[2,272,512]{2,1,0:T(8,128)(2,1)S(1)}, u32[]{:S(2)}, u32[]{:S(2)}) collective-permute-start(bf16[2,272,512]{2,1,0:T(8,128)(2,1)} %get-tuple-element.15), channel_id=1, source_target_pairs={{0,1},{1,2},{2,3},{3,4},{4,5},{5,6},{6,7},{8,9},{9,10},{10,11},{11... | collective-permute-start | bytes 1671176 | tf_op jit(solution)/shard_map/ppermute | solution.py:428
  29.2 0.8 copy-start.12
  40.0 61.6 %collective-permute-start.11 = (bf16[256,4096]{1,0:T(8,128)(2,1)}, bf16[256,4096]{1,0:T(8,128)(2,1)}, u32[]{:S(2)}, u32[]{:S(2)}) collective-permute-start(bf16[256,4096]{1,0:T(8,128)(2,1)} %shard_map.80.refs_7_), channel_id=1, source_target_pairs={{0,8},{8,0},{16,24},{24,16},{1,9},{9,1},{17,25},{25,17},{2,10},{10... | collective-permute-start | bytes 6291464 | tf_op jit(solution)/shard_map/ppermute | solution.py:430
  41.6 0.8 copy-start.10
  54.1 26.0 %collective-permute-start.8 = (bf16[464,1024]{1,0:T(8,128)(2,1)}, bf16[464,1024]{1,0:T(8,128)(2,1)S(1)}, u32[]{:S(2)}, u32[]{:S(2)}) collective-permute-start(bf16[464,1024]{1,0:T(8,128)(2,1)} %get-tuple-element.19.refs_7_.refs_1_), channel_id=1, source_target_pairs={{8,24},{16,0},{9,25},{17,1},{10,26},{18,2},{11,27},{19,3},{12,28},... | collective-permute-start | bytes 2850824 | tf_op jit(solution)/shard_map/ppermute | solution.py:432
  58.8 0.9 copy-start.4
  59.7 0.8 copy-start.6
  72.3 24.4 %collective-permute-start.5 = (bf16[464,1024]{1,0:T(8,128)(2,1)}, bf16[464,1024]{1,0:T(8,128)(2,1)}, u32[]{:S(2)}, u32[]{:S(2)}) collective-permute-start(bf16[464,1024]{1,0:T(8,128)(2,1)} %shard_map.83), channel_id=1, source_target_pairs={{8,24},{16,0},{9,25},{17,1},{10,26},{18,2},{11,27},{19,3},{12,28},... | collective-permute-start | bytes 2850824 | tf_op jit(solution)/shard_map/ppermute | solution.py:437
  74.6 36.6 %collective-permute-start.10 = (bf16[464,1024]{1,0:T(8,128)(2,1)}, bf16[464,1024]{1,0:T(8,128)(2,1)}, u32[]{:S(2)}, u32[]{:S(2)}) collective-permute-start(bf16[464,1024]{1,0:T(8,128)(2,1)} %get-tuple-element.20.refs_1_.refs_3_), channel_id=1, source_target_pairs={{8,16},{16,8},{9,17},{17,9},{10,18},{18,10},{11,19},{19,11},{12,20... | collective-permute-start | bytes 2850824 | tf_op jit(solution)/shard_map/ppermute | solution.py:436
  80.2 21.4 %copy-start.5 = (bf16[128,3072]{1,0:T(8,128)(2,1)S(1)}, bf16[128,3072]{1,0:T(8,128)(2,1)}, u32[]{:S(2)}) copy-start(bf16[128,3072]{1,0:T(8,128)(2,1)} %copy-done.4) | copy-start | bytes 2359300
  80.2 21.4 %copy-start.7 = (bf16[80,4096]{1,0:T(8,128)(2,1)S(1)}, bf16[80,4096]{1,0:T(8,128)(2,1)}, u32[]{:S(2)}) copy-start(bf16[80,4096]{1,0:T(8,128)(2,1)} %copy-done.6) | copy-start | bytes 1966084
  80.2 1.0 copy-start.11
  81.1 30.1 %copy-start = (bf16[464,1024]{1,0:T(8,128)(2,1)S(1)}, bf16[464,1024]{1,0:T(8,128)(2,1)}, u32[]{:S(2)}) copy-start(bf16[464,1024]{1,0:T(8,128)(2,1)} %get-tuple-element.20.refs_1_.refs_3_) | copy-start | bytes 2850820
  81.1 30.1 %copy-start.3 = (bf16[464,1024]{1,0:T(8,128)(2,1)S(1)}, bf16[464,1024]{1,0:T(8,128)(2,1)}, u32[]{:S(2)}) copy-start(bf16[464,1024]{1,0:T(8,128)(2,1)} %get-tuple-element.19.refs_7_.refs_1_) | copy-start | bytes 2850820
  81.1 30.1 %collective-permute-start.9 = (bf16[464,1024]{1,0:T(8,128)(2,1)}, bf16[464,1024]{1,0:T(8,128)(2,1)}, u32[]{:S(2)}, u32[]{:S(2)}) collective-permute-start(bf16[464,1024]{1,0:T(8,128)(2,1)} %shard_map.86), channel_id=1, source_target_pairs={{24,16},{0,8},{25,17},{1,9},{26,18},{2,10},{27,19},{3,11},{28,20},... | collective-permute-start | bytes 2850824 | tf_op jit(solution)/shard_map/ppermute | solution.py:439
  96.7 33.3 %collective-permute-start.6 = (bf16[464,1024]{1,0:T(8,128)(2,1)}, bf16[464,1024]{1,0:T(8,128)(2,1)S(1)}, u32[]{:S(2)}, u32[]{:S(2)}) collective-permute-start(bf16[464,1024]{1,0:T(8,128)(2,1)} %shard_map.84), channel_id=1, source_target_pairs={{24,16},{0,8},{25,17},{1,9},{26,18},{2,10},{27,19},{3,11},{28,20},... | collective-permute-start | bytes 2850824 | tf_op jit(solution)/shard_map/ppermute | solution.py:440
  98.0 32.1 %collective-permute-start.7 = (bf16[464,1024]{1,0:T(8,128)(2,1)}, bf16[464,1024]{1,0:T(8,128)(2,1)S(1)}, u32[]{:S(2)}, u32[]{:S(2)}) collective-permute-start(bf16[464,1024]{1,0:T(8,128)(2,1)} %shard_map.85), channel_id=1, source_target_pairs={{8,16},{16,8},{9,17},{17,9},{10,18},{18,10},{11,19},{19,11},{12,20... | collective-permute-start | bytes 2850824 | tf_op jit(solution)/shard_map/ppermute | solution.py:438
  101.6 1.0 copy-start.9
  111.3 18.8 %copy-start.1 = (bf16[464,1024]{1,0:T(8,128)(2,1)S(1)}, bf16[464,1024]{1,0:T(8,128)(2,1)}, u32[]{:S(2)}) copy-start(bf16[464,1024]{1,0:T(8,128)(2,1)} %get-tuple-element.18.refs_1_) | copy-start | bytes 2850820
  111.3 18.8 %copy-start.2 = (bf16[464,1024]{1,0:T(8,128)(2,1)S(1)}, bf16[464,1024]{1,0:T(8,128)(2,1)}, u32[]{:S(2)}) copy-start(bf16[464,1024]{1,0:T(8,128)(2,1)} %get-tuple-element.21.refs_3_) | copy-start | bytes 2850820

commit v4 on v3

--- a/solution.py
+++ b/solution.py
@@ -56,7 +56,7 @@
     return at + (first <= at).astype(jnp.int32)
 
 
-def attend_kernel(payload, groups, items, corner, pack, halo, *refs):
+def attend_kernel(payload, groups, items, corner, pack, halo, last, *refs):
     heads = [head for group in groups for head in group]
     refs = list(refs)
     lengths_in, queries, keys, values, seg_in, par_in = refs[:6]
@@ -73,6 +73,8 @@
         refs = refs[2:]
     if pack:
         packed = refs.pop(0)
+    if last:
+        last_q, last_out = refs[:2]
     rows = keys.shape[1]
     kv_heads = keys.shape[2] // HEAD
     width = queries.shape[2] // kv_heads
@@ -94,6 +96,11 @@
 
     lengths_copy = start(lengths_in, lengths)
     row_copies = [start(seg_in, segs), start(par_in, pars)]
+    query_copies = []
+    if last:
+        for at, head in enumerate(heads):
+            source = queries.at[path, pl.ds(TREE_MOST * BLK, BLK), pl.ds(head * width, width)]
+            query_copies.append(start(source, last_q.at[:, pl.ds(at * width, width)]))
     kv_copies = []
     for which, (source, target) in enumerate(((keys, kbuf), (values, vbuf))):
         kv_copies.append(start(source.at[path, :, lanes], target.at[pl.ds(REACH, rows)]))
@@ -135,11 +142,14 @@
             numbers = info[...].astype(jnp.float32)
             seg[:, :REACH] = (numbers[0:1, :REACH] * 128.0 + numbers[1:2, :REACH]).astype(jnp.int32)
             par[:, :REACH] = (numbers[2:3, :REACH] * 128.0 + numbers[3:4, :REACH]).astype(jnp.int32)
+
+    def all_ready():
+        rows_ready()
         for copy in kv_copies:
             copy.wait()
 
     if corner:
-        rows_ready()
+        all_ready()
     if pack:
         for each in range(2):
             at = lax.broadcasted_iota(jnp.int32, (INFO, REACH), 0)
@@ -198,56 +208,72 @@
                 corner_out[:HALF, place] = mixed[g]
                 corner_out[HALF:, place] = value[g * 16 : (g + 1) * 16]
         corner_stores = []
-        for out, heads_here in zip(outs, groups):
-            columns = pl.ds((heads_here[0] - heads[0]) * width, len(heads_here) * width)
-            corner_stores.append(start(corner_out.at[:, columns], out.at[pl.ds(len(items) * BLK, CORNER)]))
+        for at in range(taken):
+            rows_to = pl.ds(len(items) * BLK + at * CORNER, CORNER)
+            corner_stores.append(start(corner_out.at[:, pl.ds(at * width, width)], outs[0].at[rows_to]))
 
     def block_of(place):
         at = jnp.int32(items[-1])
         for other in range(len(items) - 1):
             at = jnp.where(place == other, jnp.int32(items[other]), at)
-        if min(items) >= TREE_MOST - 1:
-            return at + 1
         return at + (first <= at).astype(jnp.int32)
 
-    def body(skipped, taken, query_ref, out_ref):
-        step = marks[count]
-        marks[count] = step + 1
-        block, head = (block_of(lax.div(step, taken)), lax.rem(step, taken))
-
-        if not corner:
-            pl.when(step == 0)(rows_ready)
-
-        @pl.when(head == 0)
-        def _():
-            for back in range(TREE_MOST):
-                at = (TREE_MOST - 1 - back) * BLK
-                bias[:, at : at + BLK] = jnp.where(related(block, back), 0.0, NEG)
-
-        window = pl.ds(pl.multiple_of(block * BLK, BLK), SPAN)
-        at = pl.ds(pl.multiple_of((skipped + head) * HEAD, HEAD), HEAD)
-        scores = product_t(stacked(query_ref[0]), kbuf[window, at])
+    def build_bias(block):
+        for back in range(TREE_MOST):
+            at = (TREE_MOST - 1 - back) * BLK
+            bias[:, at : at + BLK] = jnp.where(related(block, back), 0.0, NEG)
+
+    def mixture(query, key, value):
+        scores = product_t(stacked(query), key)
         scores = scores.reshape(group, BLK, SPAN) + bias[...][None]
         top = jnp.max(scores, axis=-1, keepdims=True)
         weights = jnp.exp2((scores - top) * FACTOR)
         totals = jnp.sum(weights, axis=-1, keepdims=True)
         rounded = weights.astype(jnp.bfloat16).reshape(group * BLK, SPAN)
-        mixed = product(rounded, vbuf[window, at])
+        mixed = product(rounded, value)
         mixed = (mixed.reshape(group, BLK, HEAD) / totals).astype(jnp.bfloat16)
-        for g in range(group):
-            out_ref[:, g * HEAD : (g + 1) * HEAD] = mixed[g]
+        return jnp.concatenate([mixed[g] for g in range(group)], axis=1)
+
+    if last:
+        rows_ready()
+        build_bias(TREE_MOST)
+        for copy in kv_copies:
+            copy.wait()
+        stores = []
+        window = slice(TREE_MOST * BLK, TREE_MOST * BLK + SPAN)
+        for at, copy in enumerate(query_copies):
+            lanes = slice(at * HEAD, (at + 1) * HEAD)
+            place = slice(at * width, (at + 1) * width)
+            copy.wait()
+            last_out[:, place] = mixture(last_q[:, place], kbuf[window, lanes], vbuf[window, lanes])
+            stores.append(start(last_out.at[:, place], outs[0].at[:, place]))
+        for copy in stores:
+            copy.wait()
+        return
+
+    def body(skipped, taken, query_ref, out_ref):
+        step = marks[count]
+        marks[count] = step + 1
+        block, head = (block_of(lax.div(step, taken)), lax.rem(step, taken))
+
+        if not corner:
+            pl.when(step == 0)(all_ready)
+
+        pl.when(head == 0)(lambda: build_bias(block))
+        window = pl.ds(pl.multiple_of(block * BLK, BLK), SPAN)
+        at = pl.ds(pl.multiple_of((skipped + head) * HEAD, HEAD), HEAD)
+        out_ref[...] = mixture(query_ref[0], kbuf[window, at], vbuf[window, at])
 
     for out, heads_here in zip(outs, groups):
-        if items:
-            marks[count] = 0
-            pltpu.emit_pipeline(
-                functools.partial(body, heads_here[0] - heads[0], len(heads_here)),
-                grid=(len(items), len(heads_here)),
-                in_specs=[
-                    pl.BlockSpec((1, BLK, width), lambda i, h, at=heads_here[0]: (path, block_of(i), at + h))
-                ],
-                out_specs=[pl.BlockSpec((BLK, width), lambda i, h: (i, h))],
-            )(queries, out.at[pl.ds(0, len(items) * BLK)])
+        if not items:
+            continue
+        marks[count] = 0
+        pltpu.emit_pipeline(
+            functools.partial(body, heads_here[0] - heads[0], len(heads_here)),
+            grid=(len(items), len(heads_here)),
+            in_specs=[pl.BlockSpec((1, BLK, width), lambda i, h, at=heads_here[0]: (path, block_of(i), at + h))],
+            out_specs=[pl.BlockSpec((BLK, width), lambda i, h: (i, h))],
+        )(queries, out.at[pl.ds(0, len(items) * BLK)])
     if corner:
         for copy in corner_stores:
             copy.wait()
@@ -256,14 +282,16 @@
             copy.wait()
 
 
-def attend(payload, groups, items, operands, after=(), halo=None, corner=False, pack=False):
+def attend(payload, groups, items, operands, after=(), halo=None, corner=False, pack=False, last=False, weight=0):
     lengths, queries, keys, values, seg, par = operands
     rows, columns = queries.shape[1:]
     width = columns // (keys.shape[2] // HEAD)
     count = rows // BLK
     heads = [head for group in groups for head in group]
-    height = len(items) * BLK + (CORNER if corner else 0)
-    out_shape = [jax.ShapeDtypeStruct((height, len(group) * width), jnp.bfloat16) for group in groups]
+    sizes = [(len(items) * BLK, len(group) * width) for group in groups]
+    if corner:
+        sizes[0] = (len(items) * BLK + len(heads) * CORNER, width)
+    out_shape = [jax.ShapeDtypeStruct(size, jnp.bfloat16) for size in sizes]
     scratch = [
         pltpu.VMEM((REACH + rows, len(heads) * HEAD), jnp.bfloat16),
         pltpu.VMEM((REACH + rows, len(heads) * HEAD), jnp.bfloat16),
@@ -285,11 +313,13 @@
         packed = (2, 2, REACH + INFO, keys.shape[2])
         out_shape += [jax.ShapeDtypeStruct(packed[1:], jnp.bfloat16)] * 2
         scratch.append(pltpu.VMEM(packed, jnp.bfloat16))
+    if last:
+        scratch += [pltpu.VMEM((BLK, len(heads) * width), jnp.bfloat16)] * 2
     inputs = [lengths, queries, keys, values, seg, par] + ([] if halo is None else [halo])
 
     def kernel(*refs):
         refs = refs[: len(inputs)] + refs[len(inputs) + len(after) :]
-        attend_kernel(payload, groups, items, corner, pack, halo is not None, *refs)
+        attend_kernel(payload, groups, items, corner, pack, halo is not None, last, *refs)
 
     return pl.pallas_call(
         kernel,
@@ -298,7 +328,7 @@
         out_specs=[ANY] * len(out_shape),
         scratch_shapes=scratch,
         compiler_params=pltpu.CompilerParams(vmem_limit_bytes=VMEM_LIMIT),
-        cost_estimate=COST,
+        cost_estimate=cost(weight),
     )(*inputs, *after)
 
 
@@ -309,102 +339,118 @@
         in_specs=[ANY] * (1 + len(after)),
         out_specs=ANY,
         input_output_aliases={0: 0},
-        cost_estimate=COST,
+        cost_estimate=cost(0),
     )(value, *after)
 
 
 def place_kernel(pieces, aliased, *refs):
     refs = list(refs)
-    sources = [[refs.pop(0)] if swap else [refs.pop(0), refs.pop(0)] for swap, _, _, _ in pieces]
+    sources = [[refs.pop(0)] if piece[1] else [refs.pop(0), refs.pop(0)] for piece in pieces]
     refs = refs[aliased:]
     forward, back = refs[:2]
-    stages, blocks = (refs[2 : 2 + len(pieces)], refs[2 + len(pieces) : 2 + 2 * len(pieces)])
-    in_sems, out_sems = refs[2 + 2 * len(pieces) :]
+    stages = refs[2 : 2 + len(pieces)]
+    refs = refs[2 + len(pieces) :]
+    blocks = {at: refs.pop(0) for at, piece in enumerate(pieces) if piece[0] == "corner"}
+    in_sems, out_sems = refs
     width = forward.shape[1] // KV_HEADS
     group = width // HEAD
     where = lax.axis_index("pipe")
     even = lax.rem(where, 2) == 0
     edge = (where == 0) | (where == lax.axis_size("pipe") - 1)
 
-    for at, source in enumerate(sources):
-        if len(source) == 1:
-            pltpu.make_async_copy(source[0], stages[at], in_sems.at[at]).start()
+    parts = []
+    for at, (kind, _, _, items, top) in enumerate(pieces):
+        if kind == "plain":
+            parts += [(at, item * BLK, BLK, 0) for item in range(len(items))]
         else:
-            for own, mine in ((edge, source[1]), (jnp.logical_not(edge), source[0])):
-
-                @pl.when(own)
-                def _():
-                    pltpu.make_async_copy(mine, stages[at], in_sems.at[at]).start()
-
-    left, right = sides()
+            parts.append((at, 0, stages[at].shape[0], top))
+
+    def load(part, source):
+        at, top, height, below = parts[part]
+        view = (pl.ds(below + top, height), pl.ds(0, stages[at].shape[1]))
+        return pltpu.make_async_copy(source.at[view], stages[at].at[pl.ds(top, height)], in_sems.at[part])
+
+    for part, (at, _, _, _) in enumerate(parts):
+        if len(sources[at]) == 1:
+            load(part, sources[at][0]).start()
+        else:
+            pl.when(edge)(lambda: load(part, sources[at][1]).start())
+            pl.when(jnp.logical_not(edge))(lambda: load(part, sources[at][0]).start())
+
     first = {}
     stores = []
-    for at, (swap, heads, items, corner) in enumerate(pieces):
-        pltpu.make_async_copy(sources[at][0], stages[at], in_sems.at[at]).wait()
-        stage = stages[at]
-        top = len(items) * BLK
-        if corner:
-            tile = stage[top : top + 16, HALF : HALF + HEAD // 2].astype(jnp.float32)
-            spot = (lax.broadcasted_iota(jnp.int32, tile.shape, 0) == 0) & (lax.broadcasted_iota(jnp.int32, tile.shape, 1) == 0)
-            first[swap] = jnp.sum(jnp.where(spot, tile, 0.0)).astype(jnp.int32)
+
+    def store(at, source, block):
+        _, swap, heads, _, _ = pieces[at]
         columns = pl.ds(heads[0] * width, len(heads) * width)
-
-        def store(source, block):
-            rows = pl.ds(pl.multiple_of(block * BLK, BLK), BLK)
-            for to_forward, target in ((even != swap, forward), (even == swap, back)):
-
-                @pl.when(to_forward)
-                def _():
-                    pltpu.make_async_copy(source, target.at[rows, columns], out_sems.at[len(stores)]).start()
-
-            stores.append(pltpu.make_async_copy(source, forward.at[rows, columns], out_sems.at[len(stores)]))
-
-        for item, index in enumerate(items):
-            store(stage.at[pl.ds(item * BLK, BLK)], plain_block(first[swap], index))
-        if corner:
-            for head in range(len(heads)):
-                lanes = slice(head * width, (head + 1) * width)
-                tiles = stage[top + HALF : top + CORNER, lanes]
-                value = stacked(tiles)
-                turned = flipped(value)
-                shares = stage[top : top + HALF, lanes].astype(jnp.float32)
-                shares = stacked(shares).reshape(group, HALF, BLK)
-
-                def context(side, basis):
-                    kept = jnp.where(side[None], shares, 0.0)
-                    rest = 1.0 - jnp.sum(kept, axis=-1, keepdims=True)
-                    mixed = product(kept.astype(jnp.bfloat16).reshape(group * HALF, BLK), basis)
-                    mixed = mixed.reshape(group, HALF, HEAD) + rest * basis[HALF:].astype(jnp.float32)[None]
-                    mixed = mixed.astype(jnp.bfloat16)
-                    return jnp.concatenate([mixed[g] for g in range(group)], axis=1)
-
-                blocks[at][HALF:, lanes] = context(left, value)
-                blocks[at][:HALF, lanes] = flipped(context(right, turned))
-            store(blocks[at], first[swap])
+        rows = pl.ds(pl.multiple_of(block * BLK, BLK), BLK)
+        for to_forward, target in ((even != swap, forward), (even == swap, back)):
+
+            @pl.when(to_forward)
+            def _():
+                pltpu.make_async_copy(source, target.at[rows, columns], out_sems.at[len(stores)]).start()
+
+        stores.append(pltpu.make_async_copy(source, forward.at[rows, columns], out_sems.at[len(stores)]))
+
+    for part, (at, top, _, _) in enumerate(parts):
+        kind, swap, heads, items, _ = pieces[at]
+        load(part, sources[at][0]).wait()
+        if kind == "plain":
+            store(at, stages[at].at[pl.ds(top, BLK)], plain_block(first[swap], items[top // BLK]))
+        elif swap not in first:
+            tile = stages[at][:16, :HEAD].astype(jnp.float32)
+            row = lax.broadcasted_iota(jnp.int32, tile.shape, 0)
+            lane = lax.broadcasted_iota(jnp.int32, tile.shape, 1)
+            first[swap] = jnp.sum(jnp.where((row == 0) & (lane == HALF), tile, 0.0)).astype(jnp.int32)
+
+    left, right = sides()
+    for at, decoded in blocks.items():
+        value = stacked(stages[at][HALF:])
+        turned = flipped(value)
+        shares = stacked(stages[at][:HALF].astype(jnp.float32)).reshape(group, HALF, BLK)
+
+        def context(side, basis):
+            kept = jnp.where(side[None], shares, 0.0)
+            rest = 1.0 - jnp.sum(kept, axis=-1, keepdims=True)
+            mixed = product(kept.astype(jnp.bfloat16).reshape(group * HALF, BLK), basis)
+            mixed = mixed.reshape(group, HALF, HEAD) + rest * basis[HALF:].astype(jnp.float32)[None]
+            mixed = mixed.astype(jnp.bfloat16)
+            return jnp.concatenate([mixed[g] for g in range(group)], axis=1)
+
+        decoded[HALF:] = context(left, value)
+        decoded[:HALF] = flipped(context(right, turned))
+        store(at, decoded, first[pieces[at][1]])
     for copy in stores:
         copy.wait()
 
 
-def place(pieces, rows, outs=()):
-    arrays = [array for piece in pieces for array in piece[0]]
-    width = pieces[0][0][0].shape[1] // len(pieces[0][2])
-    shape = jax.ShapeDtypeStruct((rows, width * KV_HEADS), jnp.bfloat16)
-    held = [piece[0][0].shape for piece in pieces]
+def place(pieces, rows, outs=(), weight=0):
+    arrays = [array for piece in pieces for array in piece[1]]
+    columns = next(piece[1][0].shape[1] // len(piece[3]) for piece in pieces if piece[3]) * KV_HEADS
+    shape = jax.ShapeDtypeStruct((rows, columns), jnp.bfloat16)
+    width = columns // KV_HEADS
+    corners = {"guide": (16, HEAD), "corner": (CORNER, width)}
+    held = [corners.get(kind, (len(items) * BLK, len(heads) * width)) for kind, _, _, heads, items, _ in pieces]
+    decoded = [(BLK, width) for piece in pieces if piece[0] == "corner"]
     return pl.pallas_call(
-        functools.partial(place_kernel, [piece[1:] for piece in pieces], len(outs)),
+        functools.partial(place_kernel, [(piece[0],) + piece[2:] for piece in pieces], len(outs)),
         out_shape=[shape, shape],
         in_specs=[ANY] * len(arrays) + [HBM] * len(outs),
         out_specs=[HBM, HBM],
-        scratch_shapes=[pltpu.VMEM(size, jnp.bfloat16) for size in held]
-        + [pltpu.VMEM((BLK, size[1]), jnp.bfloat16) for size in held]
-        + [pltpu.SemaphoreType.DMA((len(pieces),)), pltpu.SemaphoreType.DMA((4 * len(pieces),))],
+        scratch_shapes=[pltpu.VMEM(size, jnp.bfloat16) for size in held + decoded]
+        + [pltpu.SemaphoreType.DMA((4 * len(pieces),))] * 2,
         input_output_aliases={len(arrays) + i: i for i in range(len(outs))},
         compiler_params=pltpu.CompilerParams(vmem_limit_bytes=24 * 1024 * 1024),
-        cost_estimate=COST,
+        cost_estimate=cost(weight),
     )(*arrays, *outs)
 
 
-COST = pl.CostEstimate(flops=1024, bytes_accessed=1024, transcendentals=0)
+def cost(weight):
+    return pl.CostEstimate(flops=1024 + weight * 1000000, bytes_accessed=1024, transcendentals=0)
+
+
+PLACE_WEIGHT = 0
+DIRECT_WEIGHT = 100000
 
 SWAP = [(0, 1), (1, 0), (2, 3), (3, 2)]
 DIAGONAL = [(1, 2), (2, 1)]
@@ -418,20 +464,27 @@
     ring = [(source, source + 1) for source in range(lax.axis_size("dp") - 1)]
     every = tuple(range(KV_HEADS))
 
-    (swap_0,) = attend(0, ((0,),), (2,), operands)
+    (swap_0,) = attend(0, ((0, 1),), (2,), operands, last=True)
     got_0 = lax.ppermute(swap_0, "pipe", SWAP)
-    (swap_1,) = attend(0, ((1, 2, 3),), (2,), operands, after=(swap_0,))
-    got_1 = lax.ppermute(swap_1, "pipe", SWAP)
-    corner, halo, far_halo = attend(0, (every,), (), operands, after=(swap_1, got_0), corner=True, pack=True)
+    corner, halo, far_halo = attend(0, (every,), (), operands, after=(swap_0,), corner=True, pack=True)
     got_corner = lax.ppermute(corner, "pipe", SWAP)
     halo = lax.ppermute(halo, "dp", ring)
     far_halo = lax.ppermute(far_halo, "dp", ring)
-    (swap_2,) = attend(0, (every,), (0, 1), operands, after=(corner,), halo=halo)
+    (swap_1,) = attend(0, ((2, 3),), (2,), operands, after=(corner, got_0), last=True)
+    got_1 = lax.ppermute(swap_1, "pipe", SWAP)
+    (swap_2,) = attend(0, (every,), (0, 1), operands, after=(swap_1,), halo=halo)
     got_2 = lax.ppermute(swap_2, "pipe", SWAP)
     routed_1, routed_2 = attend(1, ((0,), (1,)), (0, 1, 2), operands, after=(swap_2,), halo=far_halo, corner=True)
     across_1 = lax.ppermute(routed_1, "pipe", ACROSS)
     direct_1, direct_2 = attend(
-        1, ((2,), (3,)), (0, 1, 2), operands, after=(routed_1, got_1, got_corner), halo=far_halo, corner=True
+        1,
+        ((2,), (3,)),
+        (0, 1, 2),
+        operands,
+        after=(routed_1, got_1, got_corner),
+        halo=far_halo,
+        corner=True,
+        weight=DIRECT_WEIGHT,
     )
     diagonal_1 = lax.ppermute(direct_1, "pipe", DIAGONAL)
     across_2 = lax.ppermute(behind(routed_2, direct_1), "pipe", ACROSS)
@@ -439,26 +492,34 @@
     onward_1 = lax.ppermute(behind(across_1, direct_1), "pipe", ONWARD)
     onward_2 = lax.ppermute(behind(across_2, direct_1), "pipe", ONWARD)
     outs = place(
-        [
-            ((got_corner,), True, every, (), True),
-            ((got_0,), True, (0,), (2,), False),
-            ((got_1,), True, (1, 2, 3), (2,), False),
-            ((got_2,), True, every, (0, 1), False),
+        [("corner", (got_corner,), True, (head,), (), head * CORNER) for head in every]
+        + [
+            ("plain", (got_0,), True, (0, 1), (2,), 0),
+            ("plain", (got_1,), True, (2, 3), (2,), 0),
+            ("plain", (got_2,), True, every, (0, 1), 0),
         ],
         rows,
+        weight=PLACE_WEIGHT,
     )
+    below = TREE_MOST * BLK
+    onward_1, diagonal_1 = ((onward_1, routed_1), (diagonal_1, direct_1))
     outs = place(
         [
-            ((onward_1, routed_1), False, (0,), (0, 1, 2), True),
-            ((diagonal_1, direct_1), False, (2,), (0, 1, 2), True),
+            ("corner", onward_1, False, (0,), (), below),
+            ("corner", onward_1, False, (1,), (), below + CORNER),
+            ("corner", diagonal_1, False, (2,), (), below),
+            ("corner", diagonal_1, False, (3,), (), below + CORNER),
+            ("plain", onward_1, False, (0,), (0, 1, 2), 0),
+            ("plain", diagonal_1, False, (2,), (0, 1, 2), 0),
         ],
         rows,
         outs,
     )
     forward, back = place(
         [
-            ((onward_2, routed_2), False, (1,), (0, 1, 2), True),
-            ((diagonal_2, direct_2), False, (3,), (0, 1, 2), True),
+            ("guide", diagonal_1, False, (), (), below),
+            ("plain", (onward_2, routed_2), False, (1,), (0, 1, 2), 0),
+            ("plain", (diagonal_2, direct_2), False, (3,), (0, 1, 2), 0),
         ],
         rows,
         outs,

time: 134 us -> 133 us (level)
  local copies, waits for them, and re-layouts: 10.4 us -> 8.09 us
  starting transfers between devices: 24.9 us -> 27.1 us
  waiting for transfers between devices: 39.5 us -> 37.8 us
    ppermute x1, waiting for transfers between devices: 4.7 us -> 11.2 us  [on_device(): diagonal_1 = lax.ppermute(direct_1, 'pipe', DIAGONAL)]
    ppermute x1, waiting for transfers between devices: 15.6 us -> 11.2 us  [on_device(): onward_2 = lax.ppermute(behind(across_2, direct_1), 'pipe', ONWARD)]
    ppermute x1, waiting for transfers between devices: 4.27 us -> 0.01 us  [on_device(): halo = lax.ppermute(halo, 'dp', ring)]
    ppermute x1, waiting for transfers between devices: 14.1 us -> 10.8 us  [on_device(): across_2 = lax.ppermute(behind(routed_2, direct_1), 'pipe', ACROSS)]
    unnamed x28 -> x30, local copies, waits for them, and re-layouts: 10.4 us -> 8.09 us
    ppermute x1, waiting for transfers between devices: 0.01 us -> 2.09 us  [on_device(): across_1 = lax.ppermute(routed_1, 'pipe', ACROSS)]
    pallas_call x6, Pallas kernels: 47.3 us -> 45.3 us  [attend(): pl.pallas_call(kernel, out_shape=out_shape, in_specs=[HBM] * 6 + [ANY] *...]
    pallas_call x3, Pallas kernels: 9.57 us -> 11.4 us  [place(): pl.pallas_call(functools.partial(place_kernel, [(piece[0],) + piece[2:] f...]
  transfers between devices with their start and end apart: 12 -> 12, of which waited for: 6 -> 6; matrix products, arithmetic and copies ran while one was open for 3% -> 2% of each run, Pallas kernels for 38% -> 40%
where the time goes in v4:
time: 133 us; the launch traced here: 131 us
  Pallas kernels  56.7 us (43%)
  waiting for transfers between devices  37.8 us (28%)
  starting transfers between devices  27.1 us (20%)
  local copies, waits for them, and re-layouts  8.09 us (6%)
    pallas_call x6, Pallas kernels, attend(): pl.pallas_call(kernel, out_shape=out_shape, in_specs=[HBM] * 6 + [ANY] *...  45.3 us
    pallas_call x3, Pallas kernels, place(): pl.pallas_call(functools.partial(place_kernel, [(piece[0],) + piece[2:] f...  11.4 us
    ppermute x1, waiting for transfers between devices, on_device(): onward_2 = lax.ppermute(behind(across_2, direct_1), 'pipe', ONWARD)  11.2 us
    ppermute x1, waiting for transfers between devices, on_device(): diagonal_1 = lax.ppermute(direct_1, 'pipe', DIAGONAL)  11.2 us
    ppermute x1, waiting for transfers between devices, on_device(): across_2 = lax.ppermute(behind(routed_2, direct_1), 'pipe', ACROSS)  10.8 us
    unnamed x30, local copies, waits for them, and re-layouts  8.09 us
    ppermute x1, starting transfers between devices, on_device(): diagonal_1 = lax.ppermute(direct_1, 'pipe', DIAGONAL)  4.34 us
    ppermute x1, starting transfers between devices, on_device(): diagonal_2 = lax.ppermute(behind(direct_2, across_2), 'pipe', DIAGONAL)  4.28 us
  transfers between devices with their start and end apart: 12, of which 6 were waited for; matrix products, arithmetic and copies ran while one was open for 2% of the time, Pallas kernels for 40%

profile of v4, /device:TPU:20, one launch (start us, length us, event | category | flops | bytes accessed | tf_op | source)
XLA Modules:
  0.0 130.7 jit_solution(13567987474709764056)
XLA Ops:
  0.6 3.4 %shard_map.77.refs_6_ = bf16[128,2048]{1,0:T(8,128)(2,1)} custom-call(s32[2,32]{1,0:T(2,128)} %bitcast.40, bf16[2,512,4096]{2,1,0:T(8,128)(2,1)} %bitcast.8, bf16[2,512,512]{2,1,0:T(8,128)(2,1)} %bitcast.14, bf16[2,512,512]{2,1,0:T(8,128)(2,1)} %bitcast.20, s32[2,512]{1,0:T(2,128)} %bitcast.28, s32[2,512]{1,0:T(2,128)} %bitcast.34), custom_call_target="tpu_custom_call" | custom-call | flops 1024 | bytes 1024 | tf_op jit(solution)/shard_map/pallas_call | solution.py:324
  4.1 1.6 %collective-permute-start.2 = (bf16[128,2048]{1,0:T(8,128)(2,1)}, bf16[128,2048]{1,0:T(8,128)(2,1)S(1)}, u32[]{:S(2)}, u32[]{:S(2)}) collective-permute-start(bf16[128,2048]{1,0:T(8,128)(2,1)} %shard_map.77.refs_6_), channel_id=1, source_target_pairs={{0,8},{8,0},{16,24},{24,16},{1,9},{9,1},{17,25},{25,17},{2,10},{10... | collective-permute-start | bytes 1572872 | tf_op jit(solution)/shard_map/ppermute | solution.py:468
  5.6 5.0 %shard_map.78 = (bf16[320,1024]{1,0:T(8,128)(2,1)}, bf16[2,272,512]{2,1,0:T(8,128)(2,1)}, bf16[2,272,512]{2,1,0:T(8,128)(2,1)}) custom-call(s32[2,32]{1,0:T(2,128)} %bitcast.41, bf16[2,512,4096]{2,1,0:T(8,128)(2,1)} %bitcast.9, bf16[2,512,512]{2,1,0:T(8,128)(2,1)} %bitcast.15, bf16[2,512,512]{2,1,0:T(8,128)(2,1)} %bitcast.21, s32[2,512]{1,0:T(2,128)} %bitcast.29, ...), custom_call_target="tpu_custom_call" | custom-call | flops 1024 | bytes 1024 | tf_op jit(solution)/shard_map/pallas_call | solution.py:324
  11.3 1.9 %collective-permute-start.1 = (bf16[2,272,512]{2,1,0:T(8,128)(2,1)}, bf16[2,272,512]{2,1,0:T(8,128)(2,1)S(1)}, u32[]{:S(2)}, u32[]{:S(2)}) collective-permute-start(bf16[2,272,512]{2,1,0:T(8,128)(2,1)} %get-tuple-element.16), channel_id=1, source_target_pairs={{0,1},{1,2},{2,3},{3,4},{4,5},{5,6},{6,7},{8,9},{9,10},{10,11},{11... | collective-permute-start | bytes 1671176 | tf_op jit(solution)/shard_map/ppermute | solution.py:471
  13.2 3.6 %collective-permute-start = (bf16[2,272,512]{2,1,0:T(8,128)(2,1)}, bf16[2,272,512]{2,1,0:T(8,128)(2,1)S(1)}, u32[]{:S(2)}, u32[]{:S(2)}) collective-permute-start(bf16[2,272,512]{2,1,0:T(8,128)(2,1)} %get-tuple-element.15), channel_id=1, source_target_pairs={{0,1},{1,2},{2,3},{3,4},{4,5},{5,6},{6,7},{8,9},{9,10},{10,11},{11... | collective-permute-start | bytes 1671176 | tf_op jit(solution)/shard_map/ppermute | solution.py:472
  16.8 2.4 %collective-permute-done.2.refs_7_.refs_4_ = bf16[128,2048]{1,0:T(8,128)(2,1)S(1)} collective-permute-done((bf16[128,2048]{1,0:T(8,128)(2,1)}, bf16[128,2048]{1,0:T(8,128)(2,1)S(1)}, u32[]{:S(2)}, u32[]{:S(2)}) %collective-permute-start.2) | collective-permute-done | bytes 524320 | tf_op jit(solution)/shard_map/ppermute | solution.py:468
  19.2 0.8 copy-done.8
  20.0 3.5 %shard_map.79.refs_7_ = bf16[128,2048]{1,0:T(8,128)(2,1)} custom-call(s32[2,32]{1,0:T(2,128)} %bitcast.42, bf16[2,512,4096]{2,1,0:T(8,128)(2,1)} %bitcast.10, bf16[2,512,512]{2,1,0:T(8,128)(2,1)} %bitcast.16, bf16[2,512,512]{2,1,0:T(8,128)(2,1)} %bitcast.22, s32[2,512]{1,0:T(2,128)} %bitcast.30, s32[2,512]{1,0:T(2,128)} %bitcast.36, ...), custom_call_target="tpu_custom_call" | custom-call | flops 1024 | bytes 1024 | tf_op jit(solution)/shard_map/pallas_call | solution.py:324
  23.4 1.6 %collective-permute-start.3 = (bf16[128,2048]{1,0:T(8,128)(2,1)}, bf16[128,2048]{1,0:T(8,128)(2,1)S(1)}, u32[]{:S(2)}, u32[]{:S(2)}) collective-permute-start(bf16[128,2048]{1,0:T(8,128)(2,1)} %shard_map.79.refs_7_), channel_id=1, source_target_pairs={{0,8},{8,0},{16,24},{24,16},{1,9},{9,1},{17,25},{25,17},{2,10},{10... | collective-permute-start | bytes 1572872 | tf_op jit(solution)/shard_map/ppermute | solution.py:474
  25.0 0.8 copy-done.13
  25.8 9.9 %shard_map.80.refs_7_ = bf16[256,4096]{1,0:T(8,128)(2,1)} custom-call(s32[2,32]{1,0:T(2,128)} %bitcast.43, bf16[2,512,4096]{2,1,0:T(8,128)(2,1)} %bitcast.11, bf16[2,512,512]{2,1,0:T(8,128)(2,1)} %bitcast.17, bf16[2,512,512]{2,1,0:T(8,128)(2,1)} %bitcast.23, s32[2,512]{1,0:T(2,128)} %bitcast.31, s32[2,512]{1,0:T(2,128)} %bitcast.37, ...), custom_call_target="tpu_custom_call" | custom-call | flops 1024 | bytes 1024 | tf_op jit(solution)/shard_map/pallas_call | solution.py:324
  36.3 0.8 copy-done.12
  37.2 11.7 %shard_map.81 = (bf16[544,1024]{1,0:T(8,128)(2,1)}, bf16[384,1024]{1,0:T(8,128)(2,1)}) custom-call(s32[2,32]{1,0:T(2,128)} %bitcast.44, bf16[2,512,4096]{2,1,0:T(8,128)(2,1)} %bitcast.12, bf16[2,512,512]{2,1,0:T(8,128)(2,1)} %bitcast.18, bf16[2,512,512]{2,1,0:T(8,128)(2,1)} %bitcast.24, s32[2,512]{1,0:T(2,128)} %bitcast.32, s32[2,512]{1,0:T(2,128)} %bitcast.38, ...), custom_call_target="tpu_custom_call" | custom-call | flops 1024 | bytes 1024 | tf_op jit(solution)/shard_map/pallas_call | solution.py:324
  48.9 3.4 %collective-permute-start.9 = (bf16[544,1024]{1,0:T(8,128)(2,1)}, bf16[544,1024]{1,0:T(8,128)(2,1)}, u32[]{:S(2)}, u32[]{:S(2)}) collective-permute-start(bf16[544,1024]{1,0:T(8,128)(2,1)} %get-tuple-element.18.refs_7_.refs_1_.refs_3_.refs_9_), channel_id=1, source_target_pairs={{8,24},{16,0},{9,25},{17,1},{10,26},{18,2},{11,27},{19,3},{12,28},... | collective-permute-start | bytes 3342344 | tf_op jit(solution)/shard_map/ppermute | solution.py:478
  52.3 2.1 %copy.16.refs_0_ = bf16[384,1024]{1,0:T(8,128)(2,1)} copy(bf16[384,1024]{1,0:T(8,128)(2,1)} %get-tuple-element.20.refs_3_) | data formatting | bytes 1572864
  54.4 0.9 copy-done.2
  55.2 0.8 copy-done.10
  56.0 11.7 %shard_map.82 = (bf16[544,1024]{1,0:T(8,128)(2,1)}, bf16[384,1024]{1,0:T(8,128)(2,1)}) custom-call(s32[2,32]{1,0:T(2,128)} %bitcast.45, bf16[2,512,4096]{2,1,0:T(8,128)(2,1)} %bitcast.13, bf16[2,512,512]{2,1,0:T(8,128)(2,1)} %bitcast.19, bf16[2,512,512]{2,1,0:T(8,128)(2,1)} %bitcast.25, s32[2,512]{1,0:T(2,128)} %bitcast.33, s32[2,512]{1,0:T(2,128)} %bitcast.39, ...), custom_call_target="tpu_custom_call" | custom-call | flops 99999997952 | bytes 1024 | tf_op jit(solution)/shard_map/pallas_call | solution.py:324
  67.8 2.4 %collective-permute-start.6 = (bf16[384,1024]{1,0:T(8,128)(2,1)}, bf16[384,1024]{1,0:T(8,128)(2,1)}, u32[]{:S(2)}, u32[]{:S(2)}) collective-permute-start(bf16[384,1024]{1,0:T(8,128)(2,1)} %shard_map.83), channel_id=1, source_target_pairs={{8,24},{16,0},{9,25},{17,1},{10,26},{18,2},{11,27},{19,3},{12,28},... | collective-permute-start | bytes 2359304 | tf_op jit(solution)/shard_map/ppermute | solution.py:490
  70.2 4.3 %collective-permute-start.5 = (bf16[544,1024]{1,0:T(8,128)(2,1)S(1)}, bf16[544,1024]{1,0:T(8,128)(2,1)S(1)}, u32[]{:S(2)}, u32[]{:S(2)}) collective-permute-start(bf16[544,1024]{1,0:T(8,128)(2,1)S(1)} %copy-done), channel_id=1, source_target_pairs={{8,16},{16,8},{9,17},{17,9},{10,18},{18,10},{11,19},{19,11},{12,20... | collective-permute-start | bytes 3342344 | tf_op jit(solution)/shard_map/ppermute | solution.py:489
  74.5 2.1 %collective-permute-done.9.refs_0_ = bf16[544,1024]{1,0:T(8,128)(2,1)} collective-permute-done((bf16[544,1024]{1,0:T(8,128)(2,1)}, bf16[544,1024]{1,0:T(8,128)(2,1)}, u32[]{:S(2)}, u32[]{:S(2)}) %collective-permute-start.9) | collective-permute-done | bytes 1114144 | tf_op jit(solution)/shard_map/ppermute | solution.py:478
  76.6 1.5 %collective-permute-start.10 = (bf16[544,1024]{1,0:T(8,128)(2,1)}, bf16[544,1024]{1,0:T(8,128)(2,1)}, u32[]{:S(2)}, u32[]{:S(2)}) collective-permute-start(bf16[544,1024]{1,0:T(8,128)(2,1)} %shard_map.86), channel_id=1, source_target_pairs={{24,16},{0,8},{25,17},{1,9},{26,18},{2,10},{27,19},{3,11},{28,20},... | collective-permute-start | bytes 3342344 | tf_op jit(solution)/shard_map/ppermute | solution.py:492
  78.1 0.9 copy.18.refs_0_
  79.0 10.8 %collective-permute-done.6.refs_0_.refs_1_ = bf16[384,1024]{1,0:T(8,128)(2,1)} collective-permute-done((bf16[384,1024]{1,0:T(8,128)(2,1)}, bf16[384,1024]{1,0:T(8,128)(2,1)}, u32[]{:S(2)}, u32[]{:S(2)}) %collective-permute-start.6) | collective-permute-done | bytes 786464 | tf_op jit(solution)/shard_map/ppermute | solution.py:490
  89.8 1.4 %collective-permute-start.7 = (bf16[384,1024]{1,0:T(8,128)(2,1)}, bf16[384,1024]{1,0:T(8,128)(2,1)S(1)}, u32[]{:S(2)}, u32[]{:S(2)}) collective-permute-start(bf16[384,1024]{1,0:T(8,128)(2,1)} %shard_map.84), channel_id=1, source_target_pairs={{24,16},{0,8},{25,17},{1,9},{26,18},{2,10},{27,19},{3,11},{28,20},... | collective-permute-start | bytes 2359304 | tf_op jit(solution)/shard_map/ppermute | solution.py:493
  91.2 4.3 %collective-permute-start.8 = (bf16[384,1024]{1,0:T(8,128)(2,1)}, bf16[384,1024]{1,0:T(8,128)(2,1)S(1)}, u32[]{:S(2)}, u32[]{:S(2)}) collective-permute-start(bf16[384,1024]{1,0:T(8,128)(2,1)} %shard_map.85), channel_id=1, source_target_pairs={{8,16},{16,8},{9,17},{17,9},{10,18},{18,10},{11,19},{19,11},{12,20... | collective-permute-start | bytes 2359304 | tf_op jit(solution)/shard_map/ppermute | solution.py:491
  95.5 1.0 copy-done.11
  96.6 5.5 %shard_map.87 = (bf16[512,4096]{1,0:T(8,128)(2,1)}, bf16[512,4096]{1,0:T(8,128)(2,1)}) custom-call(bf16[320,1024]{1,0:T(8,128)(2,1)S(1)} %copy-done.3, bf16[320,1024]{1,0:T(8,128)(2,1)S(1)} %copy-done.3, bf16[320,1024]{1,0:T(8,128)(2,1)S(1)} %copy-done.3, bf16[320,1024]{1,0:T(8,128)(2,1)S(1)} %copy-done.3, bf16[128,2048]{1,0:T(8,128)(2,1)S(1)} %copy-done.9, ...), custom_call_target="tpu_custom_call" | custom-call | flops 1024 | bytes 1024 | tf_op jit(solution)/shard_map/pallas_call | solution.py:435
  102.0 11.2 %collective-permute-done.5.refs_4_.refs_6_.refs_10_.refs_0_ = bf16[544,1024]{1,0:T(8,128)(2,1)S(1)} collective-permute-done((bf16[544,1024]{1,0:T(8,128)(2,1)S(1)}, bf16[544,1024]{1,0:T(8,128)(2,1)S(1)}, u32[]{:S(2)}, u32[]{:S(2)}) %collective-permute-start.5) | collective-permute-done | bytes 1114144 | tf_op jit(solution)/shard_map/ppermute | solution.py:489
  113.4 4.4 %shard_map.88 = (bf16[512,4096]{1,0:T(8,128)(2,1)}, bf16[512,4096]{1,0:T(8,128)(2,1)}) custom-call(bf16[544,1024]{1,0:T(8,128)(2,1)} %collective-permute-done.10.refs_0_.refs_2_.refs_8_, bf16[544,1024]{1,0:T(8,128)(2,1)S(1)} %copy-done.4, ...), custom_call_target="tpu_custom_call", output_to_operand_aliasing={{0}: (12, {}), {1}: (13, {})} | custom-call | flops 1024 | bytes 1024 | tf_op jit(solution)/shard_map/pallas_call | solution.py:435
  117.8 11.2 %collective-permute-done.7.refs_2_ = bf16[384,1024]{1,0:T(8,128)(2,1)S(1)} collective-permute-done((bf16[384,1024]{1,0:T(8,128)(2,1)}, bf16[384,1024]{1,0:T(8,128)(2,1)S(1)}, u32[]{:S(2)}, u32[]{:S(2)}) %collective-permute-start.7) | collective-permute-done | bytes 786464 | tf_op jit(solution)/shard_map/ppermute | solution.py:493
  129.0 1.6 %shard_map.89 = (bf16[512,4096]{1,0:T(8,128)(2,1)}, bf16[512,4096]{1,0:T(8,128)(2,1)}) custom-call(bf16[544,1024]{1,0:T(8,128)(2,1)S(1)} %collective-permute-done.5.refs_4_.refs_6_.refs_10_.refs_0_, bf16[544,1024]{1,0:T(8,128)(2,1)S(1)} %copy-done.1, ...), custom_call_target="tpu_custom_call", output_to_operand_aliasing={{0}: (6, {}), {1}: (7, {})} | custom-call | flops 1024 | bytes 1024 | tf_op jit(solution)/shard_map/pallas_call | solution.py:435
  (35 shorter events, 1.4 us)
Async XLA Ops:
  4.1 15.1 %collective-permute-start.2 = (bf16[128,2048]{1,0:T(8,128)(2,1)}, bf16[128,2048]{1,0:T(8,128)(2,1)S(1)}, u32[]{:S(2)}, u32[]{:S(2)}) collective-permute-start(bf16[128,2048]{1,0:T(8,128)(2,1)} %shard_map.77.refs_6_), channel_id=1, source_target_pairs={{0,8},{8,0},{16,24},{24,16},{1,9},{9,1},{17,25},{25,17},{2,10},{10... | collective-permute-start | bytes 1572872 | tf_op jit(solution)/shard_map/ppermute | solution.py:468
  10.7 43.7 %collective-permute-start.4 = (bf16[320,1024]{1,0:T(8,128)(2,1)}, bf16[320,1024]{1,0:T(8,128)(2,1)S(1)}, u32[]{:S(2)}, u32[]{:S(2)}) collective-permute-start(bf16[320,1024]{1,0:T(8,128)(2,1)} %get-tuple-element.17.refs_6_), channel_id=1, source_target_pairs={{0,8},{8,0},{16,24},{24,16},{1,9},{9,1},{17,25},{25,17},{2,10},{10... | collective-permute-start | bytes 1966088 | tf_op jit(solution)/shard_map/ppermute | solution.py:470
  11.3 13.7 %collective-permute-start.1 = (bf16[2,272,512]{2,1,0:T(8,128)(2,1)}, bf16[2,272,512]{2,1,0:T(8,128)(2,1)S(1)}, u32[]{:S(2)}, u32[]{:S(2)}) collective-permute-start(bf16[2,272,512]{2,1,0:T(8,128)(2,1)} %get-tuple-element.16), channel_id=1, source_target_pairs={{0,1},{1,2},{2,3},{3,4},{4,5},{5,6},{6,7},{8,9},{9,10},{10,11},{11... | collective-permute-start | bytes 1671176 | tf_op jit(solution)/shard_map/ppermute | solution.py:471
  13.2 23.1 %collective-permute-start = (bf16[2,272,512]{2,1,0:T(8,128)(2,1)}, bf16[2,272,512]{2,1,0:T(8,128)(2,1)S(1)}, u32[]{:S(2)}, u32[]{:S(2)}) collective-permute-start(bf16[2,272,512]{2,1,0:T(8,128)(2,1)} %get-tuple-element.15), channel_id=1, source_target_pairs={{0,1},{1,2},{2,3},{3,4},{4,5},{5,6},{6,7},{8,9},{9,10},{10,11},{11... | collective-permute-start | bytes 1671176 | tf_op jit(solution)/shard_map/ppermute | solution.py:472
  19.2 0.8 copy-start.8
  23.4 31.0 %collective-permute-start.3 = (bf16[128,2048]{1,0:T(8,128)(2,1)}, bf16[128,2048]{1,0:T(8,128)(2,1)S(1)}, u32[]{:S(2)}, u32[]{:S(2)}) collective-permute-start(bf16[128,2048]{1,0:T(8,128)(2,1)} %shard_map.79.refs_7_), channel_id=1, source_target_pairs={{0,8},{8,0},{16,24},{24,16},{1,9},{9,1},{17,25},{25,17},{2,10},{10... | collective-permute-start | bytes 1572872 | tf_op jit(solution)/shard_map/ppermute | solution.py:474
  25.0 0.8 copy-start.13
  35.7 59.8 %collective-permute-start.11 = (bf16[256,4096]{1,0:T(8,128)(2,1)}, bf16[256,4096]{1,0:T(8,128)(2,1)}, u32[]{:S(2)}, u32[]{:S(2)}) collective-permute-start(bf16[256,4096]{1,0:T(8,128)(2,1)} %shard_map.80.refs_7_), channel_id=1, source_target_pairs={{0,8},{8,0},{16,24},{24,16},{1,9},{9,1},{17,25},{25,17},{2,10},{10... | collective-permute-start | bytes 6291464 | tf_op jit(solution)/shard_map/ppermute | solution.py:476
  36.3 0.8 copy-start.12
  48.9 27.7 %collective-permute-start.9 = (bf16[544,1024]{1,0:T(8,128)(2,1)}, bf16[544,1024]{1,0:T(8,128)(2,1)}, u32[]{:S(2)}, u32[]{:S(2)}) collective-permute-start(bf16[544,1024]{1,0:T(8,128)(2,1)} %get-tuple-element.18.refs_7_.refs_1_.refs_3_.refs_9_), channel_id=1, source_target_pairs={{8,24},{16,0},{9,25},{17,1},{10,26},{18,2},{11,27},{19,3},{12,28},... | collective-permute-start | bytes 3342344 | tf_op jit(solution)/shard_map/ppermute | solution.py:478
  54.4 0.9 copy-start.2
  55.2 0.8 copy-start.10
  67.8 2.4 %copy-start = (bf16[544,1024]{1,0:T(8,128)(2,1)S(1)}, bf16[544,1024]{1,0:T(8,128)(2,1)}, u32[]{:S(2)}) copy-start(bf16[544,1024]{1,0:T(8,128)(2,1)} %get-tuple-element.19.refs_1_.refs_5_.refs_7_.refs_11_) | copy-start | bytes 3342340
  67.8 10.3 %copy-start.6 = (bf16[384,1024]{1,0:T(8,128)(2,1)S(1)}, bf16[384,1024]{1,0:T(8,128)(2,1)}, u32[]{:S(2)}) copy-start(bf16[384,1024]{1,0:T(8,128)(2,1)} %get-tuple-element.21.refs_5_) | copy-start | bytes 2359300
  67.8 22.0 %collective-permute-start.6 = (bf16[384,1024]{1,0:T(8,128)(2,1)}, bf16[384,1024]{1,0:T(8,128)(2,1)}, u32[]{:S(2)}, u32[]{:S(2)}) collective-permute-start(bf16[384,1024]{1,0:T(8,128)(2,1)} %shard_map.83), channel_id=1, source_target_pairs={{8,24},{16,0},{9,25},{17,1},{10,26},{18,2},{11,27},{19,3},{12,28},... | collective-permute-start | bytes 2359304 | tf_op jit(solution)/shard_map/ppermute | solution.py:490
  70.2 43.0 %collective-permute-start.5 = (bf16[544,1024]{1,0:T(8,128)(2,1)S(1)}, bf16[544,1024]{1,0:T(8,128)(2,1)S(1)}, u32[]{:S(2)}, u32[]{:S(2)}) collective-permute-start(bf16[544,1024]{1,0:T(8,128)(2,1)S(1)} %copy-done), channel_id=1, source_target_pairs={{8,16},{16,8},{9,17},{17,9},{10,18},{18,10},{11,19},{19,11},{12,20... | collective-permute-start | bytes 3342344 | tf_op jit(solution)/shard_map/ppermute | solution.py:489
  76.6 36.7 %collective-permute-start.10 = (bf16[544,1024]{1,0:T(8,128)(2,1)}, bf16[544,1024]{1,0:T(8,128)(2,1)}, u32[]{:S(2)}, u32[]{:S(2)}) collective-permute-start(bf16[544,1024]{1,0:T(8,128)(2,1)} %shard_map.86), channel_id=1, source_target_pairs={{24,16},{0,8},{25,17},{1,9},{26,18},{2,10},{27,19},{3,11},{28,20},... | collective-permute-start | bytes 3342344 | tf_op jit(solution)/shard_map/ppermute | solution.py:492
  79.0 16.5 %copy-start.3 = (bf16[320,1024]{1,0:T(8,128)(2,1)S(1)}, bf16[320,1024]{1,0:T(8,128)(2,1)}, u32[]{:S(2)}) copy-start(bf16[320,1024]{1,0:T(8,128)(2,1)} %copy-done.2) | copy-start | bytes 1966084
  79.0 16.5 %copy-start.9 = (bf16[128,2048]{1,0:T(8,128)(2,1)S(1)}, bf16[128,2048]{1,0:T(8,128)(2,1)}, u32[]{:S(2)}) copy-start(bf16[128,2048]{1,0:T(8,128)(2,1)} %copy-done.8) | copy-start | bytes 1572868
  89.8 23.6 %copy-start.1 = (bf16[544,1024]{1,0:T(8,128)(2,1)S(1)}, bf16[544,1024]{1,0:T(8,128)(2,1)}, u32[]{:S(2)}) copy-start(bf16[544,1024]{1,0:T(8,128)(2,1)} %get-tuple-element.19.refs_1_.refs_5_.refs_7_.refs_11_) | copy-start | bytes 3342340
  89.8 23.6 %copy-start.4 = (bf16[544,1024]{1,0:T(8,128)(2,1)S(1)}, bf16[544,1024]{1,0:T(8,128)(2,1)}, u32[]{:S(2)}) copy-start(bf16[544,1024]{1,0:T(8,128)(2,1)} %get-tuple-element.18.refs_7_.refs_1_.refs_3_.refs_9_) | copy-start | bytes 3342340
  89.8 39.2 %collective-permute-start.7 = (bf16[384,1024]{1,0:T(8,128)(2,1)}, bf16[384,1024]{1,0:T(8,128)(2,1)S(1)}, u32[]{:S(2)}, u32[]{:S(2)}) collective-permute-start(bf16[384,1024]{1,0:T(8,128)(2,1)} %shard_map.84), channel_id=1, source_target_pairs={{24,16},{0,8},{25,17},{1,9},{26,18},{2,10},{27,19},{3,11},{28,20},... | collective-permute-start | bytes 2359304 | tf_op jit(solution)/shard_map/ppermute | solution.py:493
  91.2 37.8 %collective-permute-start.8 = (bf16[384,1024]{1,0:T(8,128)(2,1)}, bf16[384,1024]{1,0:T(8,128)(2,1)S(1)}, u32[]{:S(2)}, u32[]{:S(2)}) collective-permute-start(bf16[384,1024]{1,0:T(8,128)(2,1)} %shard_map.85), channel_id=1, source_target_pairs={{8,16},{16,8},{9,17},{17,9},{10,18},{18,10},{11,19},{19,11},{12,20... | collective-permute-start | bytes 2359304 | tf_op jit(solution)/shard_map/ppermute | solution.py:491
  95.5 1.0 copy-start.11
  113.4 15.6 %copy-start.5 = (bf16[384,1024]{1,0:T(8,128)(2,1)S(1)}, bf16[384,1024]{1,0:T(8,128)(2,1)}, u32[]{:S(2)}) copy-start(bf16[384,1024]{1,0:T(8,128)(2,1)} %get-tuple-element.20.refs_3_) | copy-start | bytes 2359300
  113.4 15.6 %copy-start.7 = (bf16[384,1024]{1,0:T(8,128)(2,1)S(1)}, bf16[384,1024]{1,0:T(8,128)(2,1)}, u32[]{:S(2)}) copy-start(bf16[384,1024]{1,0:T(8,128)(2,1)} %get-tuple-element.21.refs_5_) | copy-start | bytes 2359300

commit v5 on v4

--- a/solution.py
+++ b/solution.py
@@ -150,7 +150,9 @@
 
     if corner:
         all_ready()
-    if pack:
+    pack_stores = []
+
+    def store_pack():
         for each in range(2):
             at = lax.broadcasted_iota(jnp.int32, (INFO, REACH), 0)
             numbers = jnp.zeros((INFO, REACH), jnp.int32)
@@ -164,7 +166,11 @@
             packed[each, 1, REACH:, :] = jnp.zeros((INFO, keys.shape[2]), jnp.bfloat16)
         for copy in pack_copies:
             copy.wait()
-        pack_stores = [start(packed.at[path], pack_outs[0]), start(packed.at[1 - path], pack_outs[1])]
+        pack_stores.append(start(packed.at[path], pack_outs[0]))
+        pack_stores.append(start(packed.at[1 - path], pack_outs[1]))
+
+    if pack and not last:
+        store_pack()
 
     def column(row):
         return jnp.transpose(jnp.broadcast_to(row, (BLK, BLK)))
@@ -247,7 +253,9 @@
             copy.wait()
             last_out[:, place] = mixture(last_q[:, place], kbuf[window, lanes], vbuf[window, lanes])
             stores.append(start(last_out.at[:, place], outs[0].at[:, place]))
-        for copy in stores:
+            if pack and at == 0:
+                store_pack()
+        for copy in stores + pack_stores:
             copy.wait()
         return
 
@@ -277,9 +285,8 @@
     if corner:
         for copy in corner_stores:
             copy.wait()
-    if pack:
-        for copy in pack_stores:
-            copy.wait()
+    for copy in pack_stores:
+        copy.wait()
 
 
 def attend(payload, groups, items, operands, after=(), halo=None, corner=False, pack=False, last=False, weight=0):
@@ -302,7 +309,7 @@
         pltpu.VMEM((1, REACH + rows), jnp.int32),
         pltpu.SMEM(lengths.shape, jnp.int32),
         pltpu.SMEM((count + 1,), jnp.int32),
-        pltpu.SemaphoreType.DMA((16,)),
+        pltpu.SemaphoreType.DMA((20,)),
     ]
     if halo is not None:
         scratch.append(pltpu.VMEM((INFO, keys.shape[2]), jnp.bfloat16))
@@ -450,6 +457,7 @@
 
 
 PLACE_WEIGHT = 0
+SWAP_WEIGHT = 2000
 DIRECT_WEIGHT = 100000
 
 SWAP = [(0, 1), (1, 0), (2, 3), (3, 2)]
@@ -464,15 +472,15 @@
     ring = [(source, source + 1) for source in range(lax.axis_size("dp") - 1)]
     every = tuple(range(KV_HEADS))
 
-    (swap_0,) = attend(0, ((0, 1),), (2,), operands, last=True)
+    (swap_0,) = attend(0, ((0,),), (2,), operands, last=True)
     got_0 = lax.ppermute(swap_0, "pipe", SWAP)
-    corner, halo, far_halo = attend(0, (every,), (), operands, after=(swap_0,), corner=True, pack=True)
-    got_corner = lax.ppermute(corner, "pipe", SWAP)
+    swap_1, halo, far_halo = attend(0, ((1, 2, 3),), (2,), operands, after=(swap_0,), pack=True, last=True)
+    got_1 = lax.ppermute(swap_1, "pipe", SWAP)
     halo = lax.ppermute(halo, "dp", ring)
     far_halo = lax.ppermute(far_halo, "dp", ring)
-    (swap_1,) = attend(0, ((2, 3),), (2,), operands, after=(corner, got_0), last=True)
-    got_1 = lax.ppermute(swap_1, "pipe", SWAP)
-    (swap_2,) = attend(0, (every,), (0, 1), operands, after=(swap_1,), halo=halo)
+    (corner,) = attend(0, (every,), (), operands, after=(swap_1, got_0), corner=True)
+    got_corner = lax.ppermute(corner, "pipe", SWAP)
+    (swap_2,) = attend(0, (every,), (0, 1), operands, after=(corner,), halo=halo, weight=SWAP_WEIGHT)
     got_2 = lax.ppermute(swap_2, "pipe", SWAP)
     routed_1, routed_2 = attend(1, ((0,), (1,)), (0, 1, 2), operands, after=(swap_2,), halo=far_halo, corner=True)
     across_1 = lax.ppermute(routed_1, "pipe", ACROSS)
@@ -494,8 +502,8 @@
     outs = place(
         [("corner", (got_corner,), True, (head,), (), head * CORNER) for head in every]
         + [
-            ("plain", (got_0,), True, (0, 1), (2,), 0),
-            ("plain", (got_1,), True, (2, 3), (2,), 0),
+            ("plain", (got_0,), True, (0,), (2,), 0),
+            ("plain", (got_1,), True, (1, 2, 3), (2,), 0),
             ("plain", (got_2,), True, every, (0, 1), 0),
         ],
         rows,

time: 133 us -> 132 us (level)
    ppermute x1, waiting for transfers between devices: 10.8 us -> 14.1 us  [on_device(): across_2 = lax.ppermute(behind(routed_2, direct_1), 'pipe', ACROSS)]
    ppermute x1, waiting for transfers between devices: 2.38 us -> 0.01 us  [on_device(): got_0 = lax.ppermute(swap_0, 'pipe', SWAP)]
    ppermute x1, starting transfers between devices: 0.6 us -> 2.26 us  [on_device(): got_corner = lax.ppermute(corner, 'pipe', SWAP)]
    ppermute x1, waiting for transfers between devices: 11.2 us -> 9.58 us  [on_device(): diagonal_1 = lax.ppermute(direct_1, 'pipe', DIAGONAL)]
    unnamed x30 -> x32, local copies, waits for them, and re-layouts: 8.09 us -> 8.24 us
  transfers between devices with their start and end apart: 12 -> 12, of which waited for: 6 -> 5; matrix products, arithmetic and copies ran while one was open for 2% -> 2% of each run, Pallas kernels for 40% -> 40%
where the time goes in v5:
time: 132 us; the launch traced here: 130 us
  Pallas kernels  56.9 us (43%)
  waiting for transfers between devices  36.5 us (28%)
  starting transfers between devices  27.3 us (21%)
  local copies, waits for them, and re-layouts  8.24 us (6%)
    pallas_call x6, Pallas kernels, attend(): pl.pallas_call(kernel, out_shape=out_shape, in_specs=[HBM] * 6 + [ANY] *...  45.5 us
    ppermute x1, waiting for transfers between devices, on_device(): across_2 = lax.ppermute(behind(routed_2, direct_1), 'pipe', ACROSS)  14.1 us
    pallas_call x3, Pallas kernels, place(): pl.pallas_call(functools.partial(place_kernel, [(piece[0],) + piece[2:] f...  11.4 us
    ppermute x1, waiting for transfers between devices, on_device(): onward_2 = lax.ppermute(behind(across_2, direct_1), 'pipe', ONWARD)  10.9 us
    ppermute x1, waiting for transfers between devices, on_device(): diagonal_1 = lax.ppermute(direct_1, 'pipe', DIAGONAL)  9.58 us
    unnamed x32, local copies, waits for them, and re-layouts  8.24 us
    ppermute x1, starting transfers between devices, on_device(): diagonal_2 = lax.ppermute(behind(direct_2, across_2), 'pipe', DIAGONAL)  4.57 us
    ppermute x1, starting transfers between devices, on_device(): diagonal_1 = lax.ppermute(direct_1, 'pipe', DIAGONAL)  4.35 us
  transfers between devices with their start and end apart: 12, of which 5 were waited for; matrix products, arithmetic and copies ran while one was open for 2% of the time, Pallas kernels for 40%

profile of v5, /device:TPU:20, one launch (start us, length us, event | category | flops | bytes accessed | tf_op | source)
XLA Modules:
  0.0 130.0 jit_solution(4474801113243491582)
XLA Ops:
  0.6 2.6 %shard_map.77.refs_6_ = bf16[128,1024]{1,0:T(8,128)(2,1)} custom-call(s32[2,32]{1,0:T(2,128)} %bitcast.40, bf16[2,512,4096]{2,1,0:T(8,128)(2,1)} %bitcast.8, bf16[2,512,512]{2,1,0:T(8,128)(2,1)} %bitcast.14, bf16[2,512,512]{2,1,0:T(8,128)(2,1)} %bitcast.20, s32[2,512]{1,0:T(2,128)} %bitcast.28, s32[2,512]{1,0:T(2,128)} %bitcast.34), custom_call_target="tpu_custom_call" | custom-call | flops 1024 | bytes 1024 | tf_op jit(solution)/shard_map/pallas_call | solution.py:331
  3.3 1.6 %collective-permute-start.2 = (bf16[128,1024]{1,0:T(8,128)(2,1)}, bf16[128,1024]{1,0:T(8,128)(2,1)S(1)}, u32[]{:S(2)}, u32[]{:S(2)}) collective-permute-start(bf16[128,1024]{1,0:T(8,128)(2,1)} %shard_map.77.refs_6_), channel_id=1, source_target_pairs={{0,8},{8,0},{16,24},{24,16},{1,9},{9,1},{17,25},{25,17},{2,10},{10... | collective-permute-start | bytes 786440 | tf_op jit(solution)/shard_map/ppermute | solution.py:476
  4.8 4.3 %shard_map.78 = (bf16[128,3072]{1,0:T(8,128)(2,1)}, bf16[2,272,512]{2,1,0:T(8,128)(2,1)}, bf16[2,272,512]{2,1,0:T(8,128)(2,1)}) custom-call(s32[2,32]{1,0:T(2,128)} %bitcast.41, bf16[2,512,4096]{2,1,0:T(8,128)(2,1)} %bitcast.9, bf16[2,512,512]{2,1,0:T(8,128)(2,1)} %bitcast.15, bf16[2,512,512]{2,1,0:T(8,128)(2,1)} %bitcast.21, s32[2,512]{1,0:T(2,128)} %bitcast.29, ...), custom_call_target="tpu_custom_call" | custom-call | flops 1024 | bytes 1024 | tf_op jit(solution)/shard_map/pallas_call | solution.py:331
  9.8 2.0 %collective-permute-start.1 = (bf16[2,272,512]{2,1,0:T(8,128)(2,1)}, bf16[2,272,512]{2,1,0:T(8,128)(2,1)S(1)}, u32[]{:S(2)}, u32[]{:S(2)}) collective-permute-start(bf16[2,272,512]{2,1,0:T(8,128)(2,1)} %get-tuple-element.16), channel_id=1, source_target_pairs={{0,1},{1,2},{2,3},{3,4},{4,5},{5,6},{6,7},{8,9},{9,10},{10,11},{11... | collective-permute-start | bytes 1671176 | tf_op jit(solution)/shard_map/ppermute | solution.py:479
  11.8 0.7 copy-done.8
  12.5 5.0 %shard_map.79.refs_7_ = bf16[320,1024]{1,0:T(8,128)(2,1)} custom-call(s32[2,32]{1,0:T(2,128)} %bitcast.42, bf16[2,512,4096]{2,1,0:T(8,128)(2,1)} %bitcast.10, bf16[2,512,512]{2,1,0:T(8,128)(2,1)} %bitcast.16, bf16[2,512,512]{2,1,0:T(8,128)(2,1)} %bitcast.22, s32[2,512]{1,0:T(2,128)} %bitcast.30, s32[2,512]{1,0:T(2,128)} %bitcast.36, ...), custom_call_target="tpu_custom_call" | custom-call | flops 1024 | bytes 1024 | tf_op jit(solution)/shard_map/pallas_call | solution.py:331
  17.6 2.3 %collective-permute-start.4 = (bf16[320,1024]{1,0:T(8,128)(2,1)}, bf16[320,1024]{1,0:T(8,128)(2,1)S(1)}, u32[]{:S(2)}, u32[]{:S(2)}) collective-permute-start(bf16[320,1024]{1,0:T(8,128)(2,1)} %shard_map.79.refs_7_), channel_id=1, source_target_pairs={{0,8},{8,0},{16,24},{24,16},{1,9},{9,1},{17,25},{25,17},{2,10},{10... | collective-permute-start | bytes 1966088 | tf_op jit(solution)/shard_map/ppermute | solution.py:482
  19.8 2.6 %collective-permute-start = (bf16[2,272,512]{2,1,0:T(8,128)(2,1)S(1)}, bf16[2,272,512]{2,1,0:T(8,128)(2,1)S(1)}, u32[]{:S(2)}, u32[]{:S(2)}) collective-permute-start(bf16[2,272,512]{2,1,0:T(8,128)(2,1)S(1)} %copy-done.14), channel_id=1, source_target_pairs={{0,1},{1,2},{2,3},{3,4},{4,5},{5,6},{6,7},{8,9},{9,10},{10,11},{11... | collective-permute-start | bytes 1671176 | tf_op jit(solution)/shard_map/ppermute | solution.py:480
  22.4 0.8 copy-done.13
  23.2 10.0 %shard_map.80.refs_7_ = bf16[256,4096]{1,0:T(8,128)(2,1)} custom-call(s32[2,32]{1,0:T(2,128)} %bitcast.43, bf16[2,512,4096]{2,1,0:T(8,128)(2,1)} %bitcast.11, bf16[2,512,512]{2,1,0:T(8,128)(2,1)} %bitcast.17, bf16[2,512,512]{2,1,0:T(8,128)(2,1)} %bitcast.23, s32[2,512]{1,0:T(2,128)} %bitcast.31, s32[2,512]{1,0:T(2,128)} %bitcast.37, ...), custom_call_target="tpu_custom_call" | custom-call | flops 2000001024 | bytes 1024 | tf_op jit(solution)/shard_map/pallas_call | solution.py:331
  33.2 0.6 collective-permute-start.11
  33.8 0.8 copy-done.12
  34.7 11.7 %shard_map.81 = (bf16[544,1024]{1,0:T(8,128)(2,1)}, bf16[384,1024]{1,0:T(8,128)(2,1)}) custom-call(s32[2,32]{1,0:T(2,128)} %bitcast.44, bf16[2,512,4096]{2,1,0:T(8,128)(2,1)} %bitcast.12, bf16[2,512,512]{2,1,0:T(8,128)(2,1)} %bitcast.18, bf16[2,512,512]{2,1,0:T(8,128)(2,1)} %bitcast.24, s32[2,512]{1,0:T(2,128)} %bitcast.32, s32[2,512]{1,0:T(2,128)} %bitcast.38, ...), custom_call_target="tpu_custom_call" | custom-call | flops 1024 | bytes 1024 | tf_op jit(solution)/shard_map/pallas_call | solution.py:331
  46.4 3.4 %collective-permute-start.9 = (bf16[544,1024]{1,0:T(8,128)(2,1)}, bf16[544,1024]{1,0:T(8,128)(2,1)}, u32[]{:S(2)}, u32[]{:S(2)}) collective-permute-start(bf16[544,1024]{1,0:T(8,128)(2,1)} %get-tuple-element.18.refs_7_.refs_1_.refs_3_.refs_9_), channel_id=1, source_target_pairs={{8,24},{16,0},{9,25},{17,1},{10,26},{18,2},{11,27},{19,3},{12,28},... | collective-permute-start | bytes 3342344 | tf_op jit(solution)/shard_map/ppermute | solution.py:486
  49.8 2.1 %copy.16.refs_0_ = bf16[384,1024]{1,0:T(8,128)(2,1)} copy(bf16[384,1024]{1,0:T(8,128)(2,1)} %get-tuple-element.20.refs_3_) | data formatting | bytes 1572864
  51.9 0.9 copy-done.10
  52.8 0.9 copy-done.2
  53.7 11.8 %shard_map.82 = (bf16[544,1024]{1,0:T(8,128)(2,1)}, bf16[384,1024]{1,0:T(8,128)(2,1)}) custom-call(s32[2,32]{1,0:T(2,128)} %bitcast.45, bf16[2,512,4096]{2,1,0:T(8,128)(2,1)} %bitcast.13, bf16[2,512,512]{2,1,0:T(8,128)(2,1)} %bitcast.19, bf16[2,512,512]{2,1,0:T(8,128)(2,1)} %bitcast.25, s32[2,512]{1,0:T(2,128)} %bitcast.33, s32[2,512]{1,0:T(2,128)} %bitcast.39, ...), custom_call_target="tpu_custom_call" | custom-call | flops 99999997952 | bytes 1024 | tf_op jit(solution)/shard_map/pallas_call | solution.py:331
  65.5 2.4 %collective-permute-start.6 = (bf16[384,1024]{1,0:T(8,128)(2,1)}, bf16[384,1024]{1,0:T(8,128)(2,1)}, u32[]{:S(2)}, u32[]{:S(2)}) collective-permute-start(bf16[384,1024]{1,0:T(8,128)(2,1)} %shard_map.83), channel_id=1, source_target_pairs={{8,24},{16,0},{9,25},{17,1},{10,26},{18,2},{11,27},{19,3},{12,28},... | collective-permute-start | bytes 2359304 | tf_op jit(solution)/shard_map/ppermute | solution.py:498
  67.9 4.4 %collective-permute-start.5 = (bf16[544,1024]{1,0:T(8,128)(2,1)S(1)}, bf16[544,1024]{1,0:T(8,128)(2,1)S(1)}, u32[]{:S(2)}, u32[]{:S(2)}) collective-permute-start(bf16[544,1024]{1,0:T(8,128)(2,1)S(1)} %copy-done), channel_id=1, source_target_pairs={{8,16},{16,8},{9,17},{17,9},{10,18},{18,10},{11,19},{19,11},{12,20... | collective-permute-start | bytes 3342344 | tf_op jit(solution)/shard_map/ppermute | solution.py:497
  72.2 1.8 %collective-permute-done.9.refs_0_ = bf16[544,1024]{1,0:T(8,128)(2,1)} collective-permute-done((bf16[544,1024]{1,0:T(8,128)(2,1)}, bf16[544,1024]{1,0:T(8,128)(2,1)}, u32[]{:S(2)}, u32[]{:S(2)}) %collective-permute-start.9) | collective-permute-done | bytes 1114144 | tf_op jit(solution)/shard_map/ppermute | solution.py:486
  74.0 1.5 %collective-permute-start.10 = (bf16[544,1024]{1,0:T(8,128)(2,1)}, bf16[544,1024]{1,0:T(8,128)(2,1)}, u32[]{:S(2)}, u32[]{:S(2)}) collective-permute-start(bf16[544,1024]{1,0:T(8,128)(2,1)} %shard_map.86), channel_id=1, source_target_pairs={{24,16},{0,8},{25,17},{1,9},{26,18},{2,10},{27,19},{3,11},{28,20},... | collective-permute-start | bytes 3342344 | tf_op jit(solution)/shard_map/ppermute | solution.py:500
  75.5 0.9 copy.18.refs_0_
  76.4 14.1 %collective-permute-done.6.refs_0_.refs_1_ = bf16[384,1024]{1,0:T(8,128)(2,1)} collective-permute-done((bf16[384,1024]{1,0:T(8,128)(2,1)}, bf16[384,1024]{1,0:T(8,128)(2,1)}, u32[]{:S(2)}, u32[]{:S(2)}) %collective-permute-start.6) | collective-permute-done | bytes 786464 | tf_op jit(solution)/shard_map/ppermute | solution.py:498
  90.5 1.4 %collective-permute-start.7 = (bf16[384,1024]{1,0:T(8,128)(2,1)}, bf16[384,1024]{1,0:T(8,128)(2,1)S(1)}, u32[]{:S(2)}, u32[]{:S(2)}) collective-permute-start(bf16[384,1024]{1,0:T(8,128)(2,1)} %shard_map.84), channel_id=1, source_target_pairs={{24,16},{0,8},{25,17},{1,9},{26,18},{2,10},{27,19},{3,11},{28,20},... | collective-permute-start | bytes 2359304 | tf_op jit(solution)/shard_map/ppermute | solution.py:501
  91.9 4.6 %collective-permute-start.8 = (bf16[384,1024]{1,0:T(8,128)(2,1)}, bf16[384,1024]{1,0:T(8,128)(2,1)S(1)}, u32[]{:S(2)}, u32[]{:S(2)}) collective-permute-start(bf16[384,1024]{1,0:T(8,128)(2,1)} %shard_map.85), channel_id=1, source_target_pairs={{8,16},{16,8},{9,17},{17,9},{10,18},{18,10},{11,19},{19,11},{12,20... | collective-permute-start | bytes 2359304 | tf_op jit(solution)/shard_map/ppermute | solution.py:499
  96.5 1.1 copy-done.11
  97.6 5.5 %shard_map.87 = (bf16[512,4096]{1,0:T(8,128)(2,1)}, bf16[512,4096]{1,0:T(8,128)(2,1)}) custom-call(bf16[320,1024]{1,0:T(8,128)(2,1)S(1)} %copy-done.3, bf16[320,1024]{1,0:T(8,128)(2,1)S(1)} %copy-done.3, bf16[320,1024]{1,0:T(8,128)(2,1)S(1)} %copy-done.3, bf16[320,1024]{1,0:T(8,128)(2,1)S(1)} %copy-done.3, bf16[128,1024]{1,0:T(8,128)(2,1)S(1)} %copy-done.9, ...), custom_call_target="tpu_custom_call" | custom-call | flops 1024 | bytes 1024 | tf_op jit(solution)/shard_map/pallas_call | solution.py:442
  103.1 9.6 %collective-permute-done.5.refs_4_.refs_6_.refs_10_.refs_0_ = bf16[544,1024]{1,0:T(8,128)(2,1)S(1)} collective-permute-done((bf16[544,1024]{1,0:T(8,128)(2,1)S(1)}, bf16[544,1024]{1,0:T(8,128)(2,1)S(1)}, u32[]{:S(2)}, u32[]{:S(2)}) %collective-permute-start.5) | collective-permute-done | bytes 1114144 | tf_op jit(solution)/shard_map/ppermute | solution.py:497
  112.9 4.4 %shard_map.88 = (bf16[512,4096]{1,0:T(8,128)(2,1)}, bf16[512,4096]{1,0:T(8,128)(2,1)}) custom-call(bf16[544,1024]{1,0:T(8,128)(2,1)} %collective-permute-done.10.refs_0_.refs_2_.refs_8_, bf16[544,1024]{1,0:T(8,128)(2,1)S(1)} %copy-done.4, ...), custom_call_target="tpu_custom_call", output_to_operand_aliasing={{0}: (12, {}), {1}: (13, {})} | custom-call | flops 1024 | bytes 1024 | tf_op jit(solution)/shard_map/pallas_call | solution.py:442
  117.2 10.9 %collective-permute-done.7.refs_2_ = bf16[384,1024]{1,0:T(8,128)(2,1)S(1)} collective-permute-done((bf16[384,1024]{1,0:T(8,128)(2,1)}, bf16[384,1024]{1,0:T(8,128)(2,1)S(1)}, u32[]{:S(2)}, u32[]{:S(2)}) %collective-permute-start.7) | collective-permute-done | bytes 786464 | tf_op jit(solution)/shard_map/ppermute | solution.py:501
  128.2 1.6 %shard_map.89 = (bf16[512,4096]{1,0:T(8,128)(2,1)}, bf16[512,4096]{1,0:T(8,128)(2,1)}) custom-call(bf16[544,1024]{1,0:T(8,128)(2,1)S(1)} %collective-permute-done.5.refs_4_.refs_6_.refs_10_.refs_0_, bf16[544,1024]{1,0:T(8,128)(2,1)S(1)} %copy-done.1, ...), custom_call_target="tpu_custom_call", output_to_operand_aliasing={{0}: (6, {}), {1}: (7, {})} | custom-call | flops 1024 | bytes 1024 | tf_op jit(solution)/shard_map/pallas_call | solution.py:442
  (37 shorter events, 0.8 us)
Async XLA Ops:
  3.3 8.5 %collective-permute-start.2 = (bf16[128,1024]{1,0:T(8,128)(2,1)}, bf16[128,1024]{1,0:T(8,128)(2,1)S(1)}, u32[]{:S(2)}, u32[]{:S(2)}) collective-permute-start(bf16[128,1024]{1,0:T(8,128)(2,1)} %shard_map.77.refs_6_), channel_id=1, source_target_pairs={{0,8},{8,0},{16,24},{24,16},{1,9},{9,1},{17,25},{25,17},{2,10},{10... | collective-permute-start | bytes 786440 | tf_op jit(solution)/shard_map/ppermute | solution.py:476
  9.1 42.8 %collective-permute-start.3 = (bf16[128,3072]{1,0:T(8,128)(2,1)}, bf16[128,3072]{1,0:T(8,128)(2,1)S(1)}, u32[]{:S(2)}, u32[]{:S(2)}) collective-permute-start(bf16[128,3072]{1,0:T(8,128)(2,1)} %get-tuple-element.17.refs_6_), channel_id=1, source_target_pairs={{0,8},{8,0},{16,24},{24,16},{1,9},{9,1},{17,25},{25,17},{2,10},{10... | collective-permute-start | bytes 2359304 | tf_op jit(solution)/shard_map/ppermute | solution.py:478
  9.8 10.1 %copy-start.14 = (bf16[2,272,512]{2,1,0:T(8,128)(2,1)S(1)}, bf16[2,272,512]{2,1,0:T(8,128)(2,1)}, u32[]{:S(2)}) copy-start(bf16[2,272,512]{2,1,0:T(8,128)(2,1)} %get-tuple-element.15) | copy-start | bytes 1671172
  9.8 12.7 %collective-permute-start.1 = (bf16[2,272,512]{2,1,0:T(8,128)(2,1)}, bf16[2,272,512]{2,1,0:T(8,128)(2,1)S(1)}, u32[]{:S(2)}, u32[]{:S(2)}) collective-permute-start(bf16[2,272,512]{2,1,0:T(8,128)(2,1)} %get-tuple-element.16), channel_id=1, source_target_pairs={{0,1},{1,2},{2,3},{3,4},{4,5},{5,6},{6,7},{8,9},{9,10},{10,11},{11... | collective-permute-start | bytes 1671176 | tf_op jit(solution)/shard_map/ppermute | solution.py:479
  11.8 0.7 copy-start.8
  17.6 34.4 %collective-permute-start.4 = (bf16[320,1024]{1,0:T(8,128)(2,1)}, bf16[320,1024]{1,0:T(8,128)(2,1)S(1)}, u32[]{:S(2)}, u32[]{:S(2)}) collective-permute-start(bf16[320,1024]{1,0:T(8,128)(2,1)} %shard_map.79.refs_7_), channel_id=1, source_target_pairs={{0,8},{8,0},{16,24},{24,16},{1,9},{9,1},{17,25},{25,17},{2,10},{10... | collective-permute-start | bytes 1966088 | tf_op jit(solution)/shard_map/ppermute | solution.py:482
  19.8 14.0 %collective-permute-start = (bf16[2,272,512]{2,1,0:T(8,128)(2,1)S(1)}, bf16[2,272,512]{2,1,0:T(8,128)(2,1)S(1)}, u32[]{:S(2)}, u32[]{:S(2)}) collective-permute-start(bf16[2,272,512]{2,1,0:T(8,128)(2,1)S(1)} %copy-done.14), channel_id=1, source_target_pairs={{0,1},{1,2},{2,3},{3,4},{4,5},{5,6},{6,7},{8,9},{9,10},{10,11},{11... | collective-permute-start | bytes 1671176 | tf_op jit(solution)/shard_map/ppermute | solution.py:480
  22.4 0.8 copy-start.13
  33.2 63.3 %collective-permute-start.11 = (bf16[256,4096]{1,0:T(8,128)(2,1)}, bf16[256,4096]{1,0:T(8,128)(2,1)}, u32[]{:S(2)}, u32[]{:S(2)}) collective-permute-start(bf16[256,4096]{1,0:T(8,128)(2,1)} %shard_map.80.refs_7_), channel_id=1, source_target_pairs={{0,8},{8,0},{16,24},{24,16},{1,9},{9,1},{17,25},{25,17},{2,10},{10... | collective-permute-start | bytes 6291464 | tf_op jit(solution)/shard_map/ppermute | solution.py:484
  33.8 0.8 copy-start.12
  46.4 27.6 %collective-permute-start.9 = (bf16[544,1024]{1,0:T(8,128)(2,1)}, bf16[544,1024]{1,0:T(8,128)(2,1)}, u32[]{:S(2)}, u32[]{:S(2)}) collective-permute-start(bf16[544,1024]{1,0:T(8,128)(2,1)} %get-tuple-element.18.refs_7_.refs_1_.refs_3_.refs_9_), channel_id=1, source_target_pairs={{8,24},{16,0},{9,25},{17,1},{10,26},{18,2},{11,27},{19,3},{12,28},... | collective-permute-start | bytes 3342344 | tf_op jit(solution)/shard_map/ppermute | solution.py:486
  51.9 0.9 copy-start.10
  52.8 0.9 copy-start.2
  65.4 2.4 %copy-start = (bf16[544,1024]{1,0:T(8,128)(2,1)S(1)}, bf16[544,1024]{1,0:T(8,128)(2,1)}, u32[]{:S(2)}) copy-start(bf16[544,1024]{1,0:T(8,128)(2,1)} %get-tuple-element.19.refs_1_.refs_5_.refs_7_.refs_11_) | copy-start | bytes 3342340
  65.5 10.0 %copy-start.6 = (bf16[384,1024]{1,0:T(8,128)(2,1)S(1)}, bf16[384,1024]{1,0:T(8,128)(2,1)}, u32[]{:S(2)}) copy-start(bf16[384,1024]{1,0:T(8,128)(2,1)} %get-tuple-element.21.refs_5_) | copy-start | bytes 2359300
  65.5 25.0 %collective-permute-start.6 = (bf16[384,1024]{1,0:T(8,128)(2,1)}, bf16[384,1024]{1,0:T(8,128)(2,1)}, u32[]{:S(2)}, u32[]{:S(2)}) collective-permute-start(bf16[384,1024]{1,0:T(8,128)(2,1)} %shard_map.83), channel_id=1, source_target_pairs={{8,24},{16,0},{9,25},{17,1},{10,26},{18,2},{11,27},{19,3},{12,28},... | collective-permute-start | bytes 2359304 | tf_op jit(solution)/shard_map/ppermute | solution.py:498
  67.9 44.8 %collective-permute-start.5 = (bf16[544,1024]{1,0:T(8,128)(2,1)S(1)}, bf16[544,1024]{1,0:T(8,128)(2,1)S(1)}, u32[]{:S(2)}, u32[]{:S(2)}) collective-permute-start(bf16[544,1024]{1,0:T(8,128)(2,1)S(1)} %copy-done), channel_id=1, source_target_pairs={{8,16},{16,8},{9,17},{17,9},{10,18},{18,10},{11,19},{19,11},{12,20... | collective-permute-start | bytes 3342344 | tf_op jit(solution)/shard_map/ppermute | solution.py:497
  74.0 38.9 %collective-permute-start.10 = (bf16[544,1024]{1,0:T(8,128)(2,1)}, bf16[544,1024]{1,0:T(8,128)(2,1)}, u32[]{:S(2)}, u32[]{:S(2)}) collective-permute-start(bf16[544,1024]{1,0:T(8,128)(2,1)} %shard_map.86), channel_id=1, source_target_pairs={{24,16},{0,8},{25,17},{1,9},{26,18},{2,10},{27,19},{3,11},{28,20},... | collective-permute-start | bytes 3342344 | tf_op jit(solution)/shard_map/ppermute | solution.py:500
  76.4 20.1 %copy-start.3 = (bf16[320,1024]{1,0:T(8,128)(2,1)S(1)}, bf16[320,1024]{1,0:T(8,128)(2,1)}, u32[]{:S(2)}) copy-start(bf16[320,1024]{1,0:T(8,128)(2,1)} %copy-done.2) | copy-start | bytes 1966084
  76.4 20.1 %copy-start.9 = (bf16[128,1024]{1,0:T(8,128)(2,1)S(1)}, bf16[128,1024]{1,0:T(8,128)(2,1)}, u32[]{:S(2)}) copy-start(bf16[128,1024]{1,0:T(8,128)(2,1)} %copy-done.8) | copy-start | bytes 786436
  90.5 22.4 %copy-start.1 = (bf16[544,1024]{1,0:T(8,128)(2,1)S(1)}, bf16[544,1024]{1,0:T(8,128)(2,1)}, u32[]{:S(2)}) copy-start(bf16[544,1024]{1,0:T(8,128)(2,1)} %get-tuple-element.19.refs_1_.refs_5_.refs_7_.refs_11_) | copy-start | bytes 3342340
  90.5 22.4 %copy-start.4 = (bf16[544,1024]{1,0:T(8,128)(2,1)S(1)}, bf16[544,1024]{1,0:T(8,128)(2,1)}, u32[]{:S(2)}) copy-start(bf16[544,1024]{1,0:T(8,128)(2,1)} %get-tuple-element.18.refs_7_.refs_1_.refs_3_.refs_9_) | copy-start | bytes 3342340
  90.5 37.7 %collective-permute-start.7 = (bf16[384,1024]{1,0:T(8,128)(2,1)}, bf16[384,1024]{1,0:T(8,128)(2,1)S(1)}, u32[]{:S(2)}, u32[]{:S(2)}) collective-permute-start(bf16[384,1024]{1,0:T(8,128)(2,1)} %shard_map.84), channel_id=1, source_target_pairs={{24,16},{0,8},{25,17},{1,9},{26,18},{2,10},{27,19},{3,11},{28,20},... | collective-permute-start | bytes 2359304 | tf_op jit(solution)/shard_map/ppermute | solution.py:501
  91.9 36.3 %collective-permute-start.8 = (bf16[384,1024]{1,0:T(8,128)(2,1)}, bf16[384,1024]{1,0:T(8,128)(2,1)S(1)}, u32[]{:S(2)}, u32[]{:S(2)}) collective-permute-start(bf16[384,1024]{1,0:T(8,128)(2,1)} %shard_map.85), channel_id=1, source_target_pairs={{8,16},{16,8},{9,17},{17,9},{10,18},{18,10},{11,19},{19,11},{12,20... | collective-permute-start | bytes 2359304 | tf_op jit(solution)/shard_map/ppermute | solution.py:499
  96.5 1.1 copy-start.11
  112.9 15.3 %copy-start.5 = (bf16[384,1024]{1,0:T(8,128)(2,1)S(1)}, bf16[384,1024]{1,0:T(8,128)(2,1)}, u32[]{:S(2)}) copy-start(bf16[384,1024]{1,0:T(8,128)(2,1)} %get-tuple-element.20.refs_3_) | copy-start | bytes 2359300
  112.9 15.3 %copy-start.7 = (bf16[384,1024]{1,0:T(8,128)(2,1)S(1)}, bf16[384,1024]{1,0:T(8,128)(2,1)}, u32[]{:S(2)}) copy-start(bf16[384,1024]{1,0:T(8,128)(2,1)} %get-tuple-element.21.refs_5_) | copy-start | bytes 2359300

commit v6 on v5

--- a/solution.py
+++ b/solution.py
@@ -20,6 +20,7 @@
 HALF = BLK // 2
 CORNER = HALF + 16
 INFO = 16
+RANGE = 80.0
 VMEM_LIMIT = 60 * 1024 * 1024
 
 ANY = pl.BlockSpec(memory_space=pl.ANY)
@@ -190,22 +191,24 @@
         query_copy.wait()
         seen = related(first, 0).astype(jnp.float32).astype(jnp.bfloat16)
         turned = jnp.transpose(flipped(jnp.transpose(flipped(seen[:HALF]).astype(jnp.float32)).astype(jnp.bfloat16)).astype(jnp.float32))
-        low_bias = jnp.where(seen[HALF:].astype(jnp.float32) > 0.5, 0.0, NEG)
-        high_bias = jnp.where(turned > 0.5, 0.0, NEG)
         own_rows = pl.ds(pl.multiple_of(REACH + first * BLK, BLK), BLK)
         left, right = sides()
-
-        def shares(query, key, mask):
-            scores = product_t(query, key).reshape(group, HALF, BLK) + mask[None]
-            top = jnp.max(scores, axis=-1, keepdims=True)
-            weights = jnp.exp2((scores - top) * FACTOR)
-            return weights / jnp.sum(weights, axis=-1, keepdims=True)
+        low_bias = jnp.where(left & (seen[HALF:].astype(jnp.float32) > 0.5), 0.0, NEG)
+        high_bias = jnp.where(right & (turned > 0.5), 0.0, NEG)
+        between = jnp.logical_not(left | right)
+
+        def ratios(query, key, mask):
+            scores = product_t(query, key).reshape(group, HALF, BLK)
+            own = jnp.sum(jnp.where(between[None], scores, 0.0), axis=-1, keepdims=True)
+            scores = scores + mask[None]
+            base = jnp.maximum(own, jnp.max(scores, axis=-1, keepdims=True) - RANGE / FACTOR)
+            return jnp.exp2((scores - base) * FACTOR)
 
         for at in range(taken):
             key = kbuf[own_rows, at * HEAD : (at + 1) * HEAD]
             query = corner_q[:, at * width : (at + 1) * width]
-            low = shares(stacked(query[HALF:]), key, low_bias)
-            high = shares(stacked(flipped(query[:HALF])), flipped(key), high_bias)
+            low = ratios(stacked(query[HALF:]), key, low_bias)
+            high = ratios(stacked(flipped(query[:HALF])), flipped(key), high_bias)
             mixed = jnp.where(right[None], high, first.astype(jnp.float32))
             mixed = jnp.where(left[None], low, mixed).astype(jnp.bfloat16)
             value = vbuf[own_rows, at * HEAD : (at + 1) * HEAD]
@@ -414,14 +417,14 @@
     for at, decoded in blocks.items():
         value = stacked(stages[at][HALF:])
         turned = flipped(value)
-        shares = stacked(stages[at][:HALF].astype(jnp.float32)).reshape(group, HALF, BLK)
+        ratios = stacked(stages[at][:HALF].astype(jnp.float32)).reshape(group, HALF, BLK)
 
         def context(side, basis):
-            kept = jnp.where(side[None], shares, 0.0)
-            rest = 1.0 - jnp.sum(kept, axis=-1, keepdims=True)
+            kept = jnp.where(side[None], ratios, 0.0)
+            totals = 1.0 + jnp.sum(kept, axis=-1, keepdims=True)
             mixed = product(kept.astype(jnp.bfloat16).reshape(group * HALF, BLK), basis)
-            mixed = mixed.reshape(group, HALF, HEAD) + rest * basis[HALF:].astype(jnp.float32)[None]
-            mixed = mixed.astype(jnp.bfloat16)
+            mixed = mixed.reshape(group, HALF, HEAD) + basis[HALF:].astype(jnp.float32)[None]
+            mixed = (mixed / totals).astype(jnp.bfloat16)
             return jnp.concatenate([mixed[g] for g in range(group)], axis=1)
 
         decoded[HALF:] = context(left, value)

time: 132 us -> 132 us (level)
  no operation moved by 1% of the time
where the time goes in v6:
time: 132 us; the launch traced here: 130 us
  Pallas kernels  56.9 us (43%)
  waiting for transfers between devices  36.6 us (28%)
  starting transfers between devices  27.3 us (21%)
  local copies, waits for them, and re-layouts  8.24 us (6%)
    pallas_call x6, Pallas kernels, attend(): pl.pallas_call(kernel, out_shape=out_shape, in_specs=[HBM] * 6 + [ANY] *...  45.4 us
    ppermute x1, waiting for transfers between devices, on_device(): across_2 = lax.ppermute(behind(routed_2, direct_1), 'pipe', ACROSS)  14.2 us
    pallas_call x3, Pallas kernels, place(): pl.pallas_call(functools.partial(place_kernel, [(piece[0],) + piece[2:] f...  11.5 us
    ppermute x1, waiting for transfers between devices, on_device(): onward_2 = lax.ppermute(behind(across_2, direct_1), 'pipe', ONWARD)  10.9 us
    ppermute x1, waiting for transfers between devices, on_device(): diagonal_1 = lax.ppermute(direct_1, 'pipe', DIAGONAL)  9.47 us
    unnamed x32, local copies, waits for them, and re-layouts  8.24 us
    ppermute x1, starting transfers between devices, on_device(): diagonal_2 = lax.ppermute(behind(direct_2, across_2), 'pipe', DIAGONAL)  4.57 us
    ppermute x1, starting transfers between devices, on_device(): diagonal_1 = lax.ppermute(direct_1, 'pipe', DIAGONAL)  4.34 us
  transfers between devices with their start and end apart: 12, of which 5 were waited for; matrix products, arithmetic and copies ran while one was open for 2% of the time, Pallas kernels for 40%

profile of v6, /device:TPU:20, one launch (start us, length us, event | category | flops | bytes accessed | tf_op | source)
XLA Modules:
  0.0 130.0 jit_solution(9198214098892325382)
XLA Ops:
  0.6 2.6 %shard_map.77.refs_6_ = bf16[128,1024]{1,0:T(8,128)(2,1)} custom-call(s32[2,32]{1,0:T(2,128)} %bitcast.40, bf16[2,512,4096]{2,1,0:T(8,128)(2,1)} %bitcast.8, bf16[2,512,512]{2,1,0:T(8,128)(2,1)} %bitcast.14, bf16[2,512,512]{2,1,0:T(8,128)(2,1)} %bitcast.20, s32[2,512]{1,0:T(2,128)} %bitcast.28, s32[2,512]{1,0:T(2,128)} %bitcast.34), custom_call_target="tpu_custom_call" | custom-call | flops 1024 | bytes 1024 | tf_op jit(solution)/shard_map/pallas_call | solution.py:334
  3.3 1.6 %collective-permute-start.2 = (bf16[128,1024]{1,0:T(8,128)(2,1)}, bf16[128,1024]{1,0:T(8,128)(2,1)S(1)}, u32[]{:S(2)}, u32[]{:S(2)}) collective-permute-start(bf16[128,1024]{1,0:T(8,128)(2,1)} %shard_map.77.refs_6_), channel_id=1, source_target_pairs={{0,8},{8,0},{16,24},{24,16},{1,9},{9,1},{17,25},{25,17},{2,10},{10... | collective-permute-start | bytes 786440 | tf_op jit(solution)/shard_map/ppermute | solution.py:479
  4.8 4.3 %shard_map.78 = (bf16[128,3072]{1,0:T(8,128)(2,1)}, bf16[2,272,512]{2,1,0:T(8,128)(2,1)}, bf16[2,272,512]{2,1,0:T(8,128)(2,1)}) custom-call(s32[2,32]{1,0:T(2,128)} %bitcast.41, bf16[2,512,4096]{2,1,0:T(8,128)(2,1)} %bitcast.9, bf16[2,512,512]{2,1,0:T(8,128)(2,1)} %bitcast.15, bf16[2,512,512]{2,1,0:T(8,128)(2,1)} %bitcast.21, s32[2,512]{1,0:T(2,128)} %bitcast.29, ...), custom_call_target="tpu_custom_call" | custom-call | flops 1024 | bytes 1024 | tf_op jit(solution)/shard_map/pallas_call | solution.py:334
  9.1 0.6 collective-permute-start.3
  9.8 2.0 %collective-permute-start.1 = (bf16[2,272,512]{2,1,0:T(8,128)(2,1)}, bf16[2,272,512]{2,1,0:T(8,128)(2,1)S(1)}, u32[]{:S(2)}, u32[]{:S(2)}) collective-permute-start(bf16[2,272,512]{2,1,0:T(8,128)(2,1)} %get-tuple-element.16), channel_id=1, source_target_pairs={{0,1},{1,2},{2,3},{3,4},{4,5},{5,6},{6,7},{8,9},{9,10},{10,11},{11... | collective-permute-start | bytes 1671176 | tf_op jit(solution)/shard_map/ppermute | solution.py:482
  11.8 0.7 copy-done.8
  12.5 5.0 %shard_map.79.refs_7_ = bf16[320,1024]{1,0:T(8,128)(2,1)} custom-call(s32[2,32]{1,0:T(2,128)} %bitcast.42, bf16[2,512,4096]{2,1,0:T(8,128)(2,1)} %bitcast.10, bf16[2,512,512]{2,1,0:T(8,128)(2,1)} %bitcast.16, bf16[2,512,512]{2,1,0:T(8,128)(2,1)} %bitcast.22, s32[2,512]{1,0:T(2,128)} %bitcast.30, s32[2,512]{1,0:T(2,128)} %bitcast.36, ...), custom_call_target="tpu_custom_call" | custom-call | flops 1024 | bytes 1024 | tf_op jit(solution)/shard_map/pallas_call | solution.py:334
  17.5 2.3 %collective-permute-start.4 = (bf16[320,1024]{1,0:T(8,128)(2,1)}, bf16[320,1024]{1,0:T(8,128)(2,1)S(1)}, u32[]{:S(2)}, u32[]{:S(2)}) collective-permute-start(bf16[320,1024]{1,0:T(8,128)(2,1)} %shard_map.79.refs_7_), channel_id=1, source_target_pairs={{0,8},{8,0},{16,24},{24,16},{1,9},{9,1},{17,25},{25,17},{2,10},{10... | collective-permute-start | bytes 1966088 | tf_op jit(solution)/shard_map/ppermute | solution.py:485
  19.7 2.6 %collective-permute-start = (bf16[2,272,512]{2,1,0:T(8,128)(2,1)S(1)}, bf16[2,272,512]{2,1,0:T(8,128)(2,1)S(1)}, u32[]{:S(2)}, u32[]{:S(2)}) collective-permute-start(bf16[2,272,512]{2,1,0:T(8,128)(2,1)S(1)} %copy-done.14), channel_id=1, source_target_pairs={{0,1},{1,2},{2,3},{3,4},{4,5},{5,6},{6,7},{8,9},{9,10},{10,11},{11... | collective-permute-start | bytes 1671176 | tf_op jit(solution)/shard_map/ppermute | solution.py:483
  22.4 0.8 copy-done.13
  23.2 10.0 %shard_map.80.refs_7_ = bf16[256,4096]{1,0:T(8,128)(2,1)} custom-call(s32[2,32]{1,0:T(2,128)} %bitcast.43, bf16[2,512,4096]{2,1,0:T(8,128)(2,1)} %bitcast.11, bf16[2,512,512]{2,1,0:T(8,128)(2,1)} %bitcast.17, bf16[2,512,512]{2,1,0:T(8,128)(2,1)} %bitcast.23, s32[2,512]{1,0:T(2,128)} %bitcast.31, s32[2,512]{1,0:T(2,128)} %bitcast.37, ...), custom_call_target="tpu_custom_call" | custom-call | flops 2000001024 | bytes 1024 | tf_op jit(solution)/shard_map/pallas_call | solution.py:334
  33.7 0.8 copy-done.12
  34.6 11.7 %shard_map.81 = (bf16[544,1024]{1,0:T(8,128)(2,1)}, bf16[384,1024]{1,0:T(8,128)(2,1)}) custom-call(s32[2,32]{1,0:T(2,128)} %bitcast.44, bf16[2,512,4096]{2,1,0:T(8,128)(2,1)} %bitcast.12, bf16[2,512,512]{2,1,0:T(8,128)(2,1)} %bitcast.18, bf16[2,512,512]{2,1,0:T(8,128)(2,1)} %bitcast.24, s32[2,512]{1,0:T(2,128)} %bitcast.32, s32[2,512]{1,0:T(2,128)} %bitcast.38, ...), custom_call_target="tpu_custom_call" | custom-call | flops 1024 | bytes 1024 | tf_op jit(solution)/shard_map/pallas_call | solution.py:334
  46.3 3.4 %collective-permute-start.9 = (bf16[544,1024]{1,0:T(8,128)(2,1)}, bf16[544,1024]{1,0:T(8,128)(2,1)}, u32[]{:S(2)}, u32[]{:S(2)}) collective-permute-start(bf16[544,1024]{1,0:T(8,128)(2,1)} %get-tuple-element.18.refs_7_.refs_1_.refs_3_.refs_9_), channel_id=1, source_target_pairs={{8,24},{16,0},{9,25},{17,1},{10,26},{18,2},{11,27},{19,3},{12,28},... | collective-permute-start | bytes 3342344 | tf_op jit(solution)/shard_map/ppermute | solution.py:489
  49.7 2.1 %copy.16.refs_0_ = bf16[384,1024]{1,0:T(8,128)(2,1)} copy(bf16[384,1024]{1,0:T(8,128)(2,1)} %get-tuple-element.20.refs_3_) | data formatting | bytes 1572864
  51.8 0.9 copy-done.10
  52.7 0.9 copy-done.2
  53.6 11.8 %shard_map.82 = (bf16[544,1024]{1,0:T(8,128)(2,1)}, bf16[384,1024]{1,0:T(8,128)(2,1)}) custom-call(s32[2,32]{1,0:T(2,128)} %bitcast.45, bf16[2,512,4096]{2,1,0:T(8,128)(2,1)} %bitcast.13, bf16[2,512,512]{2,1,0:T(8,128)(2,1)} %bitcast.19, bf16[2,512,512]{2,1,0:T(8,128)(2,1)} %bitcast.25, s32[2,512]{1,0:T(2,128)} %bitcast.33, s32[2,512]{1,0:T(2,128)} %bitcast.39, ...), custom_call_target="tpu_custom_call" | custom-call | flops 99999997952 | bytes 1024 | tf_op jit(solution)/shard_map/pallas_call | solution.py:334
  65.4 2.4 %collective-permute-start.6 = (bf16[384,1024]{1,0:T(8,128)(2,1)}, bf16[384,1024]{1,0:T(8,128)(2,1)}, u32[]{:S(2)}, u32[]{:S(2)}) collective-permute-start(bf16[384,1024]{1,0:T(8,128)(2,1)} %shard_map.83), channel_id=1, source_target_pairs={{8,24},{16,0},{9,25},{17,1},{10,26},{18,2},{11,27},{19,3},{12,28},... | collective-permute-start | bytes 2359304 | tf_op jit(solution)/shard_map/ppermute | solution.py:501
  67.8 4.3 %collective-permute-start.5 = (bf16[544,1024]{1,0:T(8,128)(2,1)S(1)}, bf16[544,1024]{1,0:T(8,128)(2,1)S(1)}, u32[]{:S(2)}, u32[]{:S(2)}) collective-permute-start(bf16[544,1024]{1,0:T(8,128)(2,1)S(1)} %copy-done), channel_id=1, source_target_pairs={{8,16},{16,8},{9,17},{17,9},{10,18},{18,10},{11,19},{19,11},{12,20... | collective-permute-start | bytes 3342344 | tf_op jit(solution)/shard_map/ppermute | solution.py:500
  72.1 1.8 %collective-permute-done.9.refs_0_ = bf16[544,1024]{1,0:T(8,128)(2,1)} collective-permute-done((bf16[544,1024]{1,0:T(8,128)(2,1)}, bf16[544,1024]{1,0:T(8,128)(2,1)}, u32[]{:S(2)}, u32[]{:S(2)}) %collective-permute-start.9) | collective-permute-done | bytes 1114144 | tf_op jit(solution)/shard_map/ppermute | solution.py:489
  73.9 1.3 collective-permute-start.10
  75.2 0.9 copy.18.refs_0_
  76.1 14.2 %collective-permute-done.6.refs_0_.refs_1_ = bf16[384,1024]{1,0:T(8,128)(2,1)} collective-permute-done((bf16[384,1024]{1,0:T(8,128)(2,1)}, bf16[384,1024]{1,0:T(8,128)(2,1)}, u32[]{:S(2)}, u32[]{:S(2)}) %collective-permute-start.6) | collective-permute-done | bytes 786464 | tf_op jit(solution)/shard_map/ppermute | solution.py:501
  90.4 1.6 %collective-permute-start.7 = (bf16[384,1024]{1,0:T(8,128)(2,1)}, bf16[384,1024]{1,0:T(8,128)(2,1)S(1)}, u32[]{:S(2)}, u32[]{:S(2)}) collective-permute-start(bf16[384,1024]{1,0:T(8,128)(2,1)} %shard_map.84), channel_id=1, source_target_pairs={{24,16},{0,8},{25,17},{1,9},{26,18},{2,10},{27,19},{3,11},{28,20},... | collective-permute-start | bytes 2359304 | tf_op jit(solution)/shard_map/ppermute | solution.py:504
  92.0 4.6 %collective-permute-start.8 = (bf16[384,1024]{1,0:T(8,128)(2,1)}, bf16[384,1024]{1,0:T(8,128)(2,1)S(1)}, u32[]{:S(2)}, u32[]{:S(2)}) collective-permute-start(bf16[384,1024]{1,0:T(8,128)(2,1)} %shard_map.85), channel_id=1, source_target_pairs={{8,16},{16,8},{9,17},{17,9},{10,18},{18,10},{11,19},{19,11},{12,20... | collective-permute-start | bytes 2359304 | tf_op jit(solution)/shard_map/ppermute | solution.py:502
  96.6 1.1 copy-done.11
  97.7 5.5 %shard_map.87 = (bf16[512,4096]{1,0:T(8,128)(2,1)}, bf16[512,4096]{1,0:T(8,128)(2,1)}) custom-call(bf16[320,1024]{1,0:T(8,128)(2,1)S(1)} %copy-done.3, bf16[320,1024]{1,0:T(8,128)(2,1)S(1)} %copy-done.3, bf16[320,1024]{1,0:T(8,128)(2,1)S(1)} %copy-done.3, bf16[320,1024]{1,0:T(8,128)(2,1)S(1)} %copy-done.3, bf16[128,1024]{1,0:T(8,128)(2,1)S(1)} %copy-done.9, ...), custom_call_target="tpu_custom_call" | custom-call | flops 1024 | bytes 1024 | tf_op jit(solution)/shard_map/pallas_call | solution.py:445
  103.2 9.5 %collective-permute-done.5.refs_4_.refs_6_.refs_10_.refs_0_ = bf16[544,1024]{1,0:T(8,128)(2,1)S(1)} collective-permute-done((bf16[544,1024]{1,0:T(8,128)(2,1)S(1)}, bf16[544,1024]{1,0:T(8,128)(2,1)S(1)}, u32[]{:S(2)}, u32[]{:S(2)}) %collective-permute-start.5) | collective-permute-done | bytes 1114144 | tf_op jit(solution)/shard_map/ppermute | solution.py:500
  112.9 4.4 %shard_map.88 = (bf16[512,4096]{1,0:T(8,128)(2,1)}, bf16[512,4096]{1,0:T(8,128)(2,1)}) custom-call(bf16[544,1024]{1,0:T(8,128)(2,1)} %collective-permute-done.10.refs_0_.refs_2_.refs_8_, bf16[544,1024]{1,0:T(8,128)(2,1)S(1)} %copy-done.4, ...), custom_call_target="tpu_custom_call", output_to_operand_aliasing={{0}: (12, {}), {1}: (13, {})} | custom-call | flops 1024 | bytes 1024 | tf_op jit(solution)/shard_map/pallas_call | solution.py:445
  117.3 10.9 %collective-permute-done.7.refs_2_ = bf16[384,1024]{1,0:T(8,128)(2,1)S(1)} collective-permute-done((bf16[384,1024]{1,0:T(8,128)(2,1)}, bf16[384,1024]{1,0:T(8,128)(2,1)S(1)}, u32[]{:S(2)}, u32[]{:S(2)}) %collective-permute-start.7) | collective-permute-done | bytes 786464 | tf_op jit(solution)/shard_map/ppermute | solution.py:504
  128.2 1.6 %shard_map.89 = (bf16[512,4096]{1,0:T(8,128)(2,1)}, bf16[512,4096]{1,0:T(8,128)(2,1)}) custom-call(bf16[544,1024]{1,0:T(8,128)(2,1)S(1)} %collective-permute-done.5.refs_4_.refs_6_.refs_10_.refs_0_, bf16[544,1024]{1,0:T(8,128)(2,1)S(1)} %copy-done.1, ...), custom_call_target="tpu_custom_call", output_to_operand_aliasing={{0}: (6, {}), {1}: (7, {})} | custom-call | flops 1024 | bytes 1024 | tf_op jit(solution)/shard_map/pallas_call | solution.py:445
  (37 shorter events, 0.8 us)
Async XLA Ops:
  3.3 8.5 %collective-permute-start.2 = (bf16[128,1024]{1,0:T(8,128)(2,1)}, bf16[128,1024]{1,0:T(8,128)(2,1)S(1)}, u32[]{:S(2)}, u32[]{:S(2)}) collective-permute-start(bf16[128,1024]{1,0:T(8,128)(2,1)} %shard_map.77.refs_6_), channel_id=1, source_target_pairs={{0,8},{8,0},{16,24},{24,16},{1,9},{9,1},{17,25},{25,17},{2,10},{10... | collective-permute-start | bytes 786440 | tf_op jit(solution)/shard_map/ppermute | solution.py:479
  9.1 42.7 %collective-permute-start.3 = (bf16[128,3072]{1,0:T(8,128)(2,1)}, bf16[128,3072]{1,0:T(8,128)(2,1)S(1)}, u32[]{:S(2)}, u32[]{:S(2)}) collective-permute-start(bf16[128,3072]{1,0:T(8,128)(2,1)} %get-tuple-element.17.refs_6_), channel_id=1, source_target_pairs={{0,8},{8,0},{16,24},{24,16},{1,9},{9,1},{17,25},{25,17},{2,10},{10... | collective-permute-start | bytes 2359304 | tf_op jit(solution)/shard_map/ppermute | solution.py:481
  9.8 10.0 %copy-start.14 = (bf16[2,272,512]{2,1,0:T(8,128)(2,1)S(1)}, bf16[2,272,512]{2,1,0:T(8,128)(2,1)}, u32[]{:S(2)}) copy-start(bf16[2,272,512]{2,1,0:T(8,128)(2,1)} %get-tuple-element.15) | copy-start | bytes 1671172
  9.8 12.6 %collective-permute-start.1 = (bf16[2,272,512]{2,1,0:T(8,128)(2,1)}, bf16[2,272,512]{2,1,0:T(8,128)(2,1)S(1)}, u32[]{:S(2)}, u32[]{:S(2)}) collective-permute-start(bf16[2,272,512]{2,1,0:T(8,128)(2,1)} %get-tuple-element.16), channel_id=1, source_target_pairs={{0,1},{1,2},{2,3},{3,4},{4,5},{5,6},{6,7},{8,9},{9,10},{10,11},{11... | collective-permute-start | bytes 1671176 | tf_op jit(solution)/shard_map/ppermute | solution.py:482
  11.8 0.7 copy-start.8
  17.5 34.4 %collective-permute-start.4 = (bf16[320,1024]{1,0:T(8,128)(2,1)}, bf16[320,1024]{1,0:T(8,128)(2,1)S(1)}, u32[]{:S(2)}, u32[]{:S(2)}) collective-permute-start(bf16[320,1024]{1,0:T(8,128)(2,1)} %shard_map.79.refs_7_), channel_id=1, source_target_pairs={{0,8},{8,0},{16,24},{24,16},{1,9},{9,1},{17,25},{25,17},{2,10},{10... | collective-permute-start | bytes 1966088 | tf_op jit(solution)/shard_map/ppermute | solution.py:485
  19.7 14.0 %collective-permute-start = (bf16[2,272,512]{2,1,0:T(8,128)(2,1)S(1)}, bf16[2,272,512]{2,1,0:T(8,128)(2,1)S(1)}, u32[]{:S(2)}, u32[]{:S(2)}) collective-permute-start(bf16[2,272,512]{2,1,0:T(8,128)(2,1)S(1)} %copy-done.14), channel_id=1, source_target_pairs={{0,1},{1,2},{2,3},{3,4},{4,5},{5,6},{6,7},{8,9},{9,10},{10,11},{11... | collective-permute-start | bytes 1671176 | tf_op jit(solution)/shard_map/ppermute | solution.py:483
  22.4 0.8 copy-start.13
  33.1 63.4 %collective-permute-start.11 = (bf16[256,4096]{1,0:T(8,128)(2,1)}, bf16[256,4096]{1,0:T(8,128)(2,1)}, u32[]{:S(2)}, u32[]{:S(2)}) collective-permute-start(bf16[256,4096]{1,0:T(8,128)(2,1)} %shard_map.80.refs_7_), channel_id=1, source_target_pairs={{0,8},{8,0},{16,24},{24,16},{1,9},{9,1},{17,25},{25,17},{2,10},{10... | collective-permute-start | bytes 6291464 | tf_op jit(solution)/shard_map/ppermute | solution.py:487
  33.7 0.8 copy-start.12
  46.3 27.6 %collective-permute-start.9 = (bf16[544,1024]{1,0:T(8,128)(2,1)}, bf16[544,1024]{1,0:T(8,128)(2,1)}, u32[]{:S(2)}, u32[]{:S(2)}) collective-permute-start(bf16[544,1024]{1,0:T(8,128)(2,1)} %get-tuple-element.18.refs_7_.refs_1_.refs_3_.refs_9_), channel_id=1, source_target_pairs={{8,24},{16,0},{9,25},{17,1},{10,26},{18,2},{11,27},{19,3},{12,28},... | collective-permute-start | bytes 3342344 | tf_op jit(solution)/shard_map/ppermute | solution.py:489
  51.8 0.9 copy-start.10
  52.7 0.9 copy-start.2
  65.3 2.4 %copy-start = (bf16[544,1024]{1,0:T(8,128)(2,1)S(1)}, bf16[544,1024]{1,0:T(8,128)(2,1)}, u32[]{:S(2)}) copy-start(bf16[544,1024]{1,0:T(8,128)(2,1)} %get-tuple-element.19.refs_1_.refs_5_.refs_7_.refs_11_) | copy-start | bytes 3342340
  65.4 9.8 %copy-start.6 = (bf16[384,1024]{1,0:T(8,128)(2,1)S(1)}, bf16[384,1024]{1,0:T(8,128)(2,1)}, u32[]{:S(2)}) copy-start(bf16[384,1024]{1,0:T(8,128)(2,1)} %get-tuple-element.21.refs_5_) | copy-start | bytes 2359300
  65.4 25.0 %collective-permute-start.6 = (bf16[384,1024]{1,0:T(8,128)(2,1)}, bf16[384,1024]{1,0:T(8,128)(2,1)}, u32[]{:S(2)}, u32[]{:S(2)}) collective-permute-start(bf16[384,1024]{1,0:T(8,128)(2,1)} %shard_map.83), channel_id=1, source_target_pairs={{8,24},{16,0},{9,25},{17,1},{10,26},{18,2},{11,27},{19,3},{12,28},... | collective-permute-start | bytes 2359304 | tf_op jit(solution)/shard_map/ppermute | solution.py:501
  67.8 44.9 %collective-permute-start.5 = (bf16[544,1024]{1,0:T(8,128)(2,1)S(1)}, bf16[544,1024]{1,0:T(8,128)(2,1)S(1)}, u32[]{:S(2)}, u32[]{:S(2)}) collective-permute-start(bf16[544,1024]{1,0:T(8,128)(2,1)S(1)} %copy-done), channel_id=1, source_target_pairs={{8,16},{16,8},{9,17},{17,9},{10,18},{18,10},{11,19},{19,11},{12,20... | collective-permute-start | bytes 3342344 | tf_op jit(solution)/shard_map/ppermute | solution.py:500
  73.9 38.9 %collective-permute-start.10 = (bf16[544,1024]{1,0:T(8,128)(2,1)}, bf16[544,1024]{1,0:T(8,128)(2,1)}, u32[]{:S(2)}, u32[]{:S(2)}) collective-permute-start(bf16[544,1024]{1,0:T(8,128)(2,1)} %shard_map.86), channel_id=1, source_target_pairs={{24,16},{0,8},{25,17},{1,9},{26,18},{2,10},{27,19},{3,11},{28,20},... | collective-permute-start | bytes 3342344 | tf_op jit(solution)/shard_map/ppermute | solution.py:503
  76.1 20.4 %copy-start.3 = (bf16[320,1024]{1,0:T(8,128)(2,1)S(1)}, bf16[320,1024]{1,0:T(8,128)(2,1)}, u32[]{:S(2)}) copy-start(bf16[320,1024]{1,0:T(8,128)(2,1)} %copy-done.2) | copy-start | bytes 1966084
  76.1 20.4 %copy-start.9 = (bf16[128,1024]{1,0:T(8,128)(2,1)S(1)}, bf16[128,1024]{1,0:T(8,128)(2,1)}, u32[]{:S(2)}) copy-start(bf16[128,1024]{1,0:T(8,128)(2,1)} %copy-done.8) | copy-start | bytes 786436
  90.4 22.5 %copy-start.1 = (bf16[544,1024]{1,0:T(8,128)(2,1)S(1)}, bf16[544,1024]{1,0:T(8,128)(2,1)}, u32[]{:S(2)}) copy-start(bf16[544,1024]{1,0:T(8,128)(2,1)} %get-tuple-element.19.refs_1_.refs_5_.refs_7_.refs_11_) | copy-start | bytes 3342340
  90.4 22.5 %copy-start.4 = (bf16[544,1024]{1,0:T(8,128)(2,1)S(1)}, bf16[544,1024]{1,0:T(8,128)(2,1)}, u32[]{:S(2)}) copy-start(bf16[544,1024]{1,0:T(8,128)(2,1)} %get-tuple-element.18.refs_7_.refs_1_.refs_3_.refs_9_) | copy-start | bytes 3342340
  90.4 37.8 %collective-permute-start.7 = (bf16[384,1024]{1,0:T(8,128)(2,1)}, bf16[384,1024]{1,0:T(8,128)(2,1)S(1)}, u32[]{:S(2)}, u32[]{:S(2)}) collective-permute-start(bf16[384,1024]{1,0:T(8,128)(2,1)} %shard_map.84), channel_id=1, source_target_pairs={{24,16},{0,8},{25,17},{1,9},{26,18},{2,10},{27,19},{3,11},{28,20},... | collective-permute-start | bytes 2359304 | tf_op jit(solution)/shard_map/ppermute | solution.py:504
  92.0 36.2 %collective-permute-start.8 = (bf16[384,1024]{1,0:T(8,128)(2,1)}, bf16[384,1024]{1,0:T(8,128)(2,1)S(1)}, u32[]{:S(2)}, u32[]{:S(2)}) collective-permute-start(bf16[384,1024]{1,0:T(8,128)(2,1)} %shard_map.85), channel_id=1, source_target_pairs={{8,16},{16,8},{9,17},{17,9},{10,18},{18,10},{11,19},{19,11},{12,20... | collective-permute-start | bytes 2359304 | tf_op jit(solution)/shard_map/ppermute | solution.py:502
  96.6 1.1 copy-start.11
  112.9 15.3 %copy-start.5 = (bf16[384,1024]{1,0:T(8,128)(2,1)S(1)}, bf16[384,1024]{1,0:T(8,128)(2,1)}, u32[]{:S(2)}) copy-start(bf16[384,1024]{1,0:T(8,128)(2,1)} %get-tuple-element.20.refs_3_) | copy-start | bytes 2359300
  112.9 15.3 %copy-start.7 = (bf16[384,1024]{1,0:T(8,128)(2,1)S(1)}, bf16[384,1024]{1,0:T(8,128)(2,1)}, u32[]{:S(2)}) copy-start(bf16[384,1024]{1,0:T(8,128)(2,1)} %get-tuple-element.21.refs_5_) | copy-start | bytes 2359300

commit v7 on v6

--- a/solution.py
+++ b/solution.py
@@ -25,6 +25,7 @@
 
 ANY = pl.BlockSpec(memory_space=pl.ANY)
 HBM = pl.BlockSpec(memory_space=pltpu.HBM)
+VMEM = pl.BlockSpec(memory_space=pltpu.VMEM)
 
 
 def flipped(array):
@@ -57,13 +58,15 @@
     return at + (first <= at).astype(jnp.int32)
 
 
-def attend_kernel(payload, groups, items, corner, pack, halo, last, *refs):
+def attend_kernel(payload, groups, items, corner, pack, halo, last, resident, *refs):
     heads = [head for group in groups for head in group]
     refs = list(refs)
     lengths_in, queries, keys, values, seg_in, par_in = refs[:6]
     refs = refs[6:]
     halo_in = refs.pop(0) if halo else None
     outs = [refs.pop(0) for _ in groups]
+    if resident:
+        refs.pop(0)
     pack_outs = [refs.pop(0), refs.pop(0)] if pack else None
     kbuf, vbuf, bias, segs, pars, seg, par, lengths, marks, sems = refs[:10]
     refs = refs[10:]
@@ -254,8 +257,11 @@
             lanes = slice(at * HEAD, (at + 1) * HEAD)
             place = slice(at * width, (at + 1) * width)
             copy.wait()
-            last_out[:, place] = mixture(last_q[:, place], kbuf[window, lanes], vbuf[window, lanes])
-            stores.append(start(last_out.at[:, place], outs[0].at[:, place]))
+            if resident:
+                outs[0][:, place] = mixture(last_q[:, place], kbuf[window, lanes], vbuf[window, lanes])
+            else:
+                last_out[:, place] = mixture(last_q[:, place], kbuf[window, lanes], vbuf[window, lanes])
+                stores.append(start(last_out.at[:, place], outs[0].at[:, place]))
             if pack and at == 0:
                 store_pack()
         for copy in stores + pack_stores:
@@ -292,7 +298,7 @@
         copy.wait()
 
 
-def attend(payload, groups, items, operands, after=(), halo=None, corner=False, pack=False, last=False, weight=0):
+def attend(payload, groups, items, operands, after=(), halo=None, corner=False, pack=False, last=False, resident=False, weight=0):
     lengths, queries, keys, values, seg, par = operands
     rows, columns = queries.shape[1:]
     width = columns // (keys.shape[2] // HEAD)
@@ -325,17 +331,19 @@
         scratch.append(pltpu.VMEM(packed, jnp.bfloat16))
     if last:
         scratch += [pltpu.VMEM((BLK, len(heads) * width), jnp.bfloat16)] * 2
+    if resident:
+        out_shape = [pltpu.VMEM(sizes[0], jnp.bfloat16), jax.ShapeDtypeStruct((8, HEAD), jnp.float32)]
     inputs = [lengths, queries, keys, values, seg, par] + ([] if halo is None else [halo])
 
     def kernel(*refs):
         refs = refs[: len(inputs)] + refs[len(inputs) + len(after) :]
-        attend_kernel(payload, groups, items, corner, pack, halo is not None, last, *refs)
+        attend_kernel(payload, groups, items, corner, pack, halo is not None, last, resident, *refs)
 
     return pl.pallas_call(
         kernel,
         out_shape=out_shape,
         in_specs=[HBM] * 6 + [ANY] * (len(inputs) - 6 + len(after)),
-        out_specs=[ANY] * len(out_shape),
+        out_specs=[VMEM, ANY] if resident else [ANY] * len(out_shape),
         scratch_shapes=scratch,
         compiler_params=pltpu.CompilerParams(vmem_limit_bytes=VMEM_LIMIT),
         cost_estimate=cost(weight),
@@ -353,7 +361,7 @@
     )(value, *after)
 
 
-def place_kernel(pieces, aliased, *refs):
+def place_kernel(pieces, aliased, resident, *refs):
     refs = list(refs)
     sources = [[refs.pop(0)] if piece[1] else [refs.pop(0), refs.pop(0)] for piece in pieces]
     refs = refs[aliased:]
@@ -370,7 +378,9 @@
 
     parts = []
     for at, (kind, _, _, items, top) in enumerate(pieces):
-        if kind == "plain":
+        if kind == "plain" and resident:
+            parts.append((at, 0, 0, 0))
+        elif kind == "plain":
             parts += [(at, item * BLK, BLK, 0) for item in range(len(items))]
         else:
             parts.append((at, 0, stages[at].shape[0], top))
@@ -380,7 +390,9 @@
         view = (pl.ds(below + top, height), pl.ds(0, stages[at].shape[1]))
         return pltpu.make_async_copy(source.at[view], stages[at].at[pl.ds(top, height)], in_sems.at[part])
 
-    for part, (at, _, _, _) in enumerate(parts):
+    for part, (at, _, height, _) in enumerate(parts):
+        if height == 0:
+            continue
         if len(sources[at]) == 1:
             load(part, sources[at][0]).start()
         else:
@@ -390,20 +402,27 @@
     first = {}
     stores = []
 
-    def store(at, source, block):
+    def store(at, source, block, where_from=None):
         _, swap, heads, _, _ = pieces[at]
         columns = pl.ds(heads[0] * width, len(heads) * width)
         rows = pl.ds(pl.multiple_of(block * BLK, BLK), BLK)
         for to_forward, target in ((even != swap, forward), (even == swap, back)):
 
-            @pl.when(to_forward)
+            @pl.when(to_forward if where_from is None else to_forward & where_from)
             def _():
                 pltpu.make_async_copy(source, target.at[rows, columns], out_sems.at[len(stores)]).start()
 
         stores.append(pltpu.make_async_copy(source, forward.at[rows, columns], out_sems.at[len(stores)]))
 
-    for part, (at, top, _, _) in enumerate(parts):
+    for part, (at, top, height, _) in enumerate(parts):
         kind, swap, heads, items, _ = pieces[at]
+        if height == 0:
+            for index, item in enumerate(items):
+                view = pl.ds(index * BLK, BLK)
+                store(at, sources[at][1].at[view], plain_block(first[swap], item), edge)
+                stores.pop()
+                store(at, sources[at][0].at[view], plain_block(first[swap], item), jnp.logical_not(edge))
+            continue
         load(part, sources[at][0]).wait()
         if kind == "plain":
             store(at, stages[at].at[pl.ds(top, BLK)], plain_block(first[swap], items[top // BLK]))
@@ -434,24 +453,32 @@
         copy.wait()
 
 
-def place(pieces, rows, outs=(), weight=0):
+def place(pieces, rows, outs=(), resident=False):
     arrays = [array for piece in pieces for array in piece[1]]
     columns = next(piece[1][0].shape[1] // len(piece[3]) for piece in pieces if piece[3]) * KV_HEADS
     shape = jax.ShapeDtypeStruct((rows, columns), jnp.bfloat16)
     width = columns // KV_HEADS
     corners = {"guide": (16, HEAD), "corner": (CORNER, width)}
     held = [corners.get(kind, (len(items) * BLK, len(heads) * width)) for kind, _, _, heads, items, _ in pieces]
+    specs = [ANY] * len(arrays)
+    if resident:
+        held = [corners.get(piece[0], (16, HEAD)) for piece in pieces]
+        specs = [VMEM if piece[0] == "plain" else ANY for piece in pieces for _ in piece[1]]
+        arrays = [
+            pltpu.with_memory_space_constraint(array, pltpu.VMEM) if spec is VMEM else array
+            for array, spec in zip(arrays, specs)
+        ]
     decoded = [(BLK, width) for piece in pieces if piece[0] == "corner"]
     return pl.pallas_call(
-        functools.partial(place_kernel, [(piece[0],) + piece[2:] for piece in pieces], len(outs)),
+        functools.partial(place_kernel, [(piece[0],) + piece[2:] for piece in pieces], len(outs), resident),
         out_shape=[shape, shape],
-        in_specs=[ANY] * len(arrays) + [HBM] * len(outs),
+        in_specs=specs + [HBM] * len(outs),
         out_specs=[HBM, HBM],
         scratch_shapes=[pltpu.VMEM(size, jnp.bfloat16) for size in held + decoded]
         + [pltpu.SemaphoreType.DMA((4 * len(pieces),))] * 2,
         input_output_aliases={len(arrays) + i: i for i in range(len(outs))},
         compiler_params=pltpu.CompilerParams(vmem_limit_bytes=24 * 1024 * 1024),
-        cost_estimate=cost(weight),
+        cost_estimate=cost(0),
     )(*arrays, *outs)
 
 
@@ -459,7 +486,6 @@
     return pl.CostEstimate(flops=1024 + weight * 1000000, bytes_accessed=1024, transcendentals=0)
 
 
-PLACE_WEIGHT = 0
 SWAP_WEIGHT = 2000
 DIRECT_WEIGHT = 100000
 
@@ -475,9 +501,9 @@
     ring = [(source, source + 1) for source in range(lax.axis_size("dp") - 1)]
     every = tuple(range(KV_HEADS))
 
-    (swap_0,) = attend(0, ((0,),), (2,), operands, last=True)
+    swap_0, made_0 = attend(0, ((0,),), (2,), operands, last=True, resident=True)
     got_0 = lax.ppermute(swap_0, "pipe", SWAP)
-    swap_1, halo, far_halo = attend(0, ((1, 2, 3),), (2,), operands, after=(swap_0,), pack=True, last=True)
+    swap_1, halo, far_halo = attend(0, ((1, 2, 3),), (2,), operands, after=(made_0,), pack=True, last=True)
     got_1 = lax.ppermute(swap_1, "pipe", SWAP)
     halo = lax.ppermute(halo, "dp", ring)
     far_halo = lax.ppermute(far_halo, "dp", ring)
@@ -510,7 +536,6 @@
             ("plain", (got_2,), True, every, (0, 1), 0),
         ],
         rows,
-        weight=PLACE_WEIGHT,
     )
     below = TREE_MOST * BLK
     onward_1, diagonal_1 = ((onward_1, routed_1), (diagonal_1, direct_1))
@@ -534,6 +559,7 @@
         ],
         rows,
         outs,
+        resident=True,
     )
     return (forward[None], back[None])
 

time: 132 us -> 131 us (level)
  transfers between devices with their start and end apart: 12 -> 12, of which waited for: 5 -> 5; matrix products, arithmetic and copies ran while one was open for 2% -> 2% of each run, Pallas kernels for 40% -> 41%
where the time goes in v7:
time: 131 us; the launch traced here: 129 us
  Pallas kernels  56 us (43%)
  waiting for transfers between devices  36.6 us (28%)
  starting transfers between devices  27.2 us (21%)
  local copies, waits for them, and re-layouts  8.2 us (6%)
    pallas_call x6, Pallas kernels, attend(): pl.pallas_call(kernel, out_shape=out_shape, in_specs=[HBM] * 6 + [ANY] *...  44.6 us
    ppermute x1, waiting for transfers between devices, on_device(): across_2 = lax.ppermute(behind(routed_2, direct_1), 'pipe', ACROSS)  13.8 us
    pallas_call x3, Pallas kernels, place(): pl.pallas_call(functools.partial(place_kernel, [(piece[0],) + piece[2:] f...  11.4 us
    ppermute x1, waiting for transfers between devices, on_device(): onward_2 = lax.ppermute(behind(across_2, direct_1), 'pipe', ONWARD)  10.9 us
    ppermute x1, waiting for transfers between devices, on_device(): diagonal_1 = lax.ppermute(direct_1, 'pipe', DIAGONAL)  9.91 us
    unnamed x32, local copies, waits for them, and re-layouts  8.2 us
    ppermute x1, starting transfers between devices, on_device(): diagonal_2 = lax.ppermute(behind(direct_2, across_2), 'pipe', DIAGONAL)  4.57 us
    ppermute x1, starting transfers between devices, on_device(): diagonal_1 = lax.ppermute(direct_1, 'pipe', DIAGONAL)  4.35 us
  transfers between devices with their start and end apart: 12, of which 5 were waited for; matrix products, arithmetic and copies ran while one was open for 2% of the time, Pallas kernels for 41%

profile of v7, /device:TPU:20, one launch (start us, length us, event | category | flops | bytes accessed | tf_op | source)
XLA Modules:
  0.0 129.1 jit_solution(16320017461542495542)
XLA Ops:
  0.6 1.9 %shard_map.77 = (bf16[128,1024]{1,0:T(8,128)(2,1)S(1)}, f32[8,128]{1,0:T(8,128)}) custom-call(s32[2,32]{1,0:T(2,128)} %bitcast.40, bf16[2,512,4096]{2,1,0:T(8,128)(2,1)} %bitcast.8, bf16[2,512,512]{2,1,0:T(8,128)(2,1)} %bitcast.14, bf16[2,512,512]{2,1,0:T(8,128)(2,1)} %bitcast.20, s32[2,512]{1,0:T(2,128)} %bitcast.28, s32[2,512]{1,0:T(2,128)} %bitcast.34), custom_call_target="tpu_custom_call" | custom-call | flops 1024 | bytes 1024 | tf_op jit(solution)/shard_map/pallas_call | solution.py:342
  2.6 1.6 %collective-permute-start.2 = (bf16[128,1024]{1,0:T(8,128)(2,1)S(1)}, bf16[128,1024]{1,0:T(8,128)(2,1)S(1)}, u32[]{:S(2)}, u32[]{:S(2)}) collective-permute-start(bf16[128,1024]{1,0:T(8,128)(2,1)S(1)} %get-tuple-element.21), channel_id=1, source_target_pairs={{0,8},{8,0},{16,24},{24,16},{1,9},{9,1},{17,25},{25,17},{2,10},{10... | collective-permute-start | bytes 786440 | tf_op jit(solution)/shard_map/ppermute | solution.py:505
  4.1 4.3 %shard_map.78 = (bf16[128,3072]{1,0:T(8,128)(2,1)}, bf16[2,272,512]{2,1,0:T(8,128)(2,1)}, bf16[2,272,512]{2,1,0:T(8,128)(2,1)}) custom-call(s32[2,32]{1,0:T(2,128)} %bitcast.41, bf16[2,512,4096]{2,1,0:T(8,128)(2,1)} %bitcast.9, bf16[2,512,512]{2,1,0:T(8,128)(2,1)} %bitcast.15, bf16[2,512,512]{2,1,0:T(8,128)(2,1)} %bitcast.21, s32[2,512]{1,0:T(2,128)} %bitcast.29, ...), custom_call_target="tpu_custom_call" | custom-call | flops 1024 | bytes 1024 | tf_op jit(solution)/shard_map/pallas_call | solution.py:342
  8.4 0.6 collective-permute-start.3
  9.1 2.0 %collective-permute-start.1 = (bf16[2,272,512]{2,1,0:T(8,128)(2,1)}, bf16[2,272,512]{2,1,0:T(8,128)(2,1)S(1)}, u32[]{:S(2)}, u32[]{:S(2)}) collective-permute-start(bf16[2,272,512]{2,1,0:T(8,128)(2,1)} %get-tuple-element.19), channel_id=1, source_target_pairs={{0,1},{1,2},{2,3},{3,4},{4,5},{5,6},{6,7},{8,9},{9,10},{10,11},{11... | collective-permute-start | bytes 1671176 | tf_op jit(solution)/shard_map/ppermute | solution.py:508
  11.1 0.7 copy-done.8
  11.8 5.0 %shard_map.79.refs_7_ = bf16[320,1024]{1,0:T(8,128)(2,1)} custom-call(s32[2,32]{1,0:T(2,128)} %bitcast.42, bf16[2,512,4096]{2,1,0:T(8,128)(2,1)} %bitcast.10, bf16[2,512,512]{2,1,0:T(8,128)(2,1)} %bitcast.16, bf16[2,512,512]{2,1,0:T(8,128)(2,1)} %bitcast.22, s32[2,512]{1,0:T(2,128)} %bitcast.30, s32[2,512]{1,0:T(2,128)} %bitcast.36, ...), custom_call_target="tpu_custom_call" | custom-call | flops 1024 | bytes 1024 | tf_op jit(solution)/shard_map/pallas_call | solution.py:342
  16.8 1.8 %collective-permute-start.4 = (bf16[320,1024]{1,0:T(8,128)(2,1)}, bf16[320,1024]{1,0:T(8,128)(2,1)S(1)}, u32[]{:S(2)}, u32[]{:S(2)}) collective-permute-start(bf16[320,1024]{1,0:T(8,128)(2,1)} %shard_map.79.refs_7_), channel_id=1, source_target_pairs={{0,8},{8,0},{16,24},{24,16},{1,9},{9,1},{17,25},{25,17},{2,10},{10... | collective-permute-start | bytes 1966088 | tf_op jit(solution)/shard_map/ppermute | solution.py:511
  18.6 3.0 %collective-permute-start = (bf16[2,272,512]{2,1,0:T(8,128)(2,1)S(1)}, bf16[2,272,512]{2,1,0:T(8,128)(2,1)S(1)}, u32[]{:S(2)}, u32[]{:S(2)}) collective-permute-start(bf16[2,272,512]{2,1,0:T(8,128)(2,1)S(1)} %copy-done.14), channel_id=1, source_target_pairs={{0,1},{1,2},{2,3},{3,4},{4,5},{5,6},{6,7},{8,9},{9,10},{10,11},{11... | collective-permute-start | bytes 1671176 | tf_op jit(solution)/shard_map/ppermute | solution.py:509
  21.7 0.8 copy-done.13
  22.4 10.0 %shard_map.80.refs_7_ = bf16[256,4096]{1,0:T(8,128)(2,1)} custom-call(s32[2,32]{1,0:T(2,128)} %bitcast.43, bf16[2,512,4096]{2,1,0:T(8,128)(2,1)} %bitcast.11, bf16[2,512,512]{2,1,0:T(8,128)(2,1)} %bitcast.17, bf16[2,512,512]{2,1,0:T(8,128)(2,1)} %bitcast.23, s32[2,512]{1,0:T(2,128)} %bitcast.31, s32[2,512]{1,0:T(2,128)} %bitcast.37, ...), custom_call_target="tpu_custom_call" | custom-call | flops 2000001024 | bytes 1024 | tf_op jit(solution)/shard_map/pallas_call | solution.py:342
  33.0 0.8 copy-done.12
  33.9 11.7 %shard_map.81 = (bf16[544,1024]{1,0:T(8,128)(2,1)}, bf16[384,1024]{1,0:T(8,128)(2,1)}) custom-call(s32[2,32]{1,0:T(2,128)} %bitcast.44, bf16[2,512,4096]{2,1,0:T(8,128)(2,1)} %bitcast.12, bf16[2,512,512]{2,1,0:T(8,128)(2,1)} %bitcast.18, bf16[2,512,512]{2,1,0:T(8,128)(2,1)} %bitcast.24, s32[2,512]{1,0:T(2,128)} %bitcast.32, s32[2,512]{1,0:T(2,128)} %bitcast.38, ...), custom_call_target="tpu_custom_call" | custom-call | flops 1024 | bytes 1024 | tf_op jit(solution)/shard_map/pallas_call | solution.py:342
  45.6 3.4 %collective-permute-start.9 = (bf16[544,1024]{1,0:T(8,128)(2,1)}, bf16[544,1024]{1,0:T(8,128)(2,1)}, u32[]{:S(2)}, u32[]{:S(2)}) collective-permute-start(bf16[544,1024]{1,0:T(8,128)(2,1)} %get-tuple-element.22.refs_7_.refs_1_.refs_3_.refs_9_), channel_id=1, source_target_pairs={{8,24},{16,0},{9,25},{17,1},{10,26},{18,2},{11,27},{19,3},{12,28},... | collective-permute-start | bytes 3342344 | tf_op jit(solution)/shard_map/ppermute | solution.py:515
  49.0 2.1 %copy.16.refs_0_ = bf16[384,1024]{1,0:T(8,128)(2,1)} copy(bf16[384,1024]{1,0:T(8,128)(2,1)} %get-tuple-element.24.refs_3_) | data formatting | bytes 1572864
  51.1 0.9 copy-done.10
  52.0 0.9 copy-done.2
  52.8 11.8 %shard_map.82 = (bf16[544,1024]{1,0:T(8,128)(2,1)}, bf16[384,1024]{1,0:T(8,128)(2,1)}) custom-call(s32[2,32]{1,0:T(2,128)} %bitcast.45, bf16[2,512,4096]{2,1,0:T(8,128)(2,1)} %bitcast.13, bf16[2,512,512]{2,1,0:T(8,128)(2,1)} %bitcast.19, bf16[2,512,512]{2,1,0:T(8,128)(2,1)} %bitcast.25, s32[2,512]{1,0:T(2,128)} %bitcast.33, s32[2,512]{1,0:T(2,128)} %bitcast.39, ...), custom_call_target="tpu_custom_call" | custom-call | flops 99999997952 | bytes 1024 | tf_op jit(solution)/shard_map/pallas_call | solution.py:342
  64.6 2.4 %collective-permute-start.6 = (bf16[384,1024]{1,0:T(8,128)(2,1)}, bf16[384,1024]{1,0:T(8,128)(2,1)}, u32[]{:S(2)}, u32[]{:S(2)}) collective-permute-start(bf16[384,1024]{1,0:T(8,128)(2,1)} %shard_map.83), channel_id=1, source_target_pairs={{8,24},{16,0},{9,25},{17,1},{10,26},{18,2},{11,27},{19,3},{12,28},... | collective-permute-start | bytes 2359304 | tf_op jit(solution)/shard_map/ppermute | solution.py:527
  67.0 4.4 %collective-permute-start.5 = (bf16[544,1024]{1,0:T(8,128)(2,1)S(1)}, bf16[544,1024]{1,0:T(8,128)(2,1)S(1)}, u32[]{:S(2)}, u32[]{:S(2)}) collective-permute-start(bf16[544,1024]{1,0:T(8,128)(2,1)S(1)} %copy-done), channel_id=1, source_target_pairs={{8,16},{16,8},{9,17},{17,9},{10,18},{18,10},{11,19},{19,11},{12,20... | collective-permute-start | bytes 3342344 | tf_op jit(solution)/shard_map/ppermute | solution.py:526
  71.4 1.9 %collective-permute-done.9.refs_0_ = bf16[544,1024]{1,0:T(8,128)(2,1)} collective-permute-done((bf16[544,1024]{1,0:T(8,128)(2,1)}, bf16[544,1024]{1,0:T(8,128)(2,1)}, u32[]{:S(2)}, u32[]{:S(2)}) %collective-permute-start.9) | collective-permute-done | bytes 1114144 | tf_op jit(solution)/shard_map/ppermute | solution.py:515
  73.3 1.3 collective-permute-start.10
  74.5 0.9 copy.18.refs_0_
  75.5 13.8 %collective-permute-done.6.refs_0_.refs_1_ = bf16[384,1024]{1,0:T(8,128)(2,1)} collective-permute-done((bf16[384,1024]{1,0:T(8,128)(2,1)}, bf16[384,1024]{1,0:T(8,128)(2,1)}, u32[]{:S(2)}, u32[]{:S(2)}) %collective-permute-start.6) | collective-permute-done | bytes 786464 | tf_op jit(solution)/shard_map/ppermute | solution.py:527
  89.2 1.6 %collective-permute-start.7 = (bf16[384,1024]{1,0:T(8,128)(2,1)}, bf16[384,1024]{1,0:T(8,128)(2,1)S(1)}, u32[]{:S(2)}, u32[]{:S(2)}) collective-permute-start(bf16[384,1024]{1,0:T(8,128)(2,1)} %shard_map.84), channel_id=1, source_target_pairs={{24,16},{0,8},{25,17},{1,9},{26,18},{2,10},{27,19},{3,11},{28,20},... | collective-permute-start | bytes 2359304 | tf_op jit(solution)/shard_map/ppermute | solution.py:530
  90.8 4.6 %collective-permute-start.8 = (bf16[384,1024]{1,0:T(8,128)(2,1)}, bf16[384,1024]{1,0:T(8,128)(2,1)S(1)}, u32[]{:S(2)}, u32[]{:S(2)}) collective-permute-start(bf16[384,1024]{1,0:T(8,128)(2,1)} %shard_map.85), channel_id=1, source_target_pairs={{8,16},{16,8},{9,17},{17,9},{10,18},{18,10},{11,19},{19,11},{12,20... | collective-permute-start | bytes 2359304 | tf_op jit(solution)/shard_map/ppermute | solution.py:528
  95.5 1.1 copy-done.11
  96.6 5.5 %shard_map.87 = (bf16[512,4096]{1,0:T(8,128)(2,1)}, bf16[512,4096]{1,0:T(8,128)(2,1)}) custom-call(bf16[320,1024]{1,0:T(8,128)(2,1)S(1)} %copy-done.3, bf16[320,1024]{1,0:T(8,128)(2,1)S(1)} %copy-done.3, bf16[320,1024]{1,0:T(8,128)(2,1)S(1)} %copy-done.3, bf16[320,1024]{1,0:T(8,128)(2,1)S(1)} %copy-done.3, bf16[128,1024]{1,0:T(8,128)(2,1)S(1)} %copy-done.9, ...), custom_call_target="tpu_custom_call" | custom-call | flops 1024 | bytes 1024 | tf_op jit(solution)/shard_map/pallas_call | solution.py:472
  102.1 9.9 %collective-permute-done.5.refs_4_.refs_6_.refs_10_.refs_0_ = bf16[544,1024]{1,0:T(8,128)(2,1)S(1)} collective-permute-done((bf16[544,1024]{1,0:T(8,128)(2,1)S(1)}, bf16[544,1024]{1,0:T(8,128)(2,1)S(1)}, u32[]{:S(2)}, u32[]{:S(2)}) %collective-permute-start.5) | collective-permute-done | bytes 1114144 | tf_op jit(solution)/shard_map/ppermute | solution.py:526
  112.2 4.4 %shard_map.88 = (bf16[512,4096]{1,0:T(8,128)(2,1)}, bf16[512,4096]{1,0:T(8,128)(2,1)}) custom-call(bf16[544,1024]{1,0:T(8,128)(2,1)} %collective-permute-done.10.refs_0_.refs_2_.refs_8_, bf16[544,1024]{1,0:T(8,128)(2,1)S(1)} %copy-done.4, ...), custom_call_target="tpu_custom_call", output_to_operand_aliasing={{0}: (12, {}), {1}: (13, {})} | custom-call | flops 1024 | bytes 1024 | tf_op jit(solution)/shard_map/pallas_call | solution.py:472
  116.6 10.9 %collective-permute-done.7.refs_2_ = bf16[384,1024]{1,0:T(8,128)(2,1)S(1)} collective-permute-done((bf16[384,1024]{1,0:T(8,128)(2,1)}, bf16[384,1024]{1,0:T(8,128)(2,1)S(1)}, u32[]{:S(2)}, u32[]{:S(2)}) %collective-permute-start.7) | collective-permute-done | bytes 786464 | tf_op jit(solution)/shard_map/ppermute | solution.py:530
  127.5 1.5 %shard_map.89 = (bf16[512,4096]{1,0:T(8,128)(2,1)}, bf16[512,4096]{1,0:T(8,128)(2,1)}) custom-call(bf16[544,1024]{1,0:T(8,128)(2,1)S(1)} %collective-permute-done.5.refs_4_.refs_6_.refs_10_.refs_0_, bf16[544,1024]{1,0:T(8,128)(2,1)S(1)} %copy-done.1, ...), custom_call_target="tpu_custom_call", output_to_operand_aliasing={{0}: (6, {}), {1}: (7, {})} | custom-call | flops 1024 | bytes 1024 | tf_op jit(solution)/shard_map/pallas_call | solution.py:472
  (37 shorter events, 0.8 us)
Async XLA Ops:
  2.6 8.5 %collective-permute-start.2 = (bf16[128,1024]{1,0:T(8,128)(2,1)S(1)}, bf16[128,1024]{1,0:T(8,128)(2,1)S(1)}, u32[]{:S(2)}, u32[]{:S(2)}) collective-permute-start(bf16[128,1024]{1,0:T(8,128)(2,1)S(1)} %get-tuple-element.21), channel_id=1, source_target_pairs={{0,8},{8,0},{16,24},{24,16},{1,9},{9,1},{17,25},{25,17},{2,10},{10... | collective-permute-start | bytes 786440 | tf_op jit(solution)/shard_map/ppermute | solution.py:505
  8.4 42.6 %collective-permute-start.3 = (bf16[128,3072]{1,0:T(8,128)(2,1)}, bf16[128,3072]{1,0:T(8,128)(2,1)S(1)}, u32[]{:S(2)}, u32[]{:S(2)}) collective-permute-start(bf16[128,3072]{1,0:T(8,128)(2,1)} %get-tuple-element.20.refs_6_), channel_id=1, source_target_pairs={{0,8},{8,0},{16,24},{24,16},{1,9},{9,1},{17,25},{25,17},{2,10},{10... | collective-permute-start | bytes 2359304 | tf_op jit(solution)/shard_map/ppermute | solution.py:507
  9.1 9.6 %copy-start.14 = (bf16[2,272,512]{2,1,0:T(8,128)(2,1)S(1)}, bf16[2,272,512]{2,1,0:T(8,128)(2,1)}, u32[]{:S(2)}) copy-start(bf16[2,272,512]{2,1,0:T(8,128)(2,1)} %get-tuple-element.18) | copy-start | bytes 1671172
  9.1 12.6 %collective-permute-start.1 = (bf16[2,272,512]{2,1,0:T(8,128)(2,1)}, bf16[2,272,512]{2,1,0:T(8,128)(2,1)S(1)}, u32[]{:S(2)}, u32[]{:S(2)}) collective-permute-start(bf16[2,272,512]{2,1,0:T(8,128)(2,1)} %get-tuple-element.19), channel_id=1, source_target_pairs={{0,1},{1,2},{2,3},{3,4},{4,5},{5,6},{6,7},{8,9},{9,10},{10,11},{11... | collective-permute-start | bytes 1671176 | tf_op jit(solution)/shard_map/ppermute | solution.py:508
  11.1 0.7 copy-start.8
  16.8 34.3 %collective-permute-start.4 = (bf16[320,1024]{1,0:T(8,128)(2,1)}, bf16[320,1024]{1,0:T(8,128)(2,1)S(1)}, u32[]{:S(2)}, u32[]{:S(2)}) collective-permute-start(bf16[320,1024]{1,0:T(8,128)(2,1)} %shard_map.79.refs_7_), channel_id=1, source_target_pairs={{0,8},{8,0},{16,24},{24,16},{1,9},{9,1},{17,25},{25,17},{2,10},{10... | collective-permute-start | bytes 1966088 | tf_op jit(solution)/shard_map/ppermute | solution.py:511
  18.6 14.4 %collective-permute-start = (bf16[2,272,512]{2,1,0:T(8,128)(2,1)S(1)}, bf16[2,272,512]{2,1,0:T(8,128)(2,1)S(1)}, u32[]{:S(2)}, u32[]{:S(2)}) collective-permute-start(bf16[2,272,512]{2,1,0:T(8,128)(2,1)S(1)} %copy-done.14), channel_id=1, source_target_pairs={{0,1},{1,2},{2,3},{3,4},{4,5},{5,6},{6,7},{8,9},{9,10},{10,11},{11... | collective-permute-start | bytes 1671176 | tf_op jit(solution)/shard_map/ppermute | solution.py:509
  21.6 0.8 copy-start.13
  32.4 63.0 %collective-permute-start.11 = (bf16[256,4096]{1,0:T(8,128)(2,1)}, bf16[256,4096]{1,0:T(8,128)(2,1)}, u32[]{:S(2)}, u32[]{:S(2)}) collective-permute-start(bf16[256,4096]{1,0:T(8,128)(2,1)} %shard_map.80.refs_7_), channel_id=1, source_target_pairs={{0,8},{8,0},{16,24},{24,16},{1,9},{9,1},{17,25},{25,17},{2,10},{10... | collective-permute-start | bytes 6291464 | tf_op jit(solution)/shard_map/ppermute | solution.py:513
  33.0 0.9 copy-start.12
  45.6 27.6 %collective-permute-start.9 = (bf16[544,1024]{1,0:T(8,128)(2,1)}, bf16[544,1024]{1,0:T(8,128)(2,1)}, u32[]{:S(2)}, u32[]{:S(2)}) collective-permute-start(bf16[544,1024]{1,0:T(8,128)(2,1)} %get-tuple-element.22.refs_7_.refs_1_.refs_3_.refs_9_), channel_id=1, source_target_pairs={{8,24},{16,0},{9,25},{17,1},{10,26},{18,2},{11,27},{19,3},{12,28},... | collective-permute-start | bytes 3342344 | tf_op jit(solution)/shard_map/ppermute | solution.py:515
  51.1 0.9 copy-start.10
  52.0 0.9 copy-start.2
  64.6 2.4 %copy-start = (bf16[544,1024]{1,0:T(8,128)(2,1)S(1)}, bf16[544,1024]{1,0:T(8,128)(2,1)}, u32[]{:S(2)}) copy-start(bf16[544,1024]{1,0:T(8,128)(2,1)} %get-tuple-element.23.refs_1_.refs_5_.refs_7_.refs_11_) | copy-start | bytes 3342340
  64.6 9.9 %copy-start.6 = (bf16[384,1024]{1,0:T(8,128)(2,1)S(1)}, bf16[384,1024]{1,0:T(8,128)(2,1)}, u32[]{:S(2)}) copy-start(bf16[384,1024]{1,0:T(8,128)(2,1)} %get-tuple-element.25.refs_5_) | copy-start | bytes 2359300
  64.6 24.6 %collective-permute-start.6 = (bf16[384,1024]{1,0:T(8,128)(2,1)}, bf16[384,1024]{1,0:T(8,128)(2,1)}, u32[]{:S(2)}, u32[]{:S(2)}) collective-permute-start(bf16[384,1024]{1,0:T(8,128)(2,1)} %shard_map.83), channel_id=1, source_target_pairs={{8,24},{16,0},{9,25},{17,1},{10,26},{18,2},{11,27},{19,3},{12,28},... | collective-permute-start | bytes 2359304 | tf_op jit(solution)/shard_map/ppermute | solution.py:527
  67.0 45.0 %collective-permute-start.5 = (bf16[544,1024]{1,0:T(8,128)(2,1)S(1)}, bf16[544,1024]{1,0:T(8,128)(2,1)S(1)}, u32[]{:S(2)}, u32[]{:S(2)}) collective-permute-start(bf16[544,1024]{1,0:T(8,128)(2,1)S(1)} %copy-done), channel_id=1, source_target_pairs={{8,16},{16,8},{9,17},{17,9},{10,18},{18,10},{11,19},{19,11},{12,20... | collective-permute-start | bytes 3342344 | tf_op jit(solution)/shard_map/ppermute | solution.py:526
  73.3 38.9 %collective-permute-start.10 = (bf16[544,1024]{1,0:T(8,128)(2,1)}, bf16[544,1024]{1,0:T(8,128)(2,1)}, u32[]{:S(2)}, u32[]{:S(2)}) collective-permute-start(bf16[544,1024]{1,0:T(8,128)(2,1)} %shard_map.86), channel_id=1, source_target_pairs={{24,16},{0,8},{25,17},{1,9},{26,18},{2,10},{27,19},{3,11},{28,20},... | collective-permute-start | bytes 3342344 | tf_op jit(solution)/shard_map/ppermute | solution.py:529
  75.5 20.0 %copy-start.3 = (bf16[320,1024]{1,0:T(8,128)(2,1)S(1)}, bf16[320,1024]{1,0:T(8,128)(2,1)}, u32[]{:S(2)}) copy-start(bf16[320,1024]{1,0:T(8,128)(2,1)} %copy-done.2) | copy-start | bytes 1966084
  75.5 20.0 %copy-start.9 = (bf16[128,1024]{1,0:T(8,128)(2,1)S(1)}, bf16[128,1024]{1,0:T(8,128)(2,1)}, u32[]{:S(2)}) copy-start(bf16[128,1024]{1,0:T(8,128)(2,1)} %copy-done.8) | copy-start | bytes 786436
  89.2 22.9 %copy-start.1 = (bf16[544,1024]{1,0:T(8,128)(2,1)S(1)}, bf16[544,1024]{1,0:T(8,128)(2,1)}, u32[]{:S(2)}) copy-start(bf16[544,1024]{1,0:T(8,128)(2,1)} %get-tuple-element.23.refs_1_.refs_5_.refs_7_.refs_11_) | copy-start | bytes 3342340
  89.2 22.9 %copy-start.4 = (bf16[544,1024]{1,0:T(8,128)(2,1)S(1)}, bf16[544,1024]{1,0:T(8,128)(2,1)}, u32[]{:S(2)}) copy-start(bf16[544,1024]{1,0:T(8,128)(2,1)} %get-tuple-element.22.refs_7_.refs_1_.refs_3_.refs_9_) | copy-start | bytes 3342340
  89.2 38.2 %collective-permute-start.7 = (bf16[384,1024]{1,0:T(8,128)(2,1)}, bf16[384,1024]{1,0:T(8,128)(2,1)S(1)}, u32[]{:S(2)}, u32[]{:S(2)}) collective-permute-start(bf16[384,1024]{1,0:T(8,128)(2,1)} %shard_map.84), channel_id=1, source_target_pairs={{24,16},{0,8},{25,17},{1,9},{26,18},{2,10},{27,19},{3,11},{28,20},... | collective-permute-start | bytes 2359304 | tf_op jit(solution)/shard_map/ppermute | solution.py:530
  90.8 36.6 %collective-permute-start.8 = (bf16[384,1024]{1,0:T(8,128)(2,1)}, bf16[384,1024]{1,0:T(8,128)(2,1)S(1)}, u32[]{:S(2)}, u32[]{:S(2)}) collective-permute-start(bf16[384,1024]{1,0:T(8,128)(2,1)} %shard_map.85), channel_id=1, source_target_pairs={{8,16},{16,8},{9,17},{17,9},{10,18},{18,10},{11,19},{19,11},{12,20... | collective-permute-start | bytes 2359304 | tf_op jit(solution)/shard_map/ppermute | solution.py:528
  95.4 1.1 copy-start.11
  112.2 15.3 %copy-start.5 = (bf16[384,1024]{1,0:T(8,128)(2,1)S(1)}, bf16[384,1024]{1,0:T(8,128)(2,1)}, u32[]{:S(2)}) copy-start(bf16[384,1024]{1,0:T(8,128)(2,1)} %get-tuple-element.24.refs_3_) | copy-start | bytes 2359300
  112.2 15.3 %copy-start.7 = (bf16[384,1024]{1,0:T(8,128)(2,1)S(1)}, bf16[384,1024]{1,0:T(8,128)(2,1)}, u32[]{:S(2)}) copy-start(bf16[384,1024]{1,0:T(8,128)(2,1)} %get-tuple-element.25.refs_5_) | copy-start | bytes 2359300
